TPU v7x, 256 devices: a whole 4x4x8 slice. The times are simulated.
256 devices in a mesh: lon: 32 (over z, y), lat: 8 (over x, core).
Axes of the slice: x: 4, y: 4, z: 8, core: 2. Of those that a mesh axis runs over, the one named last changes fastest.
Arguments:
- cotangent: float32 [8, 512, 4096], P(None, 'lat', 'lon'), may hold values from -6 to 6
- diff_east: float32 [512, 4096], P('lat', 'lon'), may hold values from 0.02 to 0.2
- diff_north: float32 [512, 4096], P('lat', 'lon'), may hold values from 0.02 to 0.2
- flow_east: float32 [512, 4096], P('lat', 'lon'), may hold values from -0.2 to 0.2
- flow_north: float32 [512, 4096], P('lat', 'lon'), may hold values from -0.2 to 0.2
- sea_mask: int32 [512, 4096], P('lat', 'lon'), may hold values 0 or 1
- cutoff: int32 [512], P('lat'), may hold values from 16 to 2048, as said below
Outputs:
- adjoint_field: float32 [8, 512, 4096], P(None, 'lat', 'lon')
Inputs may be any that keep to these rules, and one draw needn't show every extreme that they name: cutoff equals 2048 on every row except the first 64 and the last 64 rows.
All inputs are finite; a program needn't handle non-finite values. No bound on the sum of `sea_mask` on one device may be relied on, other than what follows from the above.
Results may differ from a plain program's by a relative error of at most 0.00012.
Values sent between devices are 32-bit elements; how exact they have to be, the bound alone decides.
A program may use at most 64 MiB of HBM per device.

v0:
```python
import jax
import jax.numpy as jnp
from jax import lax
from jax.sharding import PartitionSpec as P

RADIX = 64
STEPS = 4


FULL_PRECISION = lax.Precision.HIGHEST
FULL_TURN = 6.283185307179586


def with_halo(cells, sides, width):
    for axis, dim in sides:
        count = lax.axis_size(axis)
        head = lax.slice_in_dim(cells, 0, width, axis=dim)
        tail = lax.slice_in_dim(cells, cells.shape[dim] - width, cells.shape[dim], axis=dim)
        cells = jnp.concatenate(
            [
                lax.ppermute(tail, axis, [(i, (i + 1) % count) for i in range(count)]),
                cells,
                lax.ppermute(head, axis, [((i + 1) % count, i) for i in range(count)]),
            ],
            axis=dim,
        )
    return cells


def angle_table(first_index, second_index, period):
    return (jnp.outer(first_index, second_index) % period).astype(jnp.float32) * (
        FULL_TURN / period
    )


def contract(form, left, right):
    return jnp.einsum(form, left, right, precision=FULL_PRECISION)


def zonal_filter(rows_field, row_cuts):
    planes, row_count, length = rows_field.shape
    indices = jnp.arange(RADIX, dtype=jnp.int32)
    small_angle = angle_table(indices, indices, RADIX)
    cos_small = jnp.cos(small_angle)
    sin_small = jnp.sin(small_angle)
    twist_angle = angle_table(indices, indices, RADIX * RADIX)
    cos_twist = jnp.cos(twist_angle)
    sin_twist = jnp.sin(twist_angle)
    blocks = rows_field.reshape(planes, row_count, RADIX, RADIX)
    first_real = contract("prab,ak->prbk", blocks, cos_small)
    first_imag = -contract("prab,ak->prbk", blocks, sin_small)
    turned_real = first_real * cos_twist + first_imag * sin_twist
    turned_imag = first_imag * cos_twist - first_real * sin_twist
    spec_real = contract("prbk,bm->prkm", turned_real, cos_small) + contract(
        "prbk,bm->prkm", turned_imag, sin_small
    )
    spec_imag = contract("prbk,bm->prkm", turned_imag, cos_small) - contract(
        "prbk,bm->prkm", turned_real, sin_small
    )
    frequency = indices[:, None] + RADIX * indices[None, :]
    wavenumber = jnp.minimum(frequency, RADIX * RADIX - frequency).astype(jnp.float32)
    kept_mask = (wavenumber[None, None] <= row_cuts[:, :, None, None]).astype(jnp.float32)
    spec_real = spec_real * kept_mask
    spec_imag = spec_imag * kept_mask
    back_real = contract("prkm,bm->prkb", spec_real, cos_small) - contract(
        "prkm,bm->prkb", spec_imag, sin_small
    )
    back_imag = contract("prkm,bm->prkb", spec_imag, cos_small) + contract(
        "prkm,bm->prkb", spec_real, sin_small
    )
    cos_turned = cos_twist.T
    sin_turned = sin_twist.T
    twisted_real = back_real * cos_turned - back_imag * sin_turned
    twisted_imag = back_imag * cos_turned + back_real * sin_turned
    result = contract("prkb,ak->prab", twisted_real, cos_small) - contract(
        "prkb,ak->prab", twisted_imag, sin_small
    )
    return (result / float(RADIX * RADIX)).reshape(planes, row_count, length)


def filter_tile(tile, tile_cuts):
    lon_count = lax.axis_size("lon")
    share_rows = tile.shape[1] // lon_count
    rows_field = lax.all_to_all(tile, "lon", split_axis=1, concat_axis=2, tiled=True)
    row_cuts = lax.dynamic_slice_in_dim(
        tile_cuts, lax.axis_index("lon") * share_rows, share_rows, 1
    )
    filtered = zonal_filter(rows_field, row_cuts)
    return lax.all_to_all(filtered, "lon", split_axis=2, concat_axis=1, tiled=True)


def shards(cotangent, diff_east, diff_north, flow_east, flow_north, sea_mask, cutoff):
    levels, lat_rows, lon_local = cotangent.shape
    lat_index = lax.axis_index("lat")
    lat_count = lax.axis_size("lat")
    sea = sea_mask.astype(jnp.float32)
    cut_float = cutoff.astype(jnp.float32)
    stacked = jnp.stack([diff_east, diff_north, flow_east, flow_north, sea])
    padded = with_halo(stacked, (("lat", 1), ("lon", 2)), 1)
    east_kappa = padded[0, 1:-1, :-1]
    east_flow = padded[2, 1:-1, :-1]
    east_open = padded[4, 1:-1, :-1] * padded[4, 1:-1, 1:]
    east_minus = east_open * (-east_kappa - 0.5 * east_flow)
    east_plus = east_open * (east_kappa - 0.5 * east_flow)
    north_kappa = padded[1, :-1, 1:-1]
    north_flow = padded[3, :-1, 1:-1]
    global_row = lat_index * lat_rows + jnp.arange(lat_rows + 1, dtype=jnp.int32) - 1
    inside = ((global_row >= 0) & (global_row < lat_rows * lat_count - 1)).astype(jnp.float32)
    north_open = padded[4, :-1, 1:-1] * padded[4, 1:, 1:-1] * inside[:, None]
    north_minus = north_open * (-north_kappa - 0.5 * north_flow)
    north_plus = north_open * (north_kappa - 0.5 * north_flow)
    all_cuts = jnp.broadcast_to(cut_float[None, :], (levels, lat_rows))
    adjoint_field = cotangent
    for section in range(STEPS):
        adjoint_field = filter_tile(adjoint_field, all_cuts)
        weighted = sea[None] * adjoint_field
        rimmed = with_halo(weighted, (("lat", 1), ("lon", 2)), 1)
        east_diff = rimmed[:, 1:-1, :-1] - rimmed[:, 1:-1, 1:]
        north_diff = rimmed[:, :-1, 1:-1] - rimmed[:, 1:, 1:-1]
        adjoint_field = (
            adjoint_field
            + east_diff[:, :, 1:] * east_minus[None, :, 1:]
            + east_diff[:, :, :-1] * east_plus[None, :, :-1]
            + north_diff[:, 1:] * north_minus[None, 1:]
            + north_diff[:, :-1] * north_plus[None, :-1]
        )
    return adjoint_field


def solution(mesh):
    return jax.shard_map(
        shards,
        mesh=mesh,
        in_specs=(
            P(None, "lat", "lon"),
            P("lat", "lon"),
            P("lat", "lon"),
            P("lat", "lon"),
            P("lat", "lon"),
            P("lat", "lon"),
            P("lat"),
        ),
        out_specs=P(None, "lat", "lon"),
        check_vma=False,
    )
```

profile of v0, /device:TPU:1, one launch (start us, length us, event | category | flops | bytes accessed | tf_op | source)
XLA Modules:
  0.0 377.8 jit_solution(7116614834118535175)
XLA Ops:
  8.9 10.5 %all-to-all-start = ((f32[8,64,128]{2,0,1:T(8,128)}), f32[8,64,128]{2,0,1:T(8,128)S(1)}, u32[]{:S(2)}, u32[]{:S(2)}) async-start(f32[8,64,128]{2,0,1:T(8,128)} %copy.158), calls=%async_computation | async-start | bytes 524288 | tf_op jit(solution)/shard_map/all_to_all | solution.py:84
  49.3 7.8 %reshape.140 = f32[32,1,2048]{2,1,0:T(1,128)} reshape(f32[4096,2,8]{2,1,0:T(2,128)} %bitcast.224) | data formatting | bytes 524288
  61.3 10.1 %all-to-all-done.1 = f32[32,1,2048]{2,1,0:T(1,128)S(1)} async-done(((f32[32,1,2048]{2,1,0:T(1,128)}), f32[32,1,2048]{2,1,0:T(1,128)S(1)}, u32[]{:S(2)}, u32[]{:S(2)}) %all-to-all-start.1) | async-done | bytes 262176 | tf_op jit(solution)/shard_map/all_to_all | solution.py:89
  73.2 7.7 %reshape.141 = f32[4096,2,8]{2,1,0:T(2,128)} reshape(f32[32,2048]{1,0:T(8,128)S(1)} %reduce) | data formatting | bytes 524288
  80.9 5.1 %copy.171 = f32[8,32,2,128]{3,0,2,1:T(8,128)S(1)} copy(f32[8,32,2,128]{0,2,3,1:T(2,128)} %bitcast.225) | data formatting | bytes 524288 | tf_op jit(solution)/shard_map/all_to_all | solution.py:89
  86.0 6.2 %collective-permute-start.1 = (f32[8,1,128]{2,0,1:T(8,128)S(1)}, f32[8,1,128]{2,0,1:T(8,128)S(1)}, u32[]{:S(2)}, u32[]{:S(2)}) collective-permute-start(f32[8,1,128]{2,0,1:T(8,128)S(1)} %get-tuple-element.22), channel_id=1, source_target_pairs={{1,0},{2,1},{3,2},{4,3},{5,4},{6,5},{7,6},{0,7},{9,8},{10,9},{11,1... | collective-permute-start | bytes 12296 | tf_op jit(solution)/shard_map/ppermute | solution.py:23
  103.7 16.6 %all_to_all.132 = f32[8,64,128]{2,0,1:T(8,128)S(1)} all-to-all(f32[8,64,128]{2,0,1:T(8,128)S(1)} %fusion.53), channel_id=1, replica_groups=mesh['lon'=32,'lat'=8] {'lon'}, dimensions={1} | all-to-all | bytes 524288 | tf_op jit(solution)/shard_map/all_to_all | solution.py:84
  139.5 7.6 %reshape.142 = f32[32,1,2048]{2,1,0:T(1,128)S(1)} reshape(f32[4096,2,8]{2,1,0:T(2,128)} %bitcast.226) | data formatting | bytes 524288
  147.1 13.8 %all_to_all.133 = f32[32,1,2048]{2,1,0:T(1,128)S(1)} all-to-all(f32[32,1,2048]{2,1,0:T(1,128)S(1)} %reshape.142), channel_id=1, replica_groups=mesh['lon'=32,'lat'=8] {'lon'}, dimensions={0} | all-to-all | bytes 524288 | tf_op jit(solution)/shard_map/all_to_all | solution.py:89
  162.3 7.7 %reshape.143 = f32[4096,2,8]{2,1,0:T(2,128)} reshape(f32[32,2048]{1,0:T(8,128)S(1)} %reduce.1) | data formatting | bytes 524288
  169.9 5.1 %copy.185 = f32[8,2,32,128]{3,0,1,2:T(8,128)S(1)} copy(f32[8,2,32,128]{0,1,3,2:T(2,128)} %bitcast.227) | data formatting | bytes 524288 | tf_op jit(solution)/shard_map/all_to_all | solution.py:89
  175.0 6.5 %collective-permute-start.9 = (f32[8,1,128]{2,0,1:T(8,128)S(1)}, f32[8,1,128]{2,0,1:T(8,128)S(1)}, u32[]{:S(2)}, u32[]{:S(2)}) collective-permute-start(f32[8,1,128]{2,0,1:T(8,128)S(1)} %get-tuple-element.20), channel_id=1, source_target_pairs={{1,0},{2,1},{3,2},{4,3},{5,4},{6,5},{7,6},{0,7},{9,8},{10,9},{11,1... | collective-permute-start | bytes 12296 | tf_op jit(solution)/shard_map/ppermute | solution.py:23
  194.3 16.6 %all_to_all.134 = f32[8,64,128]{2,0,1:T(8,128)S(1)} all-to-all(f32[8,64,128]{2,0,1:T(8,128)S(1)} %fusion.49), channel_id=1, replica_groups=mesh['lon'=32,'lat'=8] {'lon'}, dimensions={1} | all-to-all | bytes 524288 | tf_op jit(solution)/shard_map/all_to_all | solution.py:84
  230.1 7.4 %reshape.144 = f32[32,1,2048]{2,1,0:T(1,128)S(1)} reshape(f32[4096,2,8]{2,1,0:T(2,128)} %bitcast.228) | data formatting | bytes 524288
  237.5 14.0 %all_to_all.135 = f32[32,1,2048]{2,1,0:T(1,128)S(1)} all-to-all(f32[32,1,2048]{2,1,0:T(1,128)S(1)} %reshape.144), channel_id=1, replica_groups=mesh['lon'=32,'lat'=8] {'lon'}, dimensions={0} | all-to-all | bytes 524288 | tf_op jit(solution)/shard_map/all_to_all | solution.py:89
  252.8 7.7 %reshape.145 = f32[4096,2,8]{2,1,0:T(2,128)} reshape(f32[32,2048]{1,0:T(8,128)S(1)} %reduce.2) | data formatting | bytes 524288
  260.4 5.1 %copy.199 = f32[8,2,32,128]{3,0,1,2:T(8,128)S(1)} copy(f32[8,2,32,128]{0,1,3,2:T(2,128)} %bitcast.229) | data formatting | bytes 524288 | tf_op jit(solution)/shard_map/all_to_all | solution.py:89
  265.6 5.3 %collective-permute-start.13 = (f32[8,1,128]{2,0,1:T(8,128)S(1)}, f32[8,1,128]{2,0,1:T(8,128)S(1)}, u32[]{:S(2)}, u32[]{:S(2)}) collective-permute-start(f32[8,1,128]{2,0,1:T(8,128)S(1)} %get-tuple-element.18), channel_id=1, source_target_pairs={{1,0},{2,1},{3,2},{4,3},{5,4},{6,5},{7,6},{0,7},{9,8},{10,9},{11,1... | collective-permute-start | bytes 12296 | tf_op jit(solution)/shard_map/ppermute | solution.py:23
  281.3 17.0 %all_to_all.136 = f32[8,64,128]{2,0,1:T(8,128)S(1)} all-to-all(f32[8,64,128]{2,0,1:T(8,128)S(1)} %fusion.45), channel_id=1, replica_groups=mesh['lon'=32,'lat'=8] {'lon'}, dimensions={1} | all-to-all | bytes 524288 | tf_op jit(solution)/shard_map/all_to_all | solution.py:84
  317.6 7.4 %reshape.146 = f32[32,1,2048]{2,1,0:T(1,128)S(1)} reshape(f32[4096,2,8]{2,1,0:T(2,128)} %bitcast.230) | data formatting | bytes 524288
  325.0 13.9 %all_to_all.137 = f32[32,1,2048]{2,1,0:T(1,128)S(1)} all-to-all(f32[32,1,2048]{2,1,0:T(1,128)S(1)} %reshape.146), channel_id=1, replica_groups=mesh['lon'=32,'lat'=8] {'lon'}, dimensions={0} | all-to-all | bytes 524288 | tf_op jit(solution)/shard_map/all_to_all | solution.py:89
  340.2 7.7 %reshape.147 = f32[4096,2,8]{2,1,0:T(2,128)} reshape(f32[32,2048]{1,0:T(8,128)S(1)} %reduce.3) | data formatting | bytes 524288
  353.0 7.1 %collective-permute-start.17 = (f32[8,1,128]{2,0,1:T(8,128)S(1)}, f32[8,1,128]{2,0,1:T(8,128)S(1)}, u32[]{:S(2)}, u32[]{:S(2)}) collective-permute-start(f32[8,1,128]{2,0,1:T(8,128)S(1)} %get-tuple-element.16), channel_id=1, source_target_pairs={{1,0},{2,1},{3,2},{4,3},{5,4},{6,5},{7,6},{0,7},{9,8},{10,9},{11,1... | collective-permute-start | bytes 12296 | tf_op jit(solution)/shard_map/ppermute | solution.py:23
  370.3 6.2 %collective-permute-done.18 = f32[8,66,1]{2,0,1:T(8,128)S(1)} collective-permute-done((f32[8,66,1]{2,0,1:T(8,128)S(1)}, f32[8,66,1]{2,0,1:T(8,128)S(1)}, u32[]{:S(2)}, u32[]{:S(2)}) %collective-permute-start.18) | collective-permute-done | bytes 2144 | tf_op jit(solution)/shard_map/ppermute | solution.py:21
  (156 shorter events, 157.0 us)
Async XLA Ops:
  3.8 17.6 %collective-permute-start.4 = (f32[5,1,128]{2,1,0:T(1,128)S(1)}, f32[5,1,128]{2,1,0:T(1,128)S(1)}, u32[]{:S(2)}, u32[]{:S(2)}) collective-permute-start(f32[5,1,128]{2,1,0:T(1,128)S(1)} %get-tuple-element.30), channel_id=1, source_target_pairs={{0,1},{1,2},{2,3},{3,4},{4,5},{5,6},{6,7},{7,0},{8,9},{9,10},{10,1... | collective-permute-start | bytes 7688 | tf_op jit(solution)/shard_map/ppermute | solution.py:21
  6.4 15.0 %collective-permute-start.5 = (f32[5,1,128]{2,1,0:T(1,128)S(1)}, f32[5,1,128]{2,1,0:T(1,128)S(1)}, u32[]{:S(2)}, u32[]{:S(2)}) collective-permute-start(f32[5,1,128]{2,1,0:T(1,128)S(1)} %get-tuple-element.31), channel_id=1, source_target_pairs={{1,0},{2,1},{3,2},{4,3},{5,4},{6,5},{7,6},{0,7},{9,8},{10,9},{11,1... | collective-permute-start | bytes 7688 | tf_op jit(solution)/shard_map/ppermute | solution.py:23
  8.9 21.0 %all-to-all-start = ((f32[8,64,128]{2,0,1:T(8,128)}), f32[8,64,128]{2,0,1:T(8,128)S(1)}, u32[]{:S(2)}, u32[]{:S(2)}) async-start(f32[8,64,128]{2,0,1:T(8,128)} %copy.158), calls=%async_computation | async-start | bytes 524288 | tf_op jit(solution)/shard_map/all_to_all | solution.py:84
  21.6 39.6 %collective-permute-start.6 = (f32[5,66,1]{2,1,0:T(8,128)S(1)}, f32[5,66,1]{2,1,0:T(8,128)S(1)}, u32[]{:S(2)}, u32[]{:S(2)}) collective-permute-start(f32[5,66,1]{2,1,0:T(8,128)S(1)} %get-tuple-element.26), channel_id=1, source_target_pairs={{0,8},{8,16},{16,24},{24,32},{32,40},{40,48},{48,56},{56,64},{64,7... | collective-permute-start | bytes 3968 | tf_op jit(solution)/shard_map/ppermute | solution.py:21
  22.9 38.3 %collective-permute-start.7 = (f32[5,66,1]{2,1,0:T(8,128)S(1)}, f32[5,66,1]{2,1,0:T(8,128)S(1)}, u32[]{:S(2)}, u32[]{:S(2)}) collective-permute-start(f32[5,66,1]{2,1,0:T(8,128)S(1)} %get-tuple-element.27), channel_id=1, source_target_pairs={{8,0},{16,8},{24,16},{32,24},{40,32},{48,40},{56,48},{64,56},{72,6... | collective-permute-start | bytes 3968 | tf_op jit(solution)/shard_map/ppermute | solution.py:23
  57.1 14.3 %all-to-all-start.1 = ((f32[32,1,2048]{2,1,0:T(1,128)}), f32[32,1,2048]{2,1,0:T(1,128)S(1)}, u32[]{:S(2)}, u32[]{:S(2)}) async-start(f32[32,1,2048]{2,1,0:T(1,128)} %reshape.140), calls=%async_computation.1 | async-start | bytes 524288 | tf_op jit(solution)/shard_map/all_to_all | solution.py:89
  86.0 8.2 %collective-permute-start.1 = (f32[8,1,128]{2,0,1:T(8,128)S(1)}, f32[8,1,128]{2,0,1:T(8,128)S(1)}, u32[]{:S(2)}, u32[]{:S(2)}) collective-permute-start(f32[8,1,128]{2,0,1:T(8,128)S(1)} %get-tuple-element.22), channel_id=1, source_target_pairs={{1,0},{2,1},{3,2},{4,3},{5,4},{6,5},{7,6},{0,7},{9,8},{10,9},{11,1... | collective-permute-start | bytes 12296 | tf_op jit(solution)/shard_map/ppermute | solution.py:23
  92.2 1.9 collective-permute-start
  94.3 9.0 %collective-permute-start.2 = (f32[8,66,1]{2,0,1:T(8,128)S(1)}, f32[8,66,1]{2,0,1:T(8,128)S(1)}, u32[]{:S(2)}, u32[]{:S(2)}) collective-permute-start(f32[8,66,1]{2,0,1:T(8,128)S(1)} %get-tuple-element.14), channel_id=1, source_target_pairs={{0,8},{8,16},{16,24},{24,32},{32,40},{40,48},{48,56},{56,64},{64,7... | collective-permute-start | bytes 6344 | tf_op jit(solution)/shard_map/ppermute | solution.py:21
  94.4 8.9 %collective-permute-start.3 = (f32[8,66,1]{2,0,1:T(8,128)S(1)}, f32[8,66,1]{2,0,1:T(8,128)S(1)}, u32[]{:S(2)}, u32[]{:S(2)}) collective-permute-start(f32[8,66,1]{2,0,1:T(8,128)S(1)} %get-tuple-element.15), channel_id=1, source_target_pairs={{8,0},{16,8},{24,16},{32,24},{40,32},{48,40},{56,48},{64,56},{72,6... | collective-permute-start | bytes 6344 | tf_op jit(solution)/shard_map/ppermute | solution.py:23
  175.0 9.1 %collective-permute-start.9 = (f32[8,1,128]{2,0,1:T(8,128)S(1)}, f32[8,1,128]{2,0,1:T(8,128)S(1)}, u32[]{:S(2)}, u32[]{:S(2)}) collective-permute-start(f32[8,1,128]{2,0,1:T(8,128)S(1)} %get-tuple-element.20), channel_id=1, source_target_pairs={{1,0},{2,1},{3,2},{4,3},{5,4},{6,5},{7,6},{0,7},{9,8},{10,9},{11,1... | collective-permute-start | bytes 12296 | tf_op jit(solution)/shard_map/ppermute | solution.py:23
  181.6 2.5 collective-permute-start.8
  184.3 9.6 %collective-permute-start.10 = (f32[8,66,1]{2,0,1:T(8,128)S(1)}, f32[8,66,1]{2,0,1:T(8,128)S(1)}, u32[]{:S(2)}, u32[]{:S(2)}) collective-permute-start(f32[8,66,1]{2,0,1:T(8,128)S(1)} %get-tuple-element.12), channel_id=1, source_target_pairs={{0,8},{8,16},{16,24},{24,32},{32,40},{40,48},{48,56},{56,64},{64,7... | collective-permute-start | bytes 6344 | tf_op jit(solution)/shard_map/ppermute | solution.py:21
  184.4 9.6 %collective-permute-start.11 = (f32[8,66,1]{2,0,1:T(8,128)S(1)}, f32[8,66,1]{2,0,1:T(8,128)S(1)}, u32[]{:S(2)}, u32[]{:S(2)}) collective-permute-start(f32[8,66,1]{2,0,1:T(8,128)S(1)} %get-tuple-element.13), channel_id=1, source_target_pairs={{8,0},{16,8},{24,16},{32,24},{40,32},{48,40},{56,48},{64,56},{72,6... | collective-permute-start | bytes 6344 | tf_op jit(solution)/shard_map/ppermute | solution.py:23
  265.6 6.5 %collective-permute-start.13 = (f32[8,1,128]{2,0,1:T(8,128)S(1)}, f32[8,1,128]{2,0,1:T(8,128)S(1)}, u32[]{:S(2)}, u32[]{:S(2)}) collective-permute-start(f32[8,1,128]{2,0,1:T(8,128)S(1)} %get-tuple-element.18), channel_id=1, source_target_pairs={{1,0},{2,1},{3,2},{4,3},{5,4},{6,5},{7,6},{0,7},{9,8},{10,9},{11,1... | collective-permute-start | bytes 12296 | tf_op jit(solution)/shard_map/ppermute | solution.py:23
  270.8 1.3 collective-permute-start.12
  272.2 8.7 %collective-permute-start.14 = (f32[8,66,1]{2,0,1:T(8,128)S(1)}, f32[8,66,1]{2,0,1:T(8,128)S(1)}, u32[]{:S(2)}, u32[]{:S(2)}) collective-permute-start(f32[8,66,1]{2,0,1:T(8,128)S(1)} %get-tuple-element.10), channel_id=1, source_target_pairs={{0,8},{8,16},{16,24},{24,32},{32,40},{40,48},{48,56},{56,64},{64,7... | collective-permute-start | bytes 6344 | tf_op jit(solution)/shard_map/ppermute | solution.py:21
  272.3 8.6 %collective-permute-start.15 = (f32[8,66,1]{2,0,1:T(8,128)S(1)}, f32[8,66,1]{2,0,1:T(8,128)S(1)}, u32[]{:S(2)}, u32[]{:S(2)}) collective-permute-start(f32[8,66,1]{2,0,1:T(8,128)S(1)} %get-tuple-element.11), channel_id=1, source_target_pairs={{8,0},{16,8},{24,16},{32,24},{40,32},{48,40},{56,48},{64,56},{72,6... | collective-permute-start | bytes 6344 | tf_op jit(solution)/shard_map/ppermute | solution.py:23
  353.0 12.3 %collective-permute-start.17 = (f32[8,1,128]{2,0,1:T(8,128)S(1)}, f32[8,1,128]{2,0,1:T(8,128)S(1)}, u32[]{:S(2)}, u32[]{:S(2)}) collective-permute-start(f32[8,1,128]{2,0,1:T(8,128)S(1)} %get-tuple-element.16), channel_id=1, source_target_pairs={{1,0},{2,1},{3,2},{4,3},{5,4},{6,5},{7,6},{0,7},{9,8},{10,9},{11,1... | collective-permute-start | bytes 12296 | tf_op jit(solution)/shard_map/ppermute | solution.py:23
  360.0 5.2 %collective-permute-start.16 = (f32[8,1,128]{2,0,1:T(8,128)S(1)}, f32[8,1,128]{2,0,1:T(8,128)S(1)}, u32[]{:S(2)}, u32[]{:S(2)}) collective-permute-start(f32[8,1,128]{2,0,1:T(8,128)S(1)} %get-tuple-element.17), channel_id=1, source_target_pairs={{0,1},{1,2},{2,3},{3,4},{4,5},{5,6},{6,7},{7,0},{8,9},{9,10},{10,1... | collective-permute-start | bytes 12296 | tf_op jit(solution)/shard_map/ppermute | solution.py:21
  365.4 11.1 %collective-permute-start.18 = (f32[8,66,1]{2,0,1:T(8,128)S(1)}, f32[8,66,1]{2,0,1:T(8,128)S(1)}, u32[]{:S(2)}, u32[]{:S(2)}) collective-permute-start(f32[8,66,1]{2,0,1:T(8,128)S(1)} %get-tuple-element.8), channel_id=1, source_target_pairs={{0,8},{8,16},{16,24},{24,32},{32,40},{40,48},{48,56},{56,64},{64,7... | collective-permute-start | bytes 6344 | tf_op jit(solution)/shard_map/ppermute | solution.py:21
  365.5 11.0 %collective-permute-start.19 = (f32[8,66,1]{2,0,1:T(8,128)S(1)}, f32[8,66,1]{2,0,1:T(8,128)S(1)}, u32[]{:S(2)}, u32[]{:S(2)}) collective-permute-start(f32[8,66,1]{2,0,1:T(8,128)S(1)} %get-tuple-element.9), channel_id=1, source_target_pairs={{8,0},{16,8},{24,16},{32,24},{40,32},{48,40},{56,48},{64,56},{72,6... | collective-permute-start | bytes 6344 | tf_op jit(solution)/shard_map/ppermute | solution.py:23
where the time goes:
time: 382 us; the launch traced here: 378 us
  local copies, waits for them, and re-layouts  107 us (28%)
  blocking collectives  92 us (24%)
  starting transfers between devices  73.5 us (19%)
  matrix products  58.4 us (15%)
  waiting for transfers between devices  36.9 us (10%)
  other arithmetic  9.58 us (3%)
    unnamed x13, local copies, waits for them, and re-layouts  65.7 us
    dot_general x48, matrix products, contract(): return jnp.einsum(form, left, right, precision=FULL_PRECISION)  58.4 us
    all_to_all x3, blocking collectives, filter_tile(): lax.all_to_all(tile, 'lon', split_axis=1, concat_axis=2, tiled=True)  50.2 us
    ppermute x10, starting transfers between devices, with_halo(): lax.ppermute(head, axis, [((i + 1) % count, i) for i in range(count)])  48.9 us
    all_to_all x3, blocking collectives, filter_tile(): lax.all_to_all(filtered, 'lon', split_axis=2, concat_axis=1, tiled=True)  41.8 us
    all_to_all x5, local copies, waits for them, and re-layouts, filter_tile(): lax.all_to_all(filtered, 'lon', split_axis=2, concat_axis=1, tiled=True)  20.8 us
    ppermute x10, waiting for transfers between devices, with_halo(): lax.ppermute(tail, axis, [(i, (i + 1) % count) for i in range(count)])  18.9 us
    reshape x4, local copies, waits for them, and re-layouts, zonal_filter(): return (result / float(RADIX * RADIX)).reshape(planes, row_count, length)  17.6 us
  transfers between devices with their start and end apart: 22, of which 10 were waited for; matrix products, arithmetic and copies ran while one was open for 8% of the time, Pallas kernels for 0%

commit v1 on v0

v1 whole, which is shorter than its diff:
```python
import functools
import math

import jax
import jax.numpy as jnp
import numpy as np
from jax import lax
from jax.experimental import pallas as pl
from jax.experimental.pallas import tpu as pltpu
from jax.sharding import PartitionSpec as P

STEPS = 4
LEVELS = 8
ROWS = 64
LANES = 128
TILES = 32
NLON = TILES * LANES
BLOCKS = 8
PAIRS = 4
HALO = 8
EXT = ROWS + 2 * HALO
PLANES = LEVELS + 5
MASK = LEVELS + 4
EDGE = 4
LATS = 8

F32 = jnp.float32


def tables():
    n = np.arange(LANES)
    angle = 2 * np.pi * (np.outer(n, n) % LANES) / LANES
    cos, sin = np.cos(angle), np.sin(angle)
    wide = np.block([[cos, -sin], [sin, cos]])
    high = wide.astype(jnp.bfloat16)
    low = (wide - high.astype(np.float64)).astype(jnp.bfloat16)
    q = np.arange(8)[:, None, None]
    c = np.arange(4)[None, :, None]
    first = 2 * np.pi * ((q * (n[None, None, :] + LANES * c)) % NLON) / NLON
    r = np.arange(4)[:, None]
    second = 2 * np.pi * ((r * n[None, :]) % 512) / 512

    def spread(values):
        values = values.reshape(-1, 1, LANES)
        return np.broadcast_to(values, (values.shape[0], 8, LANES)).astype(np.float32)

    turn = np.concatenate(
        [spread(np.cos(first)), spread(np.sin(first)), spread(np.cos(second)), spread(np.sin(second))]
    )
    return high, low, turn


def cadd(x, y):
    return x[0] + y[0], x[1] + y[1]


def csub(x, y):
    return x[0] - y[0], x[1] - y[1]


def quarter(x, sign):
    if sign < 0:
        return x[1], -x[0]
    return -x[1], x[0]


def dft4(x, sign):
    even, odd = cadd(x[0], x[2]), csub(x[0], x[2])
    even2, odd2 = cadd(x[1], x[3]), quarter(csub(x[1], x[3]), sign)
    return [cadd(even, even2), cadd(odd, odd2), csub(even, even2), csub(odd, odd2)]


def dft8(x, sign):
    even = dft4([x[0], x[2], x[4], x[6]], sign)
    odd = dft4([x[1], x[3], x[5], x[7]], sign)
    half = math.sqrt(0.5)

    def eighth(v):
        rot = quarter(v, sign)
        return (v[0] + rot[0]) * half, (v[1] + rot[1]) * half

    odd[1] = eighth(odd[1])
    odd[2] = quarter(odd[2], sign)
    odd[3] = quarter(eighth(odd[3]), sign)
    return [cadd(e, o) for e, o in zip(even, odd)] + [csub(e, o) for e, o in zip(even, odd)]


def cmul(x, cos, sin, sign):
    if sign < 0:
        return x[0] * cos + x[1] * sin, x[1] * cos - x[0] * sin
    return x[0] * cos - x[1] * sin, x[1] * cos + x[0] * sin


def split_dot(left, high_ref, low_ref):
    high = left.astype(jnp.bfloat16)
    low = (left - high.astype(F32)).astype(jnp.bfloat16)
    dot = functools.partial(jnp.dot, preferred_element_type=F32)
    return dot(high, high_ref[...]) + (dot(low, high_ref[...]) + dot(high, low_ref[...]))


def filter_circles(real, imag, cuts, high_ref, low_ref, turn_ref):
    shape = (8, 4, 8, LANES)
    cos1 = turn_ref[0:32].reshape(shape)
    sin1 = turn_ref[32:64].reshape(shape)
    real, imag = real.reshape(shape), imag.reshape(shape)
    parts = dft8([(real[a], imag[a]) for a in range(8)], -1)
    parts = [cmul(parts[q], cos1[q], sin1[q], -1) for q in range(8)]
    real = jnp.stack([p[0] for p in parts])
    imag = jnp.stack([p[1] for p in parts])
    parts = dft4([(real[:, c], imag[:, c]) for c in range(4)], -1)
    parts = [parts[0]] + [
        cmul(parts[r], turn_ref[64 + r], turn_ref[68 + r], -1) for r in range(1, 4)
    ]
    real = jnp.concatenate([p[0] for p in parts]).reshape(256, LANES)
    imag = jnp.concatenate([p[1] for p in parts]).reshape(256, LANES)
    spec = split_dot(jnp.concatenate([real, imag], axis=1), high_ref, low_ref)
    wave = lax.broadcasted_iota(jnp.int32, (TILES, 8, LANES), 0) + TILES * lax.broadcasted_iota(
        jnp.int32, (TILES, 8, LANES), 2
    )
    wave = jnp.minimum(wave, NLON - wave)
    kept = jnp.where(wave <= cuts[None], 1.0 / NLON, 0.0).astype(F32).reshape(256, LANES)
    real = spec[:, :LANES] * kept
    imag = spec[:, LANES:] * kept
    back = split_dot(jnp.concatenate([imag, real], axis=1), high_ref, low_ref)
    real = back[:, LANES:].reshape(4, 8, 8, LANES)
    imag = back[:, :LANES].reshape(4, 8, 8, LANES)
    parts = [(real[0], imag[0])] + [
        cmul((real[r], imag[r]), turn_ref[64 + r], turn_ref[68 + r], 1) for r in range(1, 4)
    ]
    parts = dft4(parts, 1)
    real = jnp.stack([p[0] for p in parts], axis=1)
    imag = jnp.stack([p[1] for p in parts], axis=1)
    parts = [cmul((real[q], imag[q]), cos1[q], sin1[q], 1) for q in range(8)]
    parts = dft8(parts, 1)
    real = jnp.concatenate([p[0] for p in parts])
    imag = jnp.concatenate([p[1] for p in parts])
    return real, imag


def iota(shape, dim):
    return lax.broadcasted_iota(jnp.int32, shape, dim)


def circle_step(x, coef, north, south):
    shape = (TILES * 2, 8, LANES)
    lane = iota(shape, 2)
    row = iota(shape, 1)
    east = pltpu.roll(x, LANES - 1, 2)
    east = jnp.where(lane == LANES - 1, jnp.concatenate([east[2:], east[:2]]), east)
    west = pltpu.roll(x, 1, 2)
    west = jnp.where(lane == 0, jnp.concatenate([west[-2:], west[:-2]]), west)
    up = jnp.where(row == 7, north, pltpu.roll(x, 7, 1))
    down = jnp.where(row == 0, south, pltpu.roll(x, 1, 1))
    full = (TILES, 2, 8, LANES)
    x4 = x.reshape(full)
    total = x4
    for k, near in enumerate((east, west, up, down)):
        total = total + coef[:, k : k + 1] * (x4 - near.reshape(full))
    return total.reshape(shape)


def kernel(
    cot, diff_east, diff_north, flow_east, flow_north, sea, cutoff, high_ref, low_ref, turn_ref,
    out,
    ext, lam, fil, coef, coef_src, lam_x, coef_x, coef_x_src, row_x, rim_e, rim_w, rim_src,
    packed, packed_l, packed_r, wide_coef, edge_out, edge_in,
    row_send, row_recv, col_send, col_recv, in_send, in_recv, cf_send, cf_recv,
    lx_send, lx_recv, cx_send, cx_recv, step_send, step_recv, out_send, out_recv, ox_send, ox_recv,
):
    lon = lax.axis_index("lon")
    lat = lax.axis_index("lat")
    block = lon // PAIRS
    pair = lax.rem(lon, PAIRS)
    polar = jnp.logical_or(lat == 0, lat == LATS - 1)
    beside = jnp.logical_or(lat == 1, lat == LATS - 2)
    edge_block = jnp.where(lat < LATS // 2, BLOCKS - 1, 0)
    has_extra = jnp.logical_and(polar, block == edge_block)
    polar_lat = jnp.where(lat < LATS // 2, 0, LATS - 1)
    beside_lat = jnp.where(lat < LATS // 2, 1, LATS - 2)

    barrier = pltpu.get_barrier_semaphore()

    def at(to_lat, to_lon):
        return {"lon": to_lon, "lat": to_lat}

    def hail(to_lat, to_lon):
        pl.semaphore_signal(
            barrier, inc=1, device_id=at(to_lat, to_lon), device_id_type=pl.DeviceIdType.MESH
        )

    def remote(src, dst, send, recv, to_lat, to_lon):
        return pltpu.make_async_remote_copy(
            src_ref=src, dst_ref=dst, send_sem=send, recv_sem=recv,
            device_id=at(to_lat, to_lon), device_id_type=pl.DeviceIdType.MESH,
        )

    def wait_bytes(ref, sem):
        pltpu.make_async_copy(ref, ref, sem).wait()

    right = lax.rem(lon + 1, TILES)
    left = lax.rem(lon + TILES - 1, TILES)

    @pl.when(lat > 0)
    def _():
        hail(lat - 1, lon)

    @pl.when(lat < LATS - 1)
    def _():
        hail(lat + 1, lon)

    @pl.when(polar)
    def _():
        def greet(s, carry):
            hail(lat, lax.rem(lon + s, TILES))
            return carry

        lax.fori_loop(1, TILES, greet, 0)

    @pl.when(jnp.logical_not(polar))
    def _():
        hail(lat, left)
        hail(lat, right)

    @pl.when(beside)
    def _():
        for p in range(PAIRS):
            hail(polar_lat, edge_block * PAIRS + p)

    @pl.when(has_extra)
    def _():
        def greet(d, carry):
            hail(beside_lat, d)
            return carry

        lax.fori_loop(0, TILES, greet, 0)

    main = pl.ds(HALO, ROWS)
    ext[0:LEVELS, HALO : HALO + ROWS] = cot[...]
    ext[LEVELS, HALO : HALO + ROWS] = diff_east[...]
    ext[LEVELS + 1, HALO : HALO + ROWS] = flow_east[...]
    ext[LEVELS + 2, HALO : HALO + ROWS] = diff_north[...]
    ext[LEVELS + 3, HALO : HALO + ROWS] = flow_north[...]
    mask = sea[...].astype(F32)
    ext[MASK, HALO : HALO + ROWS] = mask

    @pl.when(lat == 0)
    def _():
        ext[:, 0:HALO] = jnp.zeros((PLANES, HALO, LANES), F32)

    @pl.when(lat == LATS - 1)
    def _():
        ext[:, HALO + ROWS : EXT] = jnp.zeros((PLANES, HALO, LANES), F32)

    @pl.when(polar)
    def _():
        rim_src[...] = mask * (diff_east[...] - 0.5 * flow_east[...])
        edge_in[...] = jnp.zeros(edge_in.shape, F32)
        lam[lon] = cot[pl.ds(2 * pair, 2), pl.ds(pl.multiple_of(8 * block, 8), 8), :]

    peers = jnp.where(polar, TILES, 4)
    peers = peers + jnp.where(has_extra, TILES, 0) + jnp.where(beside, PAIRS, 0)
    pl.semaphore_wait(barrier, peers)

    low_rows = ext.at[:, pl.ds(HALO, HALO)]
    high_rows = ext.at[:, pl.ds(ROWS, HALO)]
    south_rows = ext.at[:, pl.ds(0, HALO)]
    north_rows = ext.at[:, pl.ds(HALO + ROWS, HALO)]
    to_south = remote(low_rows, north_rows, row_send.at[0], row_recv.at[0], lat - 1, lon)
    to_north = remote(high_rows, south_rows, row_send.at[1], row_recv.at[1], lat + 1, lon)

    @pl.when(lat > 0)
    def _():
        to_south.start()

    @pl.when(lat < LATS - 1)
    def _():
        to_north.start()

    def wait_rows():
        @pl.when(lat < LATS - 1)
        def _():
            to_south.wait_recv()

        @pl.when(lat > 0)
        def _():
            to_north.wait_recv()

    @pl.when(polar)
    def _():
        to_left = remote(ext.at[MASK, main], rim_e, col_send.at[0], col_recv.at[0], lat, left)
        to_right = remote(rim_src, rim_w, col_send.at[1], col_recv.at[1], lat, right)
        to_left.start()
        to_right.start()

        def send_in(s, carry):
            owner = lax.rem(lon + s, TILES)
            rows = pl.ds(pl.multiple_of(8 * (owner // PAIRS), 8), 8)
            remote(
                cot.at[pl.ds(2 * lax.rem(owner, PAIRS), 2), rows], lam.at[lon],
                in_send.at[0], in_recv.at[0], lat, owner,
            ).start()
            return carry

        lax.fori_loop(1, TILES, send_in, 0)

        wait_rows()
        to_left.wait_recv()
        to_right.wait_recv()
        lane = iota((ROWS, LANES), 1)
        mine = ext[MASK, HALO : HALO + ROWS]
        mask_east = jnp.where(
            lane == LANES - 1, pltpu.roll(rim_e[...], LANES - 1, 1), pltpu.roll(mine, LANES - 1, 1)
        )
        plus_west = jnp.where(
            lane == 0, pltpu.roll(rim_w[...], 1, 1), pltpu.roll(rim_src[...], 1, 1)
        )
        mask_north = ext[MASK, HALO + 1 : HALO + ROWS + 1]
        tail = slice(HALO - 1, HALO + ROWS - 1)
        plus_south = ext[MASK, tail] * (ext[LEVELS + 2, tail] - 0.5 * ext[LEVELS + 3, tail])
        shape = (BLOCKS, 8, LANES)
        coef_src[:, 0] = (
            mine * mask_east * (-diff_east[...] - 0.5 * flow_east[...])
        ).reshape(shape)
        coef_src[:, 1] = (-mine * plus_west).reshape(shape)
        coef_src[:, 2] = (
            mine * mask_north * (-diff_north[...] - 0.5 * flow_north[...])
        ).reshape(shape)
        coef_src[:, 3] = (-mine * plus_south).reshape(shape)

        def send_coef(s, carry):
            owner = lax.rem(lon + s, TILES)
            remote(
                coef_src.at[owner // PAIRS], coef.at[lon], cf_send.at[0], cf_recv.at[0], lat, owner
            ).start()
            return carry

        lax.fori_loop(1, TILES, send_coef, 0)
        coef[lon] = coef_src[block]

        row = iota((8, LANES), 0)
        cuts = jnp.zeros((8, LANES), jnp.int32)
        for j in range(8):
            cuts = jnp.where(row == j, cutoff[8 * block + j], cuts)

        wait_bytes(lam.at[pl.ds(0, TILES - 1)], in_recv.at[0])

        def step(s, carry):
            real, imag = filter_circles(
                lam[:, 0], lam[:, 1], cuts, high_ref, low_ref, turn_ref
            )
            fil[:, 0] = real
            fil[:, 1] = imag
            x = fil[...].reshape(2 * TILES, 8, LANES)
            edge_out[s, 0] = x[:, 0:1]
            edge_out[s, 1] = x[:, 7:8]
            go_south = remote(
                edge_out.at[s, 0], edge_in.at[s, 0], step_send.at[s, 0], step_recv.at[s, 0],
                lat, lon - PAIRS,
            )
            go_north = remote(
                edge_out.at[s, 1], edge_in.at[s, 1], step_send.at[s, 1], step_recv.at[s, 1],
                lat, lon + PAIRS,
            )

            @pl.when(block > 0)
            def _():
                go_south.start()

            @pl.when(block < BLOCKS - 1)
            def _():
                go_north.start()

            @pl.when(s == 0)
            def _():
                wait_bytes(coef.at[pl.ds(0, TILES - 1)], cf_recv.at[0])

            @pl.when(jnp.logical_and(has_extra, s == 0))
            def _():
                wait_bytes(lam_x, lx_recv.at[0])
                wait_bytes(coef_x, cx_recv.at[0])

            @pl.when(has_extra)
            def _():
                beyond = lam_x[...].reshape(2 * TILES, 8, LANES)

                @pl.when(lat == 0)
                def _():
                    edge_in[s, 0] = beyond[:, 0:1]

                @pl.when(lat > 0)
                def _():
                    edge_in[s, 1] = beyond[:, 7:8]

                lam_x[...] = circle_step(
                    beyond, coef_x[...], edge_out[s, 0], edge_out[s, 1]
                ).reshape(lam_x.shape)

            @pl.when(block < BLOCKS - 1)
            def _():
                go_south.wait_recv()

            @pl.when(block > 0)
            def _():
                go_north.wait_recv()

            lam[...] = circle_step(x, coef[...], edge_in[s, 0], edge_in[s, 1]).reshape(lam.shape)
            return carry

        lax.fori_loop(0, STEPS, step, 0)

        mine_out = (pl.ds(2 * pair, 2), pl.ds(pl.multiple_of(8 * block, 8), 8))

        def send_out(s, carry):
            tile = lax.rem(lon + s, TILES)
            remote(
                lam.at[tile], out.at[mine_out], out_send.at[0], out_recv.at[0], lat, tile
            ).start()
            return carry

        lax.fori_loop(1, TILES, send_out, 0)

        @pl.when(has_extra)
        def _():
            def send_x(s, carry):
                tile = lax.rem(lon + s, TILES)
                remote(
                    lam_x.at[tile], row_x.at[pl.ds(2 * pair, 2)], ox_send.at[0], ox_recv.at[0],
                    beside_lat, tile,
                ).start()
                return carry

            lax.fori_loop(0, TILES, send_x, 0)

        out[pl.ds(2 * pair, 2), pl.ds(pl.multiple_of(8 * block, 8), 8), :] = lam[lon]

        to_left.wait_send()
        to_right.wait_send()
        wait_bytes(lam.at[pl.ds(0, TILES - 1)], in_send.at[0])
        wait_bytes(coef.at[pl.ds(0, TILES - 1)], cf_send.at[0])

        def drain(s, carry):
            @pl.when(block > 0)
            def _():
                wait_bytes(edge_out.at[s, 0], step_send.at[s, 0])

            @pl.when(block < BLOCKS - 1)
            def _():
                wait_bytes(edge_out.at[s, 1], step_send.at[s, 1])

            return carry

        lax.fori_loop(0, STEPS, drain, 0)

        @pl.when(has_extra)
        def _():
            wait_bytes(lam_x, ox_send.at[0])

        wait_bytes(lam.at[pl.ds(0, TILES - 1)], out_send.at[0])
        wait_bytes(lam.at[pl.ds(0, TILES - 1)], out_recv.at[0])

    @pl.when(jnp.logical_not(polar))
    def _():
        beside_rows = pl.ds(pl.multiple_of(jnp.where(lat == 1, 0, ROWS - 8), 8), 8)

        @pl.when(beside)
        def _():
            for p in range(PAIRS):
                remote(
                    cot.at[pl.ds(2 * p, 2), beside_rows], lam_x.at[lon],
                    lx_send.at[0], lx_recv.at[0], polar_lat, edge_block * PAIRS + p,
                ).start()

        wait_rows()
        lane = iota((EXT, LANES), 1)
        total = jnp.zeros((EXT, LANES), F32)
        for p in range(PLANES):
            v = ext[p]
            u = jnp.where(lane < EDGE, v, pltpu.roll(v, 2 * EDGE, 1))
            if p:
                u = pltpu.roll(u, 8 * p, 1)
            total = jnp.where((lane // 8) == p, u, total)
        packed[...] = total
        to_left = remote(packed, packed_r, col_send.at[0], col_recv.at[0], lat, left)
        to_right = remote(packed, packed_l, col_send.at[1], col_recv.at[1], lat, right)
        to_left.start()
        to_right.start()
        to_left.wait_recv()
        to_right.wait_recv()

        def beyond(p):
            from_right = packed_r[...]
            if p:
                from_right = pltpu.roll(from_right, LANES - 8 * p, 1)
            from_left = pltpu.roll(packed_l[...], (LANES - 8 - 8 * p) % LANES, 1)
            return jnp.where(lane < LANES // 2, from_right, from_left)

        def east_of(x):
            here, there = (pltpu.roll(v, LANES - 1, 1) for v in x)
            last = lane == LANES - 1
            return jnp.where(last, there, here), jnp.where(last, here, there)

        def west_of(x):
            here, there = (pltpu.roll(v, 1, 1) for v in x)
            last = lane == 0
            return jnp.where(last, there, here), jnp.where(last, here, there)

        def north_of(x):
            return [pltpu.roll(v, EXT - 1, 0) for v in x]

        def south_of(x):
            return [pltpu.roll(v, 1, 0) for v in x]

        def both(p):
            return ext[p], beyond(p)

        kappa_e, speed_e, kappa_n, speed_n, open_m = (both(LEVELS + k) for k in range(5))

        def minus(kappa, speed):
            return [m * (-k - 0.5 * f) for m, k, f in zip(open_m, kappa, speed)]

        def plus(kappa, speed):
            return [m * (k - 0.5 * f) for m, k, f in zip(open_m, kappa, speed)]

        faces = (
            [a * b for a, b in zip(minus(kappa_e, speed_e), east_of(open_m))],
            [-a * b for a, b in zip(open_m, west_of(plus(kappa_e, speed_e)))],
            [a * b for a, b in zip(minus(kappa_n, speed_n), north_of(open_m))],
            [-a * b for a, b in zip(open_m, south_of(plus(kappa_n, speed_n)))],
        )
        for k in range(4):
            for side in range(2):
                wide_coef[k, side] = faces[k][side]

        @pl.when(beside)
        def _():
            rows = pl.ds(pl.multiple_of(jnp.where(lat == 1, HALO, ROWS), 8), 8)
            coef_x_src[...] = wide_coef[:, 0, rows]
            for p in range(PAIRS):
                remote(
                    coef_x_src, coef_x.at[lon], cx_send.at[0], cx_recv.at[0],
                    polar_lat, edge_block * PAIRS + p,
                ).start()

        def level(p, carry):
            from_right = pltpu.roll(packed_r[...], LANES - 8 * p, 1)
            from_left = pltpu.roll(packed_l[...], LANES - 8 - 8 * p, 1)
            x = (ext[p], jnp.where(lane < LANES // 2, from_right, from_left))
            for _ in range(STEPS):
                new = list(x)
                for k, near in enumerate((east_of(x), west_of(x), north_of(x), south_of(x))):
                    for side in range(2):
                        new[side] = new[side] + wide_coef[k, side] * (x[side] - near[side])
                x = tuple(new)
            out[p] = x[0][HALO : HALO + ROWS]
            return carry

        lax.fori_loop(0, LEVELS, level, 0)

        to_left.wait_send()
        to_right.wait_send()

        @pl.when(beside)
        def _():
            wait_bytes(cot.at[:, pl.ds(0, 8)], lx_send.at[0])
            wait_bytes(coef_x.at[pl.ds(0, PAIRS)], cx_send.at[0])
            wait_bytes(row_x, ox_recv.at[0])

        row = iota((LEVELS, 8, LANES), 1)

        @pl.when(lat == 1)
        def _():
            out[:, 0:8] = jnp.where(row < EDGE, row_x[...], out[:, 0:8])

        @pl.when(lat == LATS - 2)
        def _():
            out[:, ROWS - 8 : ROWS] = jnp.where(row < EDGE, out[:, ROWS - 8 : ROWS], row_x[...])

    @pl.when(lat > 0)
    def _():
        to_south.wait_send()

    @pl.when(lat < LATS - 1)
    def _():
        to_north.wait_send()


def shards(cotangent, diff_east, diff_north, flow_east, flow_north, sea_mask, cutoff):
    high, low, turn = tables()
    vmem = pl.BlockSpec(memory_space=pltpu.VMEM)
    smem = pl.BlockSpec(memory_space=pltpu.SMEM)
    dma = pltpu.SemaphoreType.DMA
    circles = pltpu.VMEM((TILES, 2, 8, LANES), F32)
    faces = pltpu.VMEM((TILES, 4, 8, LANES), F32)
    plane = pltpu.VMEM((ROWS, LANES), F32)
    tall = pltpu.VMEM((EXT, LANES), F32)
    edges = pltpu.VMEM((STEPS, 2, 2 * TILES, 1, LANES), F32)
    return pl.pallas_call(
        kernel,
        out_shape=jax.ShapeDtypeStruct((LEVELS, ROWS, LANES), F32),
        in_specs=[vmem] * 6 + [smem] + [vmem] * 3,
        out_specs=vmem,
        scratch_shapes=[
            pltpu.VMEM((PLANES, EXT, LANES), F32),
            circles,
            circles,
            faces,
            pltpu.VMEM((BLOCKS, 4, 8, LANES), F32),
            circles,
            faces,
            pltpu.VMEM((4, 8, LANES), F32),
            pltpu.VMEM((LEVELS, 8, LANES), F32),
            plane,
            plane,
            plane,
            tall,
            tall,
            tall,
            pltpu.VMEM((4, 2, EXT, LANES), F32),
            edges,
            edges,
            dma((2,)), dma((2,)), dma((2,)), dma((2,)),
            dma((1,)), dma((1,)), dma((1,)), dma((1,)),
            dma((1,)), dma((1,)), dma((1,)), dma((1,)),
            dma((STEPS, 2)), dma((STEPS, 2)),
            dma((1,)), dma((1,)), dma((1,)), dma((1,)),
        ],
        compiler_params=pltpu.CompilerParams(
            collective_id=0, has_side_effects=True, vmem_limit_bytes=40 * 1024 * 1024
        ),
    )(
        cotangent, diff_east, diff_north, flow_east, flow_north, sea_mask, cutoff,
        jnp.asarray(high), jnp.asarray(low), jnp.asarray(turn),
    )


def solution(mesh):
    return jax.shard_map(
        shards,
        mesh=mesh,
        in_specs=(
            P(None, "lat", "lon"),
            P("lat", "lon"),
            P("lat", "lon"),
            P("lat", "lon"),
            P("lat", "lon"),
            P("lat", "lon"),
            P("lat"),
        ),
        out_specs=P(None, "lat", "lon"),
        check_vma=False,
    )
```

time: 382 us -> 56.1 us (0.15)
  local copies, waits for them, and re-layouts: 107 us -> 8.86 us
  blocking collectives: 92 us -> 0 us
  starting transfers between devices: 73.5 us -> 0 us
  matrix products: 58.4 us -> 0 us
  Pallas kernels: 0 us -> 46.2 us
  waiting for transfers between devices: 36.9 us -> 0 us
  other arithmetic: 9.58 us -> 0 us
    all_to_all x6 -> x0, blocking collectives: 92 us -> none  [the longest x3 50.2 us: filter_tile(): lax.all_to_all(tile, 'lon', split_axis=1, concat_axis=2, tiled=True)]
    ppermute x20 -> x0, starting transfers between devices: 59 us -> none  [the longest x10 48.9 us: with_halo(): lax.ppermute(head, axis, [((i + 1) % count, i) for i in range(count)])]
    dot_general x48 -> x0, matrix products: 58.4 us -> none  [contract(): return jnp.einsum(form, left, right, precision=FULL_PRECISION)]
    unnamed x13 -> x21, local copies, waits for them, and re-layouts: 65.7 us -> 8.86 us
    pallas_call x0 -> x1, Pallas kernels: none -> 46.2 us  [shards(): pl.pallas_call(kernel, out_shape=jax.ShapeDtypeStruct((LEVELS, ROWS, LANE...]
    ppermute x20 -> x0, waiting for transfers between devices: 23.9 us -> none  [the longest x10 18.9 us: with_halo(): lax.ppermute(tail, axis, [(i, (i + 1) % count) for i in range(count)])]
    all_to_all x9 -> x0, local copies, waits for them, and re-layouts: 21.1 us -> none  [the longest x5 20.8 us: filter_tile(): lax.all_to_all(filtered, 'lon', split_axis=2, concat_axis=1, tiled=True)]
    reshape x8 -> x0, local copies, waits for them, and re-layouts: 18.2 us -> none  [the longest x4 17.6 us: zonal_filter(): return (result / float(RADIX * RADIX)).reshape(planes, row_count, length)]
  transfers between devices with their start and end apart: 22 -> 0, of which waited for: 10 -> 0; matrix products, arithmetic and copies ran while one was open for 8% -> 0% of each run, Pallas kernels for 0% -> 0%
where the time goes in v1:
time: 56.1 us; the launch traced here: 55.1 us
  Pallas kernels  46.2 us (82%)
  local copies, waits for them, and re-layouts  8.86 us (16%)
    pallas_call x1, Pallas kernels, shards(): pl.pallas_call(kernel, out_shape=jax.ShapeDtypeStruct((LEVELS, ROWS, LANE...  46.2 us
    unnamed x21, local copies, waits for them, and re-layouts  8.86 us

profile of v1, /device:TPU:1, one launch (start us, length us, event | category | flops | bytes accessed | tf_op | source)
XLA Modules:
  0.0 55.1 jit_solution(5559499147168019419)
XLA Ops:
  0.0 0.0 copy-start
  0.0 1.0 %copy-done = f32[72,8,128]{2,1,0:T(8,128)S(1)} copy-done((f32[72,8,128]{2,1,0:T(8,128)S(1)}, f32[72,8,128]{2,1,0:T(8,128)}, u32[]{:S(2)}) %copy-start) | copy-done | bytes 294936
  1.0 0.0 copy-start.1
  1.0 0.9 %copy-done.1 = f32[8,64,128]{2,1,0:T(8,128)S(1)} copy-done((f32[8,64,128]{2,1,0:T(8,128)S(1)}, f32[8,64,128]{2,1,0:T(8,128)}, u32[]{:S(2)}) %copy-start.1) | copy-done | bytes 262168
  1.9 0.0 copy-start.2
  1.9 0.9 %copy-done.2 = bf16[256,256]{1,0:T(8,128)(2,1)S(1)} copy-done((bf16[256,256]{1,0:T(8,128)(2,1)S(1)}, bf16[256,256]{1,0:T(8,128)(2,1)}, u32[]{:S(2)}) %copy-start.2) | copy-done | bytes 131096
  2.8 0.0 copy-start.3
  2.8 0.9 %copy-done.3 = bf16[256,256]{1,0:T(8,128)(2,1)S(1)} copy-done((bf16[256,256]{1,0:T(8,128)(2,1)S(1)}, bf16[256,256]{1,0:T(8,128)(2,1)}, u32[]{:S(2)}) %copy-start.3) | copy-done | bytes 131096
  3.7 0.0 copy-start.4
  3.7 0.8 %copy-done.4 = f32[64,128]{1,0:T(8,128)S(1)} copy-done((f32[64,128]{1,0:T(8,128)S(1)}, f32[64,128]{1,0:T(8,128)}, u32[]{:S(2)}) %copy-start.4) | copy-done | bytes 32792
  4.5 0.0 copy-start.5
  4.5 0.8 %copy-done.5 = f32[64,128]{1,0:T(8,128)S(1)} copy-done((f32[64,128]{1,0:T(8,128)S(1)}, f32[64,128]{1,0:T(8,128)}, u32[]{:S(2)}) %copy-start.5) | copy-done | bytes 32792
  5.2 0.0 copy-start.6
  5.2 0.8 %copy-done.6 = f32[64,128]{1,0:T(8,128)S(1)} copy-done((f32[64,128]{1,0:T(8,128)S(1)}, f32[64,128]{1,0:T(8,128)}, u32[]{:S(2)}) %copy-start.6) | copy-done | bytes 32792
  6.0 0.0 copy-start.7
  6.0 0.8 %copy-done.7 = f32[64,128]{1,0:T(8,128)S(1)} copy-done((f32[64,128]{1,0:T(8,128)S(1)}, f32[64,128]{1,0:T(8,128)}, u32[]{:S(2)}) %copy-start.7) | copy-done | bytes 32792
  6.8 0.0 copy-start.8
  6.8 0.8 %copy-done.8 = s32[64,128]{1,0:T(8,128)S(1)} copy-done((s32[64,128]{1,0:T(8,128)S(1)}, s32[64,128]{1,0:T(8,128)}, u32[]{:S(2)}) %copy-start.8) | copy-done | bytes 32792
  7.5 0.0 copy-start.9
  7.5 0.7 %copy-done.9 = s32[64]{0:T(128)S(1)} copy-done((s32[64]{0:T(128)S(1)}, s32[64]{0:T(128)}, u32[]{:S(2)}) %copy-start.9) | copy-done | bytes 280
  8.2 46.2 %shard_map.100 = f32[8,64,128]{2,1,0:T(8,128)S(1)} custom-call(f32[8,64,128]{2,1,0:T(8,128)S(1)} %copy-done.1, f32[64,128]{1,0:T(8,128)S(1)} %copy-done.4, f32[64,128]{1,0:T(8,128)S(1)} %copy-done.5, f32[64,128]{1,0:T(8,128)S(1)} %copy-done.6, f32[64,128]{1,0:T(8,128)S(1)} %copy-done.7, s32[64,128]{1,0:T(8,128)S(1)} %copy-done.8, s32[64]{0:T(128)S(1)} %copy-done.9, ...), custom_call_target="tpu_custom_call" | custom-call | tf_op jit(solution)/shard_map/pallas_call | solution.py:597
  54.4 0.7 %copy.12 = f32[8,64,128]{2,1,0:T(8,128)} copy(f32[8,64,128]{2,1,0:T(8,128)S(1)} %shard_map.100) | data formatting | bytes 524288
Async XLA Ops:
  0.0 1.0 %copy-start = (f32[72,8,128]{2,1,0:T(8,128)S(1)}, f32[72,8,128]{2,1,0:T(8,128)}, u32[]{:S(2)}) copy-start(f32[72,8,128]{2,1,0:T(8,128)} %constant.8.clone.turn_ref) | copy-start | bytes 884740
  1.0 0.9 %copy-start.1 = (f32[8,64,128]{2,1,0:T(8,128)S(1)}, f32[8,64,128]{2,1,0:T(8,128)}, u32[]{:S(2)}) copy-start(f32[8,64,128]{2,1,0:T(8,128)} %cot.1) | copy-start | bytes 786436
  1.9 0.9 %copy-start.2 = (bf16[256,256]{1,0:T(8,128)(2,1)S(1)}, bf16[256,256]{1,0:T(8,128)(2,1)}, u32[]{:S(2)}) copy-start(bf16[256,256]{1,0:T(8,128)(2,1)} %constant.7.clone.low_ref) | copy-start | bytes 393220
  2.8 0.9 %copy-start.3 = (bf16[256,256]{1,0:T(8,128)(2,1)S(1)}, bf16[256,256]{1,0:T(8,128)(2,1)}, u32[]{:S(2)}) copy-start(bf16[256,256]{1,0:T(8,128)(2,1)} %constant.6.clone.high_ref) | copy-start | bytes 393220
  3.7 0.8 %copy-start.4 = (f32[64,128]{1,0:T(8,128)S(1)}, f32[64,128]{1,0:T(8,128)}, u32[]{:S(2)}) copy-start(f32[64,128]{1,0:T(8,128)} %diff_east.1) | copy-start | bytes 98308
  4.5 0.8 %copy-start.5 = (f32[64,128]{1,0:T(8,128)S(1)}, f32[64,128]{1,0:T(8,128)}, u32[]{:S(2)}) copy-start(f32[64,128]{1,0:T(8,128)} %diff_north.1) | copy-start | bytes 98308
  5.2 0.8 %copy-start.6 = (f32[64,128]{1,0:T(8,128)S(1)}, f32[64,128]{1,0:T(8,128)}, u32[]{:S(2)}) copy-start(f32[64,128]{1,0:T(8,128)} %flow_east.1) | copy-start | bytes 98308
  6.0 0.8 %copy-start.7 = (f32[64,128]{1,0:T(8,128)S(1)}, f32[64,128]{1,0:T(8,128)}, u32[]{:S(2)}) copy-start(f32[64,128]{1,0:T(8,128)} %flow_north.1) | copy-start | bytes 98308
  6.8 0.8 %copy-start.8 = (s32[64,128]{1,0:T(8,128)S(1)}, s32[64,128]{1,0:T(8,128)}, u32[]{:S(2)}) copy-start(s32[64,128]{1,0:T(8,128)} %sea.1) | copy-start | bytes 98308
  7.5 0.7 %copy-start.9 = (s32[64]{0:T(128)S(1)}, s32[64]{0:T(128)}, u32[]{:S(2)}) copy-start(s32[64]{0:T(128)} %cutoff.1) | copy-start | bytes 772

commit v2 on v1

v2 whole, which is shorter than its diff:
```python
import functools
import math

import jax
import jax.numpy as jnp
import numpy as np
from jax import lax
from jax.experimental import pallas as pl
from jax.experimental.pallas import tpu as pltpu
from jax.sharding import PartitionSpec as P

STEPS = 4
LEVELS = 8
ROWS = 64
LANES = 128
TILES = 32
NLON = TILES * LANES
BLOCKS = 8
PAIRS = 4
HALO = 16
EXT = ROWS + 2 * HALO
WIDE = ROWS + HALO
PLANES = LEVELS + 5
MASK = LEVELS + 4
EDGE = 4
LATS = 8

F32 = jnp.float32


def tables():
    n = np.arange(LANES)
    angle = 2 * np.pi * (np.outer(n, n) % LANES) / LANES
    cos, sin = np.cos(angle), np.sin(angle)
    wide = np.block([[cos, -sin], [sin, cos]])
    q = np.arange(8)[:, None, None]
    c = np.arange(4)[None, :, None]
    first = 2 * np.pi * ((q * (n[None, None, :] + LANES * c)) % NLON) / NLON
    r = np.arange(4)[:, None]
    second = 2 * np.pi * ((r * n[None, :]) % 512) / 512

    def spread(values):
        values = values.reshape(-1, 1, LANES)
        return np.broadcast_to(values, (values.shape[0], 8, LANES)).astype(np.float32)

    turn = np.concatenate(
        [spread(np.cos(first)), spread(np.sin(first)), spread(np.cos(second)), spread(np.sin(second))]
    )
    return wide.astype(np.float32), turn


def cadd(x, y):
    return x[0] + y[0], x[1] + y[1]


def csub(x, y):
    return x[0] - y[0], x[1] - y[1]


def quarter(x, sign):
    if sign < 0:
        return x[1], -x[0]
    return -x[1], x[0]


def dft4(x, sign):
    even, odd = cadd(x[0], x[2]), csub(x[0], x[2])
    even2, odd2 = cadd(x[1], x[3]), quarter(csub(x[1], x[3]), sign)
    return [cadd(even, even2), cadd(odd, odd2), csub(even, even2), csub(odd, odd2)]


def dft8(x, sign):
    even = dft4([x[0], x[2], x[4], x[6]], sign)
    odd = dft4([x[1], x[3], x[5], x[7]], sign)
    half = math.sqrt(0.5)

    def eighth(v):
        rot = quarter(v, sign)
        return (v[0] + rot[0]) * half, (v[1] + rot[1]) * half

    odd[1] = eighth(odd[1])
    odd[2] = quarter(odd[2], sign)
    odd[3] = quarter(eighth(odd[3]), sign)
    return [cadd(e, o) for e, o in zip(even, odd)] + [csub(e, o) for e, o in zip(even, odd)]


def cmul(x, cos, sin, sign):
    if sign < 0:
        return x[0] * cos + x[1] * sin, x[1] * cos - x[0] * sin
    return x[0] * cos - x[1] * sin, x[1] * cos + x[0] * sin


def split_dot(left, high_ref, low_ref):
    high = left.astype(jnp.bfloat16)
    low = (left - high.astype(F32)).astype(jnp.bfloat16)
    dot = functools.partial(jnp.dot, preferred_element_type=F32)
    return dot(high, high_ref[...]) + (dot(low, high_ref[...]) + dot(high, low_ref[...]))


def filter_circles(real, imag, cuts, high_ref, low_ref, turn_ref):
    shape = (8, 4, 8, LANES)
    cos1 = turn_ref[0:32].reshape(shape)
    sin1 = turn_ref[32:64].reshape(shape)
    real, imag = real.reshape(shape), imag.reshape(shape)
    parts = dft8([(real[a], imag[a]) for a in range(8)], -1)
    parts = [cmul(parts[q], cos1[q], sin1[q], -1) for q in range(8)]
    real = jnp.stack([p[0] for p in parts])
    imag = jnp.stack([p[1] for p in parts])
    parts = dft4([(real[:, c], imag[:, c]) for c in range(4)], -1)
    parts = [parts[0]] + [
        cmul(parts[r], turn_ref[64 + r], turn_ref[68 + r], -1) for r in range(1, 4)
    ]
    real = jnp.concatenate([p[0] for p in parts]).reshape(256, LANES)
    imag = jnp.concatenate([p[1] for p in parts]).reshape(256, LANES)
    spec = split_dot(jnp.concatenate([real, imag], axis=1), high_ref, low_ref)
    wave = lax.broadcasted_iota(jnp.int32, (TILES, 8, LANES), 0) + TILES * lax.broadcasted_iota(
        jnp.int32, (TILES, 8, LANES), 2
    )
    wave = jnp.minimum(wave, NLON - wave)
    kept = jnp.where(wave <= cuts[None], 1.0 / NLON, 0.0).astype(F32).reshape(256, LANES)
    real = spec[:, :LANES] * kept
    imag = spec[:, LANES:] * kept
    back = split_dot(jnp.concatenate([imag, real], axis=1), high_ref, low_ref)
    real = back[:, LANES:].reshape(4, 8, 8, LANES)
    imag = back[:, :LANES].reshape(4, 8, 8, LANES)
    parts = [(real[0], imag[0])] + [
        cmul((real[r], imag[r]), turn_ref[64 + r], turn_ref[68 + r], 1) for r in range(1, 4)
    ]
    parts = dft4(parts, 1)
    real = jnp.stack([p[0] for p in parts], axis=1)
    imag = jnp.stack([p[1] for p in parts], axis=1)
    parts = [cmul((real[q], imag[q]), cos1[q], sin1[q], 1) for q in range(8)]
    parts = dft8(parts, 1)
    real = jnp.concatenate([p[0] for p in parts])
    imag = jnp.concatenate([p[1] for p in parts])
    return real, imag


def iota(shape, dim):
    return lax.broadcasted_iota(jnp.int32, shape, dim)


def circle_step(x, coef):
    shape = (TILES * 4, 8, LANES)
    full = (TILES, 2, 2, 8, LANES)
    lane = iota(shape, 2)
    row = iota(full, 3)
    flat = x.reshape(shape)
    east = pltpu.roll(flat, LANES - 1, 2)
    east = jnp.where(lane == LANES - 1, jnp.concatenate([east[4:], east[:4]]), east)
    west = pltpu.roll(flat, 1, 2)
    west = jnp.where(lane == 0, jnp.concatenate([west[-4:], west[:-4]]), west)

    def across(turned, edge):
        turned = turned.reshape(full)
        other = jnp.stack([turned[:, :, 1], turned[:, :, 0]], axis=2)
        return jnp.where(row == edge, other, turned)

    up = across(pltpu.roll(flat, 7, 1), 7)
    down = across(pltpu.roll(flat, 1, 1), 0)
    total = x
    for k, near in enumerate((east.reshape(full), west.reshape(full), up, down)):
        total = total + coef[:, k : k + 1] * (x - near)
    return total


def kernel(
    cot, diff_east_in, diff_north_in, flow_east_in, flow_north_in, sea_in, cutoff_in, wide_in,
    turn_in,
    out,
    sea, cutoff, wide_ref, high_ref, low_ref, turn_ref,
    ext, lam_src, coef_src, cut_src, rim_e, rim_w, rim_src,
    lam, fil, coef, cuts_ref, row_x, packed, packed_l, packed_r, wide_coef, mid_out,
    load_sem, row_send, row_recv, col_send, col_recv, cut_send, cut_recv, in_send, in_recv,
    cf_send, cf_recv, out_send, out_recv, ox_recv, store_sem,
):
    lon = lax.axis_index("lon")
    lat = lax.axis_index("lat")
    y = lax.rem(lon, 4)
    z = lon // 4
    first_band = lat < LATS // 2
    polar = jnp.logical_or(lat == 0, lat == LATS - 1)
    beside = jnp.logical_or(lat == 1, lat == LATS - 2)
    polar_lat = jnp.where(first_band, 0, LATS - 1)
    beside_lat = jnp.where(first_band, 1, LATS - 2)
    plane = jnp.where(first_band, lat - 1, LATS - 2 - lat)
    skew = lax.rem(y + 8 - z, 4)
    odd = lax.rem(skew, 2) == 1
    is_owner = jnp.logical_and(
        jnp.logical_and(plane >= 0, plane < 2), jnp.logical_or(jnp.logical_not(odd), z == 0)
    )
    block = jnp.where(odd, BLOCKS, z)
    pair = 2 * jnp.clip(plane, 0, 1) + skew // 2
    last_block = block == BLOCKS

    def owner_of(b, p):
        spot = lax.rem(b, 8) * 4 + lax.rem(b + b // 8 + 2 * (p % 2), 4)
        return jnp.where(first_band, 1 + p // 2, LATS - 2 - p // 2), spot

    main = pl.ds(HALO, ROWS)
    plane_loads = [
        pltpu.make_async_copy(src, dst, load_sem.at[k])
        for k, (src, dst) in enumerate(
            (
                (sea_in, sea),
                (diff_east_in, ext.at[LEVELS, main]),
                (flow_east_in, ext.at[LEVELS + 1, main]),
                (diff_north_in, ext.at[LEVELS + 2, main]),
                (flow_north_in, ext.at[LEVELS + 3, main]),
                (cot, ext.at[pl.ds(0, LEVELS), main]),
            )
        )
    ]
    cut_load = pltpu.make_async_copy(cutoff_in, cutoff, load_sem.at[6])
    table_loads = [
        pltpu.make_async_copy(turn_in, turn_ref, load_sem.at[7]),
        pltpu.make_async_copy(wide_in, wide_ref, load_sem.at[8]),
    ]
    for load in plane_loads:
        load.start()

    @pl.when(polar)
    def _():
        cut_load.start()

    @pl.when(is_owner)
    def _():
        for load in table_loads:
            load.start()

    barrier = pltpu.get_barrier_semaphore()

    def at(to_lat, to_lon):
        return {"lon": to_lon, "lat": to_lat}

    def hail(to_lat, to_lon):
        pl.semaphore_signal(
            barrier, inc=1, device_id=at(to_lat, to_lon), device_id_type=pl.DeviceIdType.MESH
        )

    def remote(src, dst, send, recv, to_lat, to_lon):
        return pltpu.make_async_remote_copy(
            src_ref=src, dst_ref=dst, send_sem=send, recv_sem=recv,
            device_id=at(to_lat, to_lon), device_id_type=pl.DeviceIdType.MESH,
        )

    def wait_bytes(ref, sem):
        pltpu.make_async_copy(ref, ref, sem).wait()

    def over(count, body):
        def go(k, carry):
            body(k)
            return carry

        lax.fori_loop(0, count, go, 0)

    right = lax.rem(lon + 1, TILES)
    left = lax.rem(lon + TILES - 1, TILES)

    @pl.when(polar)
    def _():
        def greet(t):
            b = lax.rem(z + 4 + t, BLOCKS)
            for p in range(PAIRS):
                hail(*owner_of(b, p))

        over(BLOCKS, greet)

    @pl.when(is_owner)
    def _():
        over(TILES, lambda t: hail(polar_lat, lax.rem(lon + TILES // 2 + t, TILES)))

    @pl.when(beside)
    def _():
        for p in range(PAIRS):
            to_lat, to_lon = owner_of(BLOCKS, p)

            @pl.when(jnp.logical_not(jnp.logical_and(to_lat == lat, to_lon == lon)))
            def _():
                hail(to_lat, to_lon)

    hail(lat, left)
    hail(lat, right)

    @pl.when(lat > 0)
    def _():
        hail(lat - 1, lon)

    @pl.when(lat < LATS - 1)
    def _():
        hail(lat + 1, lon)

    for load in plane_loads:
        load.wait()
    ext[MASK, HALO : HALO + ROWS] = sea[...].astype(F32)
    sub = iota((LEVELS, 8, LANES), 1)

    def fill(b, tile):
        rows = 8 * tile
        lam_src[b, :, 0] = ext[0:LEVELS, rows : rows + 8]
        lam_src[b, :, 1] = jnp.where(
            sub < EDGE, ext[0:LEVELS, rows + 8 : rows + 16], ext[0:LEVELS, rows - 8 : rows]
        )

    def plus_face(kappa, rows):
        return ext[MASK, rows] * (ext[LEVELS + kappa, rows] - 0.5 * ext[LEVELS + kappa + 1, rows])

    def minus_face(kappa, rows):
        return -ext[MASK, rows] * (ext[LEVELS + kappa, rows] + 0.5 * ext[LEVELS + kappa + 1, rows])

    @pl.when(polar)
    def _():
        zeros = jnp.zeros((PLANES, 8, LANES), F32)
        ext[:, 0:8] = zeros
        ext[:, EXT - 8 : EXT] = zeros

        @pl.when(lat == 0)
        def _():
            ext[:, 8:16] = zeros
            rim_e[8:16] = zeros[0]
            rim_w[8:16] = zeros[0]
            for b in range(BLOCKS - 1):
                fill(b, b + 2)

        @pl.when(lat > 0)
        def _():
            ext[:, EXT - 16 : EXT - 8] = zeros
            rim_e[EXT - 16 : EXT - 8] = zeros[0]
            rim_w[EXT - 16 : EXT - 8] = zeros[0]
            for b in range(1, BLOCKS):
                fill(b, b + 2)

        rim_src[...] = jnp.zeros((EXT, LANES), F32)
        rim_src[HALO : HALO + ROWS] = plus_face(0, slice(HALO, HALO + ROWS))

        cut_load.wait()
        row = iota((8, LANES), 0)
        open_cut = jnp.full((8, LANES), float(NLON // 2), F32)
        cuts = [open_cut, open_cut]
        for b in range(BLOCKS):
            tile = open_cut
            for j in range(8):
                tile = jnp.where(row == j, cutoff[8 * b + j].astype(F32), tile)
            cuts.append(tile)
        cuts += [open_cut, open_cut]
        for b in range(BLOCKS):
            cut_src[b, 0] = cuts[b + 2]
            cut_src[b, 1] = jnp.where(row < EDGE, cuts[b + 3], cuts[b + 1])
        cut_src[BLOCKS, 0] = open_cut
        low_half = jnp.where(first_band, open_cut, cuts[2])
        high_half = jnp.where(first_band, cuts[BLOCKS + 1], open_cut)
        cut_src[BLOCKS, 1] = jnp.where(row < EDGE, low_half, high_half)

    peers = jnp.where(polar, 3 + 9 * PAIRS, 4)
    own_beside = jnp.logical_and(last_block, plane == 0)
    from_tiles = jnp.where(own_beside, TILES - 1, TILES)
    peers = peers + jnp.where(is_owner, from_tiles, 0)
    pl.semaphore_wait(barrier, peers)

    low_rows = ext.at[:, pl.ds(HALO, 8)]
    high_rows = ext.at[:, pl.ds(HALO + ROWS - 8, 8)]
    south_rows = ext.at[:, pl.ds(HALO - 8, 8)]
    north_rows = ext.at[:, pl.ds(HALO + ROWS, 8)]
    to_south = remote(low_rows, north_rows, row_send.at[0], row_recv.at[0], lat - 1, lon)
    to_north = remote(high_rows, south_rows, row_send.at[1], row_recv.at[1], lat + 1, lon)

    @pl.when(lat > 0)
    def _():
        to_south.start()

    @pl.when(lat < LATS - 1)
    def _():
        to_north.start()

    def wait_rows():
        @pl.when(lat < LATS - 1)
        def _():
            to_south.wait_recv()

        @pl.when(lat > 0)
        def _():
            to_north.wait_recv()

    @pl.when(polar)
    def _():
        extra = pl.ds(pl.multiple_of(jnp.where(lat == 0, HALO + ROWS, HALO - 8), 8), 8)
        rims = [
            remote(ext.at[MASK, main], rim_e.at[main], col_send.at[0], col_recv.at[0], lat, left),
            remote(rim_src.at[main], rim_w.at[main], col_send.at[1], col_recv.at[1], lat, right),
            remote(ext.at[MASK, extra], rim_e.at[extra], col_send.at[2], col_recv.at[2], lat, left),
            remote(rim_src.at[extra], rim_w.at[extra], col_send.at[3], col_recv.at[3], lat, right),
        ]
        rims[0].start()
        rims[1].start()
        wait_rows()

        @pl.when(lat == 0)
        def _():
            rim_src[HALO + ROWS : HALO + ROWS + 8] = plus_face(
                0, slice(HALO + ROWS, HALO + ROWS + 8)
            )

        @pl.when(lat > 0)
        def _():
            rim_src[HALO - 8 : HALO] = plus_face(0, slice(HALO - 8, HALO))

        rims[2].start()
        rims[3].start()

        @pl.when(lat == 0)
        def _():
            fill(BLOCKS - 1, BLOCKS + 1)
            fill(BLOCKS, BLOCKS + 2)

        @pl.when(lat > 0)
        def _():
            fill(0, 2)
            fill(BLOCKS, 1)

        cut_sends = []
        for h in range(2):
            to_lat = jnp.where(first_band, 1 + h, LATS - 2 - h)
            cut_sends.append(
                remote(
                    cut_src.at[block], cuts_ref, cut_send.at[h], cut_recv.at[0], to_lat, lon
                )
            )
        owner_spot = jnp.logical_or(jnp.logical_not(odd), z == 0)

        @pl.when(owner_spot)
        def _():
            for send in cut_sends:
                send.start()

        def send_in(t):
            b = lax.rem(z + 4 + t, BLOCKS + 1)
            for p in range(PAIRS):
                remote(
                    lam_src.at[b, pl.ds(2 * p, 2)], lam.at[lon], in_send.at[0], in_recv.at[0],
                    *owner_of(b, p),
                ).start()

        over(BLOCKS + 1, send_in)

        for rim in rims:
            rim.wait_recv()
        here = slice(8, 8 + WIDE)
        lane = iota((WIDE, LANES), 1)
        mine = ext[MASK, here]
        mask_east = jnp.where(
            lane == LANES - 1, pltpu.roll(rim_e[here], LANES - 1, 1), pltpu.roll(mine, LANES - 1, 1)
        )
        plus_west = jnp.where(
            lane == 0, pltpu.roll(rim_w[here], 1, 1), pltpu.roll(rim_src[here], 1, 1)
        )
        faces = (
            minus_face(0, here) * mask_east,
            -mine * plus_west,
            minus_face(2, here) * ext[MASK, 9 : 9 + WIDE],
            -mine * plus_face(2, slice(7, 7 + WIDE)),
        )
        low = iota((8, LANES), 0) < EDGE
        for k in range(4):
            face = faces[k].reshape(WIDE // 8, 8, LANES)
            coef_src[0:BLOCKS, k, 0] = face[1:9]
            coef_src[0:BLOCKS, k, 1] = jnp.where(low[None], face[2:10], face[0:8])

            @pl.when(lat == 0)
            def _():
                coef_src[BLOCKS, k, 0] = face[9]
                coef_src[BLOCKS, k, 1] = jnp.where(low, 0.0, face[8])

            @pl.when(lat > 0)
            def _():
                coef_src[BLOCKS, k, 0] = face[0]
                coef_src[BLOCKS, k, 1] = jnp.where(low, face[1], 0.0)

        def send_coef(t):
            b = lax.rem(z + 4 + t, BLOCKS + 1)
            for p in range(PAIRS):
                remote(
                    coef_src.at[b], coef.at[lon], cf_send.at[p], cf_recv.at[0], *owner_of(b, p)
                ).start()

        over(BLOCKS + 1, send_coef)

        for rim in rims:
            rim.wait_send()

        @pl.when(owner_spot)
        def _():
            for send in cut_sends:
                send.wait_send()

        wait_bytes(lam_src, in_send.at[0])
        for p in range(PAIRS):
            wait_bytes(coef_src, cf_send.at[p])
        wait_bytes(out, out_recv.at[0])

    @pl.when(jnp.logical_not(polar))
    def _():
        wait_rows()
        here = slice(8, 8 + WIDE)
        lane = iota((WIDE, LANES), 1)
        total = jnp.zeros((WIDE, LANES), F32)
        for p in range(PLANES):
            v = ext[p, here]
            u = jnp.where(lane < EDGE, v, pltpu.roll(v, 2 * EDGE, 1))
            if p:
                u = pltpu.roll(u, 8 * p, 1)
            total = jnp.where((lane // 8) == p, u, total)
        packed[...] = total
        to_left = remote(packed, packed_r, col_send.at[0], col_recv.at[0], lat, left)
        to_right = remote(packed, packed_l, col_send.at[1], col_recv.at[1], lat, right)
        to_left.start()
        to_right.start()
        to_left.wait_recv()
        to_right.wait_recv()

        def beyond(p):
            from_right = packed_r[...]
            if p:
                from_right = pltpu.roll(from_right, LANES - 8 * p, 1)
            from_left = pltpu.roll(packed_l[...], (LANES - 8 - 8 * p) % LANES, 1)
            return jnp.where(lane < LANES // 2, from_right, from_left)

        def east_of(x):
            near, far = (pltpu.roll(v, LANES - 1, 1) for v in x)
            last = lane == LANES - 1
            return jnp.where(last, far, near), jnp.where(last, near, far)

        def west_of(x):
            near, far = (pltpu.roll(v, 1, 1) for v in x)
            last = lane == 0
            return jnp.where(last, far, near), jnp.where(last, near, far)

        def north_of(x):
            return [pltpu.roll(v, WIDE - 1, 0) for v in x]

        def south_of(x):
            return [pltpu.roll(v, 1, 0) for v in x]

        kappa_e, speed_e, kappa_n, speed_n, open_m = (
            (ext[LEVELS + k, here], beyond(LEVELS + k)) for k in range(5)
        )

        def minus(kappa, speed):
            return [m * (-k - 0.5 * f) for m, k, f in zip(open_m, kappa, speed)]

        def plus(kappa, speed):
            return [m * (k - 0.5 * f) for m, k, f in zip(open_m, kappa, speed)]

        faces = (
            [a * b for a, b in zip(minus(kappa_e, speed_e), east_of(open_m))],
            [-a * b for a, b in zip(open_m, west_of(plus(kappa_e, speed_e)))],
            [a * b for a, b in zip(minus(kappa_n, speed_n), north_of(open_m))],
            [-a * b for a, b in zip(open_m, south_of(plus(kappa_n, speed_n)))],
        )
        for k in range(4):
            for side in range(2):
                wide_coef[k, side] = faces[k][side]

        def level(p):
            from_right = pltpu.roll(packed_r[...], LANES - 8 * p, 1)
            from_left = pltpu.roll(packed_l[...], LANES - 8 - 8 * p, 1)
            x = (ext[p, here], jnp.where(lane < LANES // 2, from_right, from_left))
            for _ in range(STEPS):
                new = list(x)
                for k, near in enumerate((east_of(x), west_of(x), north_of(x), south_of(x))):
                    for side in range(2):
                        new[side] = new[side] + wide_coef[k, side] * (x[side] - near[side])
                x = tuple(new)
            mid_out[p] = x[0][8 : 8 + ROWS]

        over(LEVELS, level)

        kept = pl.ds(pl.multiple_of(jnp.where(first_band, 8, 0), 8), ROWS - 8)
        shared = pl.ds(pl.multiple_of(jnp.where(first_band, 0, ROWS - 8), 8), 8)
        store_kept = pltpu.make_async_copy(mid_out.at[:, kept], out.at[:, kept], store_sem.at[0])
        store_shared = pltpu.make_async_copy(
            mid_out.at[:, shared], out.at[:, shared], store_sem.at[1]
        )
        store_kept.start()

        @pl.when(jnp.logical_not(beside))
        def _():
            store_shared.start()

        @pl.when(is_owner)
        def _():
            for load in table_loads:
                load.wait()
            high = wide_ref[...].astype(jnp.bfloat16)
            high_ref[...] = high
            low_ref[...] = (wide_ref[...] - high.astype(F32)).astype(jnp.bfloat16)
            wait_bytes(cuts_ref, cut_recv.at[0])
            cuts = cuts_ref[...].astype(jnp.int32)
            wait_bytes(lam, in_recv.at[0])

            def step(s):
                for half in range(2):
                    real, imag = filter_circles(
                        lam[:, 0, half], lam[:, 1, half], cuts[half], high_ref, low_ref, turn_ref
                    )
                    fil[:, 0, half] = real
                    fil[:, 1, half] = imag

                @pl.when(s == 0)
                def _():
                    wait_bytes(coef, cf_recv.at[0])

                lam[...] = circle_step(fil[...], coef[...])

            over(STEPS, step)

            my_levels = pl.ds(2 * pair, 2)

            @pl.when(jnp.logical_not(last_block))
            def _():
                rows = pl.ds(pl.multiple_of(8 * jnp.minimum(block, BLOCKS - 1), 8), 8)

                def send_out(t):
                    tile = lax.rem(lon + TILES // 2 + t, TILES)
                    remote(
                        lam.at[tile, :, 0], out.at[my_levels, rows], out_send.at[0],
                        out_recv.at[0], polar_lat, tile,
                    ).start()

                over(TILES, send_out)
                wait_bytes(lam.at[:, :, 0], out_send.at[0])

            @pl.when(last_block)
            def _():
                def send_x(t):
                    tile = lax.rem(lon + 1 + t, TILES)
                    remote(
                        lam.at[tile, :, 0], row_x.at[my_levels], out_send.at[0], ox_recv.at[0],
                        beside_lat, tile,
                    ).start()

                over(TILES - 1, send_x)

                @pl.when(plane > 0)
                def _():
                    send_x(TILES - 1)
                    wait_bytes(lam.at[0, :, 0], out_send.at[0])

                @pl.when(plane == 0)
                def _():
                    pltpu.make_async_copy(
                        lam.at[lon, :, 0], row_x.at[my_levels], ox_recv.at[0]
                    ).start()

                wait_bytes(lam.at[pl.ds(0, TILES - 1), :, 0], out_send.at[0])

        to_left.wait_send()
        to_right.wait_send()

        @pl.when(beside)
        def _():
            wait_bytes(row_x, ox_recv.at[0])

            @pl.when(lat == 1)
            def _():
                mid_out[:, 0:8] = jnp.where(sub < EDGE, row_x[...], mid_out[:, 0:8])

            @pl.when(lat > 1)
            def _():
                mid_out[:, ROWS - 8 : ROWS] = jnp.where(
                    sub < EDGE, mid_out[:, ROWS - 8 : ROWS], row_x[...]
                )

            store_shared.start()

        store_kept.wait()
        store_shared.wait()

    @pl.when(lat > 0)
    def _():
        to_south.wait_send()

    @pl.when(lat < LATS - 1)
    def _():
        to_north.wait_send()


def shards(cotangent, diff_east, diff_north, flow_east, flow_north, sea_mask, cutoff):
    wide, turn = tables()
    hbm = pl.BlockSpec(memory_space=pltpu.HBM)
    dma = pltpu.SemaphoreType.DMA

    def room(*shape):
        return pltpu.VMEM(shape, F32)

    table = pltpu.VMEM((2 * LANES, 2 * LANES), jnp.bfloat16)
    return pl.pallas_call(
        kernel,
        out_shape=jax.ShapeDtypeStruct((LEVELS, ROWS, LANES), F32),
        in_specs=[hbm] * 9,
        out_specs=hbm,
        scratch_shapes=[
            pltpu.VMEM((ROWS, LANES), jnp.int32),
            pltpu.SMEM((ROWS,), jnp.int32),
            room(2 * LANES, 2 * LANES),
            table,
            table,
            room(72, 8, LANES),
            room(PLANES, EXT, LANES),
            room(BLOCKS + 1, LEVELS, 2, 8, LANES),
            room(BLOCKS + 1, 4, 2, 8, LANES),
            room(BLOCKS + 1, 2, 8, LANES),
            room(EXT, LANES),
            room(EXT, LANES),
            room(EXT, LANES),
            room(TILES, 2, 2, 8, LANES),
            room(TILES, 2, 2, 8, LANES),
            room(TILES, 4, 2, 8, LANES),
            room(2, 8, LANES),
            room(LEVELS, 8, LANES),
            room(WIDE, LANES),
            room(WIDE, LANES),
            room(WIDE, LANES),
            room(4, 2, WIDE, LANES),
            room(LEVELS, ROWS, LANES),
            dma((9,)),
            dma((2,)), dma((2,)), dma((4,)), dma((4,)), dma((2,)), dma((1,)), dma((1,)), dma((1,)),
            dma((4,)), dma((1,)), dma((1,)), dma((1,)), dma((1,)), dma((2,)),
        ],
        compiler_params=pltpu.CompilerParams(
            collective_id=0, has_side_effects=True, vmem_limit_bytes=63 * 1024 * 1024
        ),
    )(
        cotangent, diff_east, diff_north, flow_east, flow_north, sea_mask, cutoff,
        jnp.asarray(wide), jnp.asarray(turn),
    )


def solution(mesh):
    return jax.shard_map(
        shards,
        mesh=mesh,
        in_specs=(
            P(None, "lat", "lon"),
            P("lat", "lon"),
            P("lat", "lon"),
            P("lat", "lon"),
            P("lat", "lon"),
            P("lat", "lon"),
            P("lat"),
        ),
        out_specs=P(None, "lat", "lon"),
        check_vma=False,
    )
```

time: 56.1 us -> 53.1 us (0.947)
  the two profiles are of different devices: /device:TPU:1 before, /device:TPU:8 now
where the time goes in v2:
time: 53.1 us; the launch traced here: 52.9 us
  Pallas kernels  51.2 us (96%)
  local copies, waits for them, and re-layouts  1.67 us (3%)
    pallas_call x1, Pallas kernels, shards(): pl.pallas_call(kernel, out_shape=jax.ShapeDtypeStruct((LEVELS, ROWS, LANE...  51.2 us
    unnamed x1, local copies, waits for them, and re-layouts  1.67 us

profile of v2, /device:TPU:8, one launch (start us, length us, event | category | flops | bytes accessed | tf_op | source)
XLA Modules:
  0.0 52.9 jit_solution(12748879329633956797)
XLA Ops:
  0.0 51.2 %shard_map.91 = f32[8,64,128]{2,1,0:T(8,128)} custom-call(f32[8,64,128]{2,1,0:T(8,128)} %cot.1, f32[64,128]{1,0:T(8,128)} %diff_east_in.1, f32[64,128]{1,0:T(8,128)} %diff_north_in.1, f32[64,128]{1,0:T(8,128)} %flow_east_in.1, f32[64,128]{1,0:T(8,128)} %flow_north_in.1, s32[64,128]{1,0:T(8,128)} %sea_in.1, s32[64]{0:T(128)} %cutoff_in.1, ...), custom_call_target="tpu_custom_call" | custom-call | tf_op jit(solution)/shard_map/pallas_call | solution.py:696
  51.3 1.7 %copy.11 = f32[8,64,128]{2,1,0:T(8,128)} copy(f32[8,64,128]{2,1,0:T(8,128)} %shard_map.91) | data formatting | bytes 524288

commit v3 on v2

--- a/solution.py
+++ b/solution.py
@@ -24,6 +24,9 @@
 MASK = LEVELS + 4
 EDGE = 4
 LATS = 8
+COLS = 4
+RINGS = 8
+LAST_RING = 4
 
 F32 = jnp.float32
 
@@ -160,7 +163,8 @@
     down = across(pltpu.roll(flat, 1, 1), 0)
     total = x
     for k, near in enumerate((east.reshape(full), west.reshape(full), up, down)):
-        total = total + coef[:, k : k + 1] * (x - near)
+        face = jnp.stack([coef[c, :, k] for c in range(COLS)], axis=1).reshape(TILES, 1, 2, 8, LANES)
+        total = total + face * (x - near)
     return total
 
 
@@ -172,7 +176,7 @@
     ext, lam_src, coef_src, cut_src, rim_e, rim_w, rim_src,
     lam, fil, coef, cuts_ref, row_x, packed, packed_l, packed_r, wide_coef, mid_out,
     load_sem, row_send, row_recv, col_send, col_recv, cut_send, cut_recv, in_send, in_recv,
-    cf_send, cf_recv, out_send, out_recv, ox_recv, store_sem,
+    cf_send, cf_recv, pass_send, pass_recv, out_send, out_recv, ox_recv, store_sem,
 ):
     lon = lax.axis_index("lon")
     lat = lax.axis_index("lat")
@@ -183,19 +187,15 @@
     beside = jnp.logical_or(lat == 1, lat == LATS - 2)
     polar_lat = jnp.where(first_band, 0, LATS - 1)
     beside_lat = jnp.where(first_band, 1, LATS - 2)
-    plane = jnp.where(first_band, lat - 1, LATS - 2 - lat)
-    skew = lax.rem(y + 8 - z, 4)
-    odd = lax.rem(skew, 2) == 1
-    is_owner = jnp.logical_and(
-        jnp.logical_and(plane >= 0, plane < 2), jnp.logical_or(jnp.logical_not(odd), z == 0)
-    )
-    block = jnp.where(odd, BLOCKS, z)
-    pair = 2 * jnp.clip(plane, 0, 1) + skew // 2
-    last_block = block == BLOCKS
+    last_lat = jnp.where(first_band, 2, LATS - 3)
+    last_block = jnp.logical_and(lat == last_lat, z == LAST_RING)
+    is_owner = jnp.logical_or(beside, last_block)
+    block = jnp.where(beside, z, BLOCKS)
+    pair = y
 
     def owner_of(b, p):
-        spot = lax.rem(b, 8) * 4 + lax.rem(b + b // 8 + 2 * (p % 2), 4)
-        return jnp.where(first_band, 1 + p // 2, LATS - 2 - p // 2), spot
+        to_lat = jnp.where(b == BLOCKS, last_lat, beside_lat)
+        return to_lat, COLS * jnp.where(b == BLOCKS, LAST_RING, b) + p
 
     main = pl.ds(HALO, ROWS)
     plane_loads = [
@@ -269,15 +269,13 @@
     @pl.when(is_owner)
     def _():
         over(TILES, lambda t: hail(polar_lat, lax.rem(lon + TILES // 2 + t, TILES)))
+        for c in range(1, COLS):
+            hail(lat, COLS * z + lax.rem(y + c, COLS))
 
     @pl.when(beside)
     def _():
         for p in range(PAIRS):
-            to_lat, to_lon = owner_of(BLOCKS, p)
-
-            @pl.when(jnp.logical_not(jnp.logical_and(to_lat == lat, to_lon == lon)))
-            def _():
-                hail(to_lat, to_lon)
+            hail(*owner_of(BLOCKS, p))
 
     hail(lat, left)
     hail(lat, right)
@@ -352,9 +350,7 @@
         cut_src[BLOCKS, 1] = jnp.where(row < EDGE, low_half, high_half)
 
     peers = jnp.where(polar, 3 + 9 * PAIRS, 4)
-    own_beside = jnp.logical_and(last_block, plane == 0)
-    from_tiles = jnp.where(own_beside, TILES - 1, TILES)
-    peers = peers + jnp.where(is_owner, from_tiles, 0)
+    peers = peers + jnp.where(is_owner, TILES + COLS - 1, 0)
     pl.semaphore_wait(barrier, peers)
 
     low_rows = ext.at[:, pl.ds(HALO, 8)]
@@ -392,55 +388,57 @@
         ]
         rims[0].start()
         rims[1].start()
-        wait_rows()
-
-        @pl.when(lat == 0)
-        def _():
-            rim_src[HALO + ROWS : HALO + ROWS + 8] = plus_face(
-                0, slice(HALO + ROWS, HALO + ROWS + 8)
-            )
-
-        @pl.when(lat > 0)
-        def _():
-            rim_src[HALO - 8 : HALO] = plus_face(0, slice(HALO - 8, HALO))
-
-        rims[2].start()
-        rims[3].start()
-
-        @pl.when(lat == 0)
-        def _():
-            fill(BLOCKS - 1, BLOCKS + 1)
-            fill(BLOCKS, BLOCKS + 2)
-
-        @pl.when(lat > 0)
-        def _():
-            fill(0, 2)
-            fill(BLOCKS, 1)
-
-        cut_sends = []
-        for h in range(2):
-            to_lat = jnp.where(first_band, 1 + h, LATS - 2 - h)
-            cut_sends.append(
-                remote(
-                    cut_src.at[block], cuts_ref, cut_send.at[h], cut_recv.at[0], to_lat, lon
-                )
-            )
-        owner_spot = jnp.logical_or(jnp.logical_not(odd), z == 0)
-
-        @pl.when(owner_spot)
-        def _():
-            for send in cut_sends:
-                send.start()
-
-        def send_in(t):
-            b = lax.rem(z + 4 + t, BLOCKS + 1)
+        pltpu.make_async_remote_copy(
+            src_ref=cut_src.at[z], dst_ref=cuts_ref, send_sem=cut_send.at[0],
+            recv_sem=cut_recv.at[0], device_id=at(beside_lat, lon),
+            device_id_type=pl.DeviceIdType.MESH,
+        ).start()
+
+        @pl.when(z == LAST_RING)
+        def _():
+            remote(
+                cut_src.at[BLOCKS], cuts_ref, cut_send.at[1], cut_recv.at[0], last_lat, lon
+            ).start()
+
+        def send_block(b):
             for p in range(PAIRS):
                 remote(
                     lam_src.at[b, pl.ds(2 * p, 2)], lam.at[lon], in_send.at[0], in_recv.at[0],
                     *owner_of(b, p),
                 ).start()
 
-        over(BLOCKS + 1, send_in)
+        def send_free(t):
+            send_block(lax.rem(z + 4 + t, BLOCKS - 1) + jnp.where(lat == 0, 0, 1))
+
+        def send_some(first, count):
+            over(count, lambda t: send_free(first + t))
+
+        send_some(0, 2)
+        wait_rows()
+
+        @pl.when(lat == 0)
+        def _():
+            rim_src[HALO + ROWS : HALO + ROWS + 8] = plus_face(
+                0, slice(HALO + ROWS, HALO + ROWS + 8)
+            )
+
+        @pl.when(lat > 0)
+        def _():
+            rim_src[HALO - 8 : HALO] = plus_face(0, slice(HALO - 8, HALO))
+
+        rims[2].start()
+        rims[3].start()
+        send_some(2, 2)
+
+        @pl.when(lat == 0)
+        def _():
+            fill(BLOCKS - 1, BLOCKS + 1)
+            fill(BLOCKS, BLOCKS + 2)
+
+        @pl.when(lat > 0)
+        def _():
+            fill(0, 2)
+            fill(BLOCKS, 1)
 
         for rim in rims:
             rim.wait_recv()
@@ -477,24 +475,25 @@
 
         def send_coef(t):
             b = lax.rem(z + 4 + t, BLOCKS + 1)
-            for p in range(PAIRS):
-                remote(
-                    coef_src.at[b], coef.at[lon], cf_send.at[p], cf_recv.at[0], *owner_of(b, p)
-                ).start()
+            remote(
+                coef_src.at[b], coef.at[y, z], cf_send.at[0], cf_recv.at[z], *owner_of(b, y)
+            ).start()
 
         over(BLOCKS + 1, send_coef)
+        send_some(4, BLOCKS - 5)
+        send_block(jnp.where(lat == 0, BLOCKS - 1, 0))
+        send_block(jnp.int32(BLOCKS))
 
         for rim in rims:
             rim.wait_send()
-
-        @pl.when(owner_spot)
-        def _():
-            for send in cut_sends:
-                send.wait_send()
+        wait_bytes(cuts_ref, cut_send.at[0])
+
+        @pl.when(z == LAST_RING)
+        def _():
+            wait_bytes(cuts_ref, cut_send.at[1])
 
         wait_bytes(lam_src, in_send.at[0])
-        for p in range(PAIRS):
-            wait_bytes(coef_src, cf_send.at[p])
+        wait_bytes(coef_src, cf_send.at[0])
         wait_bytes(out, out_recv.at[0])
 
     @pl.when(jnp.logical_not(polar))
@@ -514,6 +513,19 @@
         to_right = remote(packed, packed_l, col_send.at[1], col_recv.at[1], lat, right)
         to_left.start()
         to_right.start()
+        @pl.when(is_owner)
+        def _():
+            def hand_on(t):
+                ring = lax.rem(z + t, RINGS)
+                wait_bytes(coef.at[y, ring], cf_recv.at[ring])
+                for c in range(1, COLS):
+                    remote(
+                        coef.at[y, ring], coef.at[y, ring], pass_send.at[0], pass_recv.at[0],
+                        lat, COLS * z + lax.rem(y + c, COLS),
+                    ).start()
+
+            over(RINGS, hand_on)
+
         to_left.wait_recv()
         to_right.wait_recv()
 
@@ -607,9 +619,9 @@
 
                 @pl.when(s == 0)
                 def _():
-                    wait_bytes(coef, cf_recv.at[0])
-
-                lam[...] = circle_step(fil[...], coef[...])
+                    wait_bytes(coef.at[pl.ds(0, COLS - 1)], pass_recv.at[0])
+
+                lam[...] = circle_step(fil[...], coef)
 
             over(STEPS, step)
 
@@ -627,31 +639,20 @@
                     ).start()
 
                 over(TILES, send_out)
-                wait_bytes(lam.at[:, :, 0], out_send.at[0])
 
             @pl.when(last_block)
             def _():
                 def send_x(t):
-                    tile = lax.rem(lon + 1 + t, TILES)
+                    tile = lax.rem(lon + TILES // 2 + t, TILES)
                     remote(
                         lam.at[tile, :, 0], row_x.at[my_levels], out_send.at[0], ox_recv.at[0],
                         beside_lat, tile,
                     ).start()
 
-                over(TILES - 1, send_x)
-
-                @pl.when(plane > 0)
-                def _():
-                    send_x(TILES - 1)
-                    wait_bytes(lam.at[0, :, 0], out_send.at[0])
-
-                @pl.when(plane == 0)
-                def _():
-                    pltpu.make_async_copy(
-                        lam.at[lon, :, 0], row_x.at[my_levels], ox_recv.at[0]
-                    ).start()
-
-                wait_bytes(lam.at[pl.ds(0, TILES - 1), :, 0], out_send.at[0])
+                over(TILES, send_x)
+
+            wait_bytes(coef.at[pl.ds(0, COLS - 1)], pass_send.at[0])
+            wait_bytes(lam.at[:, :, 0], out_send.at[0])
 
         to_left.wait_send()
         to_right.wait_send()
@@ -714,7 +715,7 @@
             room(EXT, LANES),
             room(TILES, 2, 2, 8, LANES),
             room(TILES, 2, 2, 8, LANES),
-            room(TILES, 4, 2, 8, LANES),
+            room(COLS, RINGS, 4, 2, 8, LANES),
             room(2, 8, LANES),
             room(LEVELS, 8, LANES),
             room(WIDE, LANES),
@@ -724,7 +725,7 @@
             room(LEVELS, ROWS, LANES),
             dma((9,)),
             dma((2,)), dma((2,)), dma((4,)), dma((4,)), dma((2,)), dma((1,)), dma((1,)), dma((1,)),
-            dma((4,)), dma((1,)), dma((1,)), dma((1,)), dma((1,)), dma((2,)),
+            dma((1,)), dma((RINGS,)), dma((1,)), dma((1,)), dma((1,)), dma((1,)), dma((1,)), dma((2,)),
         ],
         compiler_params=pltpu.CompilerParams(
             collective_id=0, has_side_effects=True, vmem_limit_bytes=63 * 1024 * 1024

time: 53.1 us -> 50.1 us (0.944)
  the two profiles are of different devices: /device:TPU:8 before, /device:TPU:1 now
where the time goes in v3:
time: 50.1 us; the launch traced here: 50 us
  Pallas kernels  48.3 us (96%)
  local copies, waits for them, and re-layouts  1.67 us (3%)
    pallas_call x1, Pallas kernels, shards(): pl.pallas_call(kernel, out_shape=jax.ShapeDtypeStruct((LEVELS, ROWS, LANE...  48.3 us
    unnamed x1, local copies, waits for them, and re-layouts  1.67 us

profile of v3, /device:TPU:1, one launch (start us, length us, event | category | flops | bytes accessed | tf_op | source)
XLA Modules:
  0.0 50.0 jit_solution(2097289122629738917)
XLA Ops:
  0.0 48.3 %shard_map.91 = f32[8,64,128]{2,1,0:T(8,128)} custom-call(f32[8,64,128]{2,1,0:T(8,128)} %cot.1, f32[64,128]{1,0:T(8,128)} %diff_east_in.1, f32[64,128]{1,0:T(8,128)} %diff_north_in.1, f32[64,128]{1,0:T(8,128)} %flow_east_in.1, f32[64,128]{1,0:T(8,128)} %flow_north_in.1, s32[64,128]{1,0:T(8,128)} %sea_in.1, s32[64]{0:T(128)} %cutoff_in.1, ...), custom_call_target="tpu_custom_call" | custom-call | tf_op jit(solution)/shard_map/pallas_call | solution.py:697
  48.3 1.7 %copy.11 = f32[8,64,128]{2,1,0:T(8,128)} copy(f32[8,64,128]{2,1,0:T(8,128)} %shard_map.91) | data formatting | bytes 524288

commit v4 on v3

--- a/solution.py
+++ b/solution.py
@@ -27,6 +27,7 @@
 COLS = 4
 RINGS = 8
 LAST_RING = 4
+EARLY = 3
 
 F32 = jnp.float32
 
@@ -171,10 +172,10 @@
 def kernel(
     cot, diff_east_in, diff_north_in, flow_east_in, flow_north_in, sea_in, cutoff_in, wide_in,
     turn_in,
-    out,
+    out, row_x,
     sea, cutoff, wide_ref, high_ref, low_ref, turn_ref,
     ext, lam_src, coef_src, cut_src, rim_e, rim_w, rim_src,
-    lam, fil, coef, cuts_ref, row_x, packed, packed_l, packed_r, wide_coef, mid_out,
+    lam, fil, coef, cuts_ref, packed, packed_l, packed_r, wide_coef, mid_out,
     load_sem, row_send, row_recv, col_send, col_recv, cut_send, cut_recv, in_send, in_recv,
     cf_send, cf_recv, pass_send, pass_recv, out_send, out_recv, ox_recv, store_sem,
 ):
@@ -254,13 +255,16 @@
 
         lax.fori_loop(0, count, go, 0)
 
+    def far_first(i):
+        return lax.rem(z + 4 + ((i + 1) // 2) * (1 - 2 * lax.rem(i, 2)), RINGS)
+
     right = lax.rem(lon + 1, TILES)
     left = lax.rem(lon + TILES - 1, TILES)
 
     @pl.when(polar)
     def _():
-        def greet(t):
-            b = lax.rem(z + 4 + t, BLOCKS)
+        def greet(i):
+            b = far_first(i)
             for p in range(PAIRS):
                 hail(*owner_of(b, p))
 
@@ -268,7 +272,11 @@
 
     @pl.when(is_owner)
     def _():
-        over(TILES, lambda t: hail(polar_lat, lax.rem(lon + TILES // 2 + t, TILES)))
+        def greet(i):
+            for c in range(COLS):
+                hail(polar_lat, COLS * far_first(i) + lax.rem(y + c, COLS))
+
+        over(RINGS, greet)
         for c in range(1, COLS):
             hail(lat, COLS * z + lax.rem(y + c, COLS))
 
@@ -407,13 +415,19 @@
                     *owner_of(b, p),
                 ).start()
 
-        def send_free(t):
-            send_block(lax.rem(z + 4 + t, BLOCKS - 1) + jnp.where(lat == 0, 0, 1))
-
-        def send_some(first, count):
-            over(count, lambda t: send_free(first + t))
-
-        send_some(0, 2)
+        edge = jnp.where(lat == 0, BLOCKS - 1, 0)
+
+        def send_early(i):
+            @pl.when(far_first(i) != edge)
+            def _():
+                send_block(far_first(i))
+
+        def send_skipped(i):
+            @pl.when(far_first(i) == edge)
+            def _():
+                send_block(edge)
+
+        over(EARLY, send_early)
         wait_rows()
 
         @pl.when(lat == 0)
@@ -428,7 +442,6 @@
 
         rims[2].start()
         rims[3].start()
-        send_some(2, 2)
 
         @pl.when(lat == 0)
         def _():
@@ -440,6 +453,9 @@
             fill(0, 2)
             fill(BLOCKS, 1)
 
+        over(EARLY, send_skipped)
+        send_block(jnp.int32(BLOCKS))
+        over(2, lambda i: send_block(far_first(EARLY + i)))
         for rim in rims:
             rim.wait_recv()
         here = slice(8, 8 + WIDE)
@@ -473,16 +489,14 @@
                 coef_src[BLOCKS, k, 0] = face[0]
                 coef_src[BLOCKS, k, 1] = jnp.where(low, face[1], 0.0)
 
-        def send_coef(t):
-            b = lax.rem(z + 4 + t, BLOCKS + 1)
+        def send_coef(b):
             remote(
                 coef_src.at[b], coef.at[y, z], cf_send.at[0], cf_recv.at[z], *owner_of(b, y)
             ).start()
 
-        over(BLOCKS + 1, send_coef)
-        send_some(4, BLOCKS - 5)
-        send_block(jnp.where(lat == 0, BLOCKS - 1, 0))
-        send_block(jnp.int32(BLOCKS))
+        send_coef(jnp.int32(BLOCKS))
+        over(RINGS, lambda i: send_coef(far_first(i)))
+        over(RINGS - EARLY - 2, lambda i: send_block(far_first(EARLY + 2 + i)))
 
         for rim in rims:
             rim.wait_send()
@@ -515,6 +529,12 @@
         to_right.start()
         @pl.when(is_owner)
         def _():
+            for load in table_loads:
+                load.wait()
+            high = wide_ref[...].astype(jnp.bfloat16)
+            high_ref[...] = high
+            low_ref[...] = (wide_ref[...] - high.astype(F32)).astype(jnp.bfloat16)
+
             def hand_on(t):
                 ring = lax.rem(z + t, RINGS)
                 wait_bytes(coef.at[y, ring], cf_recv.at[ring])
@@ -525,6 +545,53 @@
                     ).start()
 
             over(RINGS, hand_on)
+            wait_bytes(cuts_ref, cut_recv.at[0])
+            cuts = cuts_ref[...].astype(jnp.int32)
+            wait_bytes(lam, in_recv.at[0])
+
+            def step(s):
+                for half in range(2):
+                    real, imag = filter_circles(
+                        lam[:, 0, half], lam[:, 1, half], cuts[half], high_ref, low_ref, turn_ref
+                    )
+                    fil[:, 0, half] = real
+                    fil[:, 1, half] = imag
+
+                @pl.when(s == 0)
+                def _():
+                    wait_bytes(coef.at[pl.ds(0, COLS - 1)], pass_recv.at[0])
+
+                lam[...] = circle_step(fil[...], coef)
+
+            over(STEPS, step)
+
+            my_levels = pl.ds(2 * pair, 2)
+
+            @pl.when(jnp.logical_not(last_block))
+            def _():
+                rows = pl.ds(pl.multiple_of(8 * jnp.minimum(block, BLOCKS - 1), 8), 8)
+
+                def send_out(i):
+                    for c in range(COLS):
+                        tile = COLS * far_first(i) + lax.rem(y + c, COLS)
+                        remote(
+                            lam.at[tile, :, 0], out.at[my_levels, rows], out_send.at[0],
+                            out_recv.at[0], polar_lat, tile,
+                        ).start()
+
+                over(RINGS, send_out)
+
+            @pl.when(last_block)
+            def _():
+                def send_x(i):
+                    for c in range(COLS):
+                        tile = COLS * far_first(i) + lax.rem(y + c, COLS)
+                        remote(
+                            lam.at[tile, :, 0], row_x.at[my_levels], out_send.at[0], ox_recv.at[0],
+                            beside_lat, tile,
+                        ).start()
+
+                over(RINGS, send_x)
 
         to_left.wait_recv()
         to_right.wait_recv()
@@ -586,71 +653,11 @@
 
         over(LEVELS, level)
 
-        kept = pl.ds(pl.multiple_of(jnp.where(first_band, 8, 0), 8), ROWS - 8)
-        shared = pl.ds(pl.multiple_of(jnp.where(first_band, 0, ROWS - 8), 8), 8)
-        store_kept = pltpu.make_async_copy(mid_out.at[:, kept], out.at[:, kept], store_sem.at[0])
-        store_shared = pltpu.make_async_copy(
-            mid_out.at[:, shared], out.at[:, shared], store_sem.at[1]
-        )
-        store_kept.start()
-
-        @pl.when(jnp.logical_not(beside))
-        def _():
-            store_shared.start()
+        store = pltpu.make_async_copy(mid_out, out, store_sem.at[0])
+        store.start()
 
         @pl.when(is_owner)
         def _():
-            for load in table_loads:
-                load.wait()
-            high = wide_ref[...].astype(jnp.bfloat16)
-            high_ref[...] = high
-            low_ref[...] = (wide_ref[...] - high.astype(F32)).astype(jnp.bfloat16)
-            wait_bytes(cuts_ref, cut_recv.at[0])
-            cuts = cuts_ref[...].astype(jnp.int32)
-            wait_bytes(lam, in_recv.at[0])
-
-            def step(s):
-                for half in range(2):
-                    real, imag = filter_circles(
-                        lam[:, 0, half], lam[:, 1, half], cuts[half], high_ref, low_ref, turn_ref
-                    )
-                    fil[:, 0, half] = real
-                    fil[:, 1, half] = imag
-
-                @pl.when(s == 0)
-                def _():
-                    wait_bytes(coef.at[pl.ds(0, COLS - 1)], pass_recv.at[0])
-
-                lam[...] = circle_step(fil[...], coef)
-
-            over(STEPS, step)
-
-            my_levels = pl.ds(2 * pair, 2)
-
-            @pl.when(jnp.logical_not(last_block))
-            def _():
-                rows = pl.ds(pl.multiple_of(8 * jnp.minimum(block, BLOCKS - 1), 8), 8)
-
-                def send_out(t):
-                    tile = lax.rem(lon + TILES // 2 + t, TILES)
-                    remote(
-                        lam.at[tile, :, 0], out.at[my_levels, rows], out_send.at[0],
-                        out_recv.at[0], polar_lat, tile,
-                    ).start()
-
-                over(TILES, send_out)
-
-            @pl.when(last_block)
-            def _():
-                def send_x(t):
-                    tile = lax.rem(lon + TILES // 2 + t, TILES)
-                    remote(
-                        lam.at[tile, :, 0], row_x.at[my_levels], out_send.at[0], ox_recv.at[0],
-                        beside_lat, tile,
-                    ).start()
-
-                over(TILES, send_x)
-
             wait_bytes(coef.at[pl.ds(0, COLS - 1)], pass_send.at[0])
             wait_bytes(lam.at[:, :, 0], out_send.at[0])
 
@@ -661,20 +668,7 @@
         def _():
             wait_bytes(row_x, ox_recv.at[0])
 
-            @pl.when(lat == 1)
-            def _():
-                mid_out[:, 0:8] = jnp.where(sub < EDGE, row_x[...], mid_out[:, 0:8])
-
-            @pl.when(lat > 1)
-            def _():
-                mid_out[:, ROWS - 8 : ROWS] = jnp.where(
-                    sub < EDGE, mid_out[:, ROWS - 8 : ROWS], row_x[...]
-                )
-
-            store_shared.start()
-
-        store_kept.wait()
-        store_shared.wait()
+        store.wait()
 
     @pl.when(lat > 0)
     def _():
@@ -694,11 +688,14 @@
         return pltpu.VMEM(shape, F32)
 
     table = pltpu.VMEM((2 * LANES, 2 * LANES), jnp.bfloat16)
-    return pl.pallas_call(
+    field, shared = pl.pallas_call(
         kernel,
-        out_shape=jax.ShapeDtypeStruct((LEVELS, ROWS, LANES), F32),
+        out_shape=[
+            jax.ShapeDtypeStruct((LEVELS, ROWS, LANES), F32),
+            jax.ShapeDtypeStruct((LEVELS, 8, LANES), F32),
+        ],
         in_specs=[hbm] * 9,
-        out_specs=hbm,
+        out_specs=[hbm, hbm],
         scratch_shapes=[
             pltpu.VMEM((ROWS, LANES), jnp.int32),
             pltpu.SMEM((ROWS,), jnp.int32),
@@ -717,7 +714,6 @@
             room(TILES, 2, 2, 8, LANES),
             room(COLS, RINGS, 4, 2, 8, LANES),
             room(2, 8, LANES),
-            room(LEVELS, 8, LANES),
             room(WIDE, LANES),
             room(WIDE, LANES),
             room(WIDE, LANES),
@@ -725,7 +721,7 @@
             room(LEVELS, ROWS, LANES),
             dma((9,)),
             dma((2,)), dma((2,)), dma((4,)), dma((4,)), dma((2,)), dma((1,)), dma((1,)), dma((1,)),
-            dma((1,)), dma((RINGS,)), dma((1,)), dma((1,)), dma((1,)), dma((1,)), dma((1,)), dma((2,)),
+            dma((1,)), dma((RINGS,)), dma((1,)), dma((1,)), dma((1,)), dma((1,)), dma((1,)), dma((1,)),
         ],
         compiler_params=pltpu.CompilerParams(
             collective_id=0, has_side_effects=True, vmem_limit_bytes=63 * 1024 * 1024
@@ -734,6 +730,12 @@
         cotangent, diff_east, diff_north, flow_east, flow_north, sea_mask, cutoff,
         jnp.asarray(wide), jnp.asarray(turn),
     )
+    lat = lax.axis_index("lat")
+    row = lax.broadcasted_iota(jnp.int32, field.shape, 1)
+    taken = jnp.logical_or(
+        jnp.logical_and(lat == 1, row < EDGE), jnp.logical_and(lat == LATS - 2, row >= ROWS - EDGE)
+    )
+    return jnp.where(taken, jnp.tile(shared, (1, ROWS // 8, 1)), field)
 
 
 def solution(mesh):

time: 50.1 us -> 47 us (0.938)
  Pallas kernels: 48.3 us -> 45.2 us
  other arithmetic: 0 us -> 1.75 us
  local copies, waits for them, and re-layouts: 1.67 us -> 0 us
    pallas_call x1, Pallas kernels: 48.3 us -> 45.2 us  [shards(): pl.pallas_call(kernel, out_shape=[jax.ShapeDtypeStruct((LEVELS, ROWS, LAN...]
    select_n x0 -> x1, other arithmetic: none -> 1.74 us  [shards(): return jnp.where(taken, jnp.tile(shared, (1, ROWS // 8, 1)), field)]
    unnamed x1 -> x0, local copies, waits for them, and re-layouts: 1.67 us -> none
where the time goes in v4:
time: 47 us; the launch traced here: 46.9 us
  Pallas kernels  45.2 us (96%)
  other arithmetic  1.75 us (4%)
    pallas_call x1, Pallas kernels, shards(): pl.pallas_call(kernel, out_shape=[jax.ShapeDtypeStruct((LEVELS, ROWS, LAN...  45.2 us
    select_n x1, other arithmetic, shards(): return jnp.where(taken, jnp.tile(shared, (1, ROWS // 8, 1)), field)  1.74 us

profile of v4, /device:TPU:1, one launch (start us, length us, event | category | flops | bytes accessed | tf_op | source)
XLA Modules:
  0.0 46.9 jit_solution(2617441267460786599)
XLA Ops:
  0.0 45.2 %shard_map.91 = (f32[8,64,128]{2,1,0:T(8,128)}, f32[8,8,128]{2,1,0:T(8,128)}) custom-call(f32[8,64,128]{2,1,0:T(8,128)} %cot.1, f32[64,128]{1,0:T(8,128)} %diff_east_in.1, f32[64,128]{1,0:T(8,128)} %diff_north_in.1, f32[64,128]{1,0:T(8,128)} %flow_east_in.1, f32[64,128]{1,0:T(8,128)} %flow_north_in.1, s32[64,128]{1,0:T(8,128)} %sea_in.1, s32[64]{0:T(128)} %cutoff_in.1, ...), custom_call_target="tpu_custom_call" | custom-call | tf_op jit(solution)/shard_map/pallas_call | solution.py:691
  45.2 1.7 %bitcast_select_fusion = f32[8,64,128]{2,1,0:T(8,128)} fusion(f32[8,64,128]{2,1,0:T(8,128)} %get-tuple-element.8, f32[8,8,128]{2,1,0:T(8,128)} %get-tuple-element.7, pred[64]{0:T(512)(128)(4,1)S(1)} %and_or_fusion), kind=kLoop, calls=%fused_computation | loop fusion | flops 65536 | bytes 557120 | tf_op jit(solution)/shard_map/jit(_where)/select_n | solution.py:738
  (1 shorter events, 0.0 us)

commit v5 on v4

--- a/solution.py
+++ b/solution.py
@@ -27,7 +27,6 @@
 COLS = 4
 RINGS = 8
 LAST_RING = 4
-EARLY = 3
 
 F32 = jnp.float32
 
@@ -101,7 +100,7 @@
     return dot(high, high_ref[...]) + (dot(low, high_ref[...]) + dot(high, low_ref[...]))
 
 
-def filter_circles(real, imag, cuts, high_ref, low_ref, turn_ref):
+def filter_circles(real, imag, kept, high_ref, low_ref, turn_ref):
     shape = (8, 4, 8, LANES)
     cos1 = turn_ref[0:32].reshape(shape)
     sin1 = turn_ref[32:64].reshape(shape)
@@ -117,11 +116,6 @@
     real = jnp.concatenate([p[0] for p in parts]).reshape(256, LANES)
     imag = jnp.concatenate([p[1] for p in parts]).reshape(256, LANES)
     spec = split_dot(jnp.concatenate([real, imag], axis=1), high_ref, low_ref)
-    wave = lax.broadcasted_iota(jnp.int32, (TILES, 8, LANES), 0) + TILES * lax.broadcasted_iota(
-        jnp.int32, (TILES, 8, LANES), 2
-    )
-    wave = jnp.minimum(wave, NLON - wave)
-    kept = jnp.where(wave <= cuts[None], 1.0 / NLON, 0.0).astype(F32).reshape(256, LANES)
     real = spec[:, :LANES] * kept
     imag = spec[:, LANES:] * kept
     back = split_dot(jnp.concatenate([imag, real], axis=1), high_ref, low_ref)
@@ -164,9 +158,17 @@
     down = across(pltpu.roll(flat, 1, 1), 0)
     total = x
     for k, near in enumerate((east.reshape(full), west.reshape(full), up, down)):
-        face = jnp.stack([coef[c, :, k] for c in range(COLS)], axis=1).reshape(TILES, 1, 2, 8, LANES)
-        total = total + face * (x - near)
+        total = total + coef[:, k : k + 1] * (x - near)
     return total
+
+
+def neighbour(x, step):
+    shape = (TILES * 2, 8, LANES)
+    lane = iota(shape, 2)
+    turned = pltpu.roll(x.reshape(shape), step % LANES, 2)
+    moved = jnp.concatenate([turned[-2 * step :], turned[: -2 * step]])
+    edge = 0 if step > 0 else LANES - 1
+    return jnp.where(lane == edge, moved, turned).reshape(x.shape)
 
 
 def kernel(
@@ -174,8 +176,8 @@
     turn_in,
     out, row_x,
     sea, cutoff, wide_ref, high_ref, low_ref, turn_ref,
-    ext, lam_src, coef_src, cut_src, rim_e, rim_w, rim_src,
-    lam, fil, coef, cuts_ref, packed, packed_l, packed_r, wide_coef, mid_out,
+    ext, lam_src, coef_src, cut_src,
+    lam, fil, coef, faces, kept_ref, cuts_ref, packed, packed_l, packed_r, wide_coef, mid_out,
     load_sem, row_send, row_recv, col_send, col_recv, cut_send, cut_recv, in_send, in_recv,
     cf_send, cf_recv, pass_send, pass_recv, out_send, out_recv, ox_recv, store_sem,
 ):
@@ -285,8 +287,10 @@
         for p in range(PAIRS):
             hail(*owner_of(BLOCKS, p))
 
-    hail(lat, left)
-    hail(lat, right)
+    @pl.when(jnp.logical_not(polar))
+    def _():
+        hail(lat, left)
+        hail(lat, right)
 
     @pl.when(lat > 0)
     def _():
@@ -308,11 +312,24 @@
             sub < EDGE, ext[0:LEVELS, rows + 8 : rows + 16], ext[0:LEVELS, rows - 8 : rows]
         )
 
-    def plus_face(kappa, rows):
-        return ext[MASK, rows] * (ext[LEVELS + kappa, rows] - 0.5 * ext[LEVELS + kappa + 1, rows])
-
-    def minus_face(kappa, rows):
-        return -ext[MASK, rows] * (ext[LEVELS + kappa, rows] + 0.5 * ext[LEVELS + kappa + 1, rows])
+    def face_tiles(start, count):
+        rows = pl.ds(pl.multiple_of(start, 8), 8 * count)
+        mine = ext[MASK, rows]
+        kappa_e, speed_e, kappa_n, speed_n = (ext[LEVELS + k, rows] for k in range(4))
+        minus_n = mine * (-kappa_n - 0.5 * speed_n)
+        plus_n = mine * (kappa_n - 0.5 * speed_n)
+        planes = (
+            mine * (-kappa_e - 0.5 * speed_e),
+            mine * (kappa_e - 0.5 * speed_e),
+            minus_n * pltpu.roll(mine, 8 * count - 1, 0),
+            -mine * pltpu.roll(plus_n, 1, 0),
+            mine,
+        )
+        return [plane.reshape(count, 8, LANES) for plane in planes]
+
+    low = iota((1, 8, LANES), 1) < EDGE
+    free = jnp.where(first_band, 0, 1)
+    edge = jnp.where(first_band, BLOCKS - 1, 0)
 
     @pl.when(polar)
     def _():
@@ -323,21 +340,18 @@
         @pl.when(lat == 0)
         def _():
             ext[:, 8:16] = zeros
-            rim_e[8:16] = zeros[0]
-            rim_w[8:16] = zeros[0]
             for b in range(BLOCKS - 1):
                 fill(b, b + 2)
 
         @pl.when(lat > 0)
         def _():
             ext[:, EXT - 16 : EXT - 8] = zeros
-            rim_e[EXT - 16 : EXT - 8] = zeros[0]
-            rim_w[EXT - 16 : EXT - 8] = zeros[0]
             for b in range(1, BLOCKS):
                 fill(b, b + 2)
 
-        rim_src[...] = jnp.zeros((EXT, LANES), F32)
-        rim_src[HALO : HALO + ROWS] = plus_face(0, slice(HALO, HALO + ROWS))
+        for k, face in enumerate(face_tiles(jnp.where(first_band, 8, 16), BLOCKS + 1)):
+            coef_src[pl.ds(free, BLOCKS - 1), k, 0] = face[1:8]
+            coef_src[pl.ds(free, BLOCKS - 1), k, 1] = jnp.where(low, face[2:9], face[0:7])
 
         cut_load.wait()
         row = iota((8, LANES), 0)
@@ -357,7 +371,7 @@
         high_half = jnp.where(first_band, cuts[BLOCKS + 1], open_cut)
         cut_src[BLOCKS, 1] = jnp.where(row < EDGE, low_half, high_half)
 
-    peers = jnp.where(polar, 3 + 9 * PAIRS, 4)
+    peers = jnp.where(polar, 1 + 9 * PAIRS, 4)
     peers = peers + jnp.where(is_owner, TILES + COLS - 1, 0)
     pl.semaphore_wait(barrier, peers)
 
@@ -387,15 +401,6 @@
 
     @pl.when(polar)
     def _():
-        extra = pl.ds(pl.multiple_of(jnp.where(lat == 0, HALO + ROWS, HALO - 8), 8), 8)
-        rims = [
-            remote(ext.at[MASK, main], rim_e.at[main], col_send.at[0], col_recv.at[0], lat, left),
-            remote(rim_src.at[main], rim_w.at[main], col_send.at[1], col_recv.at[1], lat, right),
-            remote(ext.at[MASK, extra], rim_e.at[extra], col_send.at[2], col_recv.at[2], lat, left),
-            remote(rim_src.at[extra], rim_w.at[extra], col_send.at[3], col_recv.at[3], lat, right),
-        ]
-        rims[0].start()
-        rims[1].start()
         pltpu.make_async_remote_copy(
             src_ref=cut_src.at[z], dst_ref=cuts_ref, send_sem=cut_send.at[0],
             recv_sem=cut_recv.at[0], device_id=at(beside_lat, lon),
@@ -415,91 +420,41 @@
                     *owner_of(b, p),
                 ).start()
 
-        edge = jnp.where(lat == 0, BLOCKS - 1, 0)
-
-        def send_early(i):
-            @pl.when(far_first(i) != edge)
-            def _():
-                send_block(far_first(i))
-
-        def send_skipped(i):
-            @pl.when(far_first(i) == edge)
-            def _():
-                send_block(edge)
-
-        over(EARLY, send_early)
-        wait_rows()
-
-        @pl.when(lat == 0)
-        def _():
-            rim_src[HALO + ROWS : HALO + ROWS + 8] = plus_face(
-                0, slice(HALO + ROWS, HALO + ROWS + 8)
-            )
-
-        @pl.when(lat > 0)
-        def _():
-            rim_src[HALO - 8 : HALO] = plus_face(0, slice(HALO - 8, HALO))
-
-        rims[2].start()
-        rims[3].start()
-
-        @pl.when(lat == 0)
-        def _():
-            fill(BLOCKS - 1, BLOCKS + 1)
-            fill(BLOCKS, BLOCKS + 2)
-
-        @pl.when(lat > 0)
-        def _():
-            fill(0, 2)
-            fill(BLOCKS, 1)
-
-        over(EARLY, send_skipped)
-        send_block(jnp.int32(BLOCKS))
-        over(2, lambda i: send_block(far_first(EARLY + i)))
-        for rim in rims:
-            rim.wait_recv()
-        here = slice(8, 8 + WIDE)
-        lane = iota((WIDE, LANES), 1)
-        mine = ext[MASK, here]
-        mask_east = jnp.where(
-            lane == LANES - 1, pltpu.roll(rim_e[here], LANES - 1, 1), pltpu.roll(mine, LANES - 1, 1)
-        )
-        plus_west = jnp.where(
-            lane == 0, pltpu.roll(rim_w[here], 1, 1), pltpu.roll(rim_src[here], 1, 1)
-        )
-        faces = (
-            minus_face(0, here) * mask_east,
-            -mine * plus_west,
-            minus_face(2, here) * ext[MASK, 9 : 9 + WIDE],
-            -mine * plus_face(2, slice(7, 7 + WIDE)),
-        )
-        low = iota((8, LANES), 0) < EDGE
-        for k in range(4):
-            face = faces[k].reshape(WIDE // 8, 8, LANES)
-            coef_src[0:BLOCKS, k, 0] = face[1:9]
-            coef_src[0:BLOCKS, k, 1] = jnp.where(low[None], face[2:10], face[0:8])
-
-            @pl.when(lat == 0)
-            def _():
-                coef_src[BLOCKS, k, 0] = face[9]
-                coef_src[BLOCKS, k, 1] = jnp.where(low, 0.0, face[8])
-
-            @pl.when(lat > 0)
-            def _():
-                coef_src[BLOCKS, k, 0] = face[0]
-                coef_src[BLOCKS, k, 1] = jnp.where(low, face[1], 0.0)
-
         def send_coef(b):
             remote(
                 coef_src.at[b], coef.at[y, z], cf_send.at[0], cf_recv.at[z], *owner_of(b, y)
             ).start()
 
+        def send_free(i):
+            @pl.when(far_first(i) != edge)
+            def _():
+                send_coef(far_first(i))
+
+        over(RINGS, send_free)
+        wait_rows()
+        slots = (jnp.where(first_band, edge, BLOCKS), jnp.where(first_band, BLOCKS, edge))
+        for k, face in enumerate(face_tiles(jnp.where(first_band, ROWS, 0), 4)):
+            for j in range(2):
+                coef_src[slots[j], k, 0] = face[1 + j]
+                coef_src[slots[j], k, 1] = jnp.where(low[0], face[2 + j], face[j])
+
         send_coef(jnp.int32(BLOCKS))
-        over(RINGS, lambda i: send_coef(far_first(i)))
-        over(RINGS - EARLY - 2, lambda i: send_block(far_first(EARLY + 2 + i)))
-
-        for rim in rims:
-            rim.wait_send()
+        send_coef(edge)
+
+        @pl.when(lat == 0)
+        def _():
+            fill(BLOCKS - 1, BLOCKS + 1)
+            fill(BLOCKS, BLOCKS + 2)
+
+        @pl.when(lat > 0)
+        def _():
+            fill(0, 2)
+            fill(BLOCKS, 1)
+
+        over(2, lambda i: send_block(far_first(i)))
+        send_block(jnp.int32(BLOCKS))
+        over(RINGS - 2, lambda i: send_block(far_first(2 + i)))
+
         wait_bytes(cuts_ref, cut_send.at[0])
 
         @pl.when(z == LAST_RING)
@@ -547,12 +502,19 @@
             over(RINGS, hand_on)
             wait_bytes(cuts_ref, cut_recv.at[0])
             cuts = cuts_ref[...].astype(jnp.int32)
+            shape = (TILES, 8, LANES)
+            wave = iota(shape, 0) + TILES * iota(shape, 2)
+            wave = jnp.minimum(wave, NLON - wave)
+            for half in range(2):
+                kept_ref[half] = jnp.where(wave <= cuts[half][None], 1.0 / NLON, 0.0).astype(
+                    F32
+                ).reshape(2 * LANES, LANES)
             wait_bytes(lam, in_recv.at[0])
 
             def step(s):
                 for half in range(2):
                     real, imag = filter_circles(
-                        lam[:, 0, half], lam[:, 1, half], cuts[half], high_ref, low_ref, turn_ref
+                        lam[:, 0, half], lam[:, 1, half], kept_ref[half], high_ref, low_ref, turn_ref
                     )
                     fil[:, 0, half] = real
                     fil[:, 1, half] = imag
@@ -561,7 +523,17 @@
                 def _():
                     wait_bytes(coef.at[pl.ds(0, COLS - 1)], pass_recv.at[0])
 
-                lam[...] = circle_step(fil[...], coef)
+                    def circle(k):
+                        parts = [coef[c, :, k] for c in range(COLS)]
+                        return jnp.stack(parts, axis=1).reshape(TILES, 2, 8, LANES)
+
+                    mine = circle(4)
+                    faces[:, 0] = circle(0) * neighbour(mine, -1)
+                    faces[:, 1] = -mine * neighbour(circle(1), 1)
+                    faces[:, 2] = circle(2)
+                    faces[:, 3] = circle(3)
+
+                lam[...] = circle_step(fil[...], faces[...])
 
             over(STEPS, step)
 
@@ -629,7 +601,7 @@
         def plus(kappa, speed):
             return [m * (k - 0.5 * f) for m, k, f in zip(open_m, kappa, speed)]
 
-        faces = (
+        wide_faces = (
             [a * b for a, b in zip(minus(kappa_e, speed_e), east_of(open_m))],
             [-a * b for a, b in zip(open_m, west_of(plus(kappa_e, speed_e)))],
             [a * b for a, b in zip(minus(kappa_n, speed_n), north_of(open_m))],
@@ -637,7 +609,7 @@
         )
         for k in range(4):
             for side in range(2):
-                wide_coef[k, side] = faces[k][side]
+                wide_coef[k, side] = wide_faces[k][side]
 
         def level(p):
             from_right = pltpu.roll(packed_r[...], LANES - 8 * p, 1)
@@ -705,14 +677,13 @@
             room(72, 8, LANES),
             room(PLANES, EXT, LANES),
             room(BLOCKS + 1, LEVELS, 2, 8, LANES),
-            room(BLOCKS + 1, 4, 2, 8, LANES),
+            room(BLOCKS + 1, 5, 2, 8, LANES),
             room(BLOCKS + 1, 2, 8, LANES),
-            room(EXT, LANES),
-            room(EXT, LANES),
-            room(EXT, LANES),
             room(TILES, 2, 2, 8, LANES),
             room(TILES, 2, 2, 8, LANES),
-            room(COLS, RINGS, 4, 2, 8, LANES),
+            room(COLS, RINGS, 5, 2, 8, LANES),
+            room(TILES, 4, 2, 8, LANES),
+            room(2, 2 * LANES, LANES),
             room(2, 8, LANES),
             room(WIDE, LANES),
             room(WIDE, LANES),
@@ -720,7 +691,7 @@
             room(4, 2, WIDE, LANES),
             room(LEVELS, ROWS, LANES),
             dma((9,)),
-            dma((2,)), dma((2,)), dma((4,)), dma((4,)), dma((2,)), dma((1,)), dma((1,)), dma((1,)),
+            dma((2,)), dma((2,)), dma((2,)), dma((2,)), dma((2,)), dma((1,)), dma((1,)), dma((1,)),
             dma((1,)), dma((RINGS,)), dma((1,)), dma((1,)), dma((1,)), dma((1,)), dma((1,)), dma((1,)),
         ],
         compiler_params=pltpu.CompilerParams(

time: 47 us -> 43 us (0.915)
  Pallas kernels: 45.2 us -> 41.1 us
    pallas_call x1, Pallas kernels: 45.2 us -> 41.1 us  [shards(): pl.pallas_call(kernel, out_shape=[jax.ShapeDtypeStruct((LEVELS, ROWS, LAN...]
where the time goes in v5:
time: 43 us; the launch traced here: 42.9 us
  Pallas kernels  41.1 us (96%)
  other arithmetic  1.75 us (4%)
    pallas_call x1, Pallas kernels, shards(): pl.pallas_call(kernel, out_shape=[jax.ShapeDtypeStruct((LEVELS, ROWS, LAN...  41.1 us
    select_n x1, other arithmetic, shards(): return jnp.where(taken, jnp.tile(shared, (1, ROWS // 8, 1)), field)  1.74 us

profile of v5, /device:TPU:1, one launch (start us, length us, event | category | flops | bytes accessed | tf_op | source)
XLA Modules:
  0.0 42.9 jit_solution(9565981233288703409)
XLA Ops:
  0.0 41.1 %shard_map.91 = (f32[8,64,128]{2,1,0:T(8,128)}, f32[8,8,128]{2,1,0:T(8,128)}) custom-call(f32[8,64,128]{2,1,0:T(8,128)} %cot.1, f32[64,128]{1,0:T(8,128)} %diff_east_in.1, f32[64,128]{1,0:T(8,128)} %diff_north_in.1, f32[64,128]{1,0:T(8,128)} %flow_east_in.1, f32[64,128]{1,0:T(8,128)} %flow_north_in.1, s32[64,128]{1,0:T(8,128)} %sea_in.1, s32[64]{0:T(128)} %cutoff_in.1, ...), custom_call_target="tpu_custom_call" | custom-call | tf_op jit(solution)/shard_map/pallas_call | solution.py:663
  41.2 1.7 %bitcast_select_fusion = f32[8,64,128]{2,1,0:T(8,128)} fusion(f32[8,64,128]{2,1,0:T(8,128)} %get-tuple-element.8, f32[8,8,128]{2,1,0:T(8,128)} %get-tuple-element.7, pred[64]{0:T(512)(128)(4,1)S(1)} %and_or_fusion), kind=kLoop, calls=%fused_computation | loop fusion | flops 65536 | bytes 557120 | tf_op jit(solution)/shard_map/jit(_where)/select_n | solution.py:709
  (1 shorter events, 0.0 us)

commit v6 on v5

--- a/solution.py
+++ b/solution.py
@@ -162,6 +162,31 @@
     return total
 
 
+def last_step(cells, before, after, coef):
+    x = cells[:, :, 0]
+    rim = cells[:, :, 1]
+    count = x.shape[0]
+    lane = iota(x.shape, 3)
+    row = iota(x.shape, 2)
+
+    def turn(v, step, dim):
+        flat = pltpu.roll(v.reshape(-1, 8, LANES), step % v.shape[dim], dim - 1)
+        return flat.reshape(v.shape)
+
+    east = turn(x, -1, 3)
+    next_east = turn(jnp.concatenate([x[1:], after[None]]), -1, 3)
+    east = jnp.where(lane == LANES - 1, next_east, east)
+    west = turn(x, 1, 3)
+    next_west = turn(jnp.concatenate([before[None], x[: count - 1]]), 1, 3)
+    west = jnp.where(lane == 0, next_west, west)
+    up = jnp.where(row == 7, turn(rim, -1, 2), turn(x, -1, 2))
+    down = jnp.where(row == 0, turn(rim, 1, 2), turn(x, 1, 2))
+    total = x
+    for k, near in enumerate((east, west, up, down)):
+        total = total + coef[:, k : k + 1] * (x - near)
+    return total
+
+
 def neighbour(x, step):
     shape = (TILES * 2, 8, LANES)
     lane = iota(shape, 2)
@@ -177,7 +202,7 @@
     out, row_x,
     sea, cutoff, wide_ref, high_ref, low_ref, turn_ref,
     ext, lam_src, coef_src, cut_src,
-    lam, fil, coef, faces, kept_ref, cuts_ref, packed, packed_l, packed_r, wide_coef, mid_out,
+    lam, fil, done, coef, faces, kept_ref, cuts_ref, packed, packed_l, packed_r, wide_coef, mid_out,
     load_sem, row_send, row_recv, col_send, col_recv, cut_send, cut_recv, in_send, in_recv,
     cf_send, cf_recv, pass_send, pass_recv, out_send, out_recv, ox_recv, store_sem,
 ):
@@ -401,18 +426,6 @@
 
     @pl.when(polar)
     def _():
-        pltpu.make_async_remote_copy(
-            src_ref=cut_src.at[z], dst_ref=cuts_ref, send_sem=cut_send.at[0],
-            recv_sem=cut_recv.at[0], device_id=at(beside_lat, lon),
-            device_id_type=pl.DeviceIdType.MESH,
-        ).start()
-
-        @pl.when(z == LAST_RING)
-        def _():
-            remote(
-                cut_src.at[BLOCKS], cuts_ref, cut_send.at[1], cut_recv.at[0], last_lat, lon
-            ).start()
-
         def send_block(b):
             for p in range(PAIRS):
                 remote(
@@ -431,6 +444,18 @@
                 send_coef(far_first(i))
 
         over(RINGS, send_free)
+        pltpu.make_async_remote_copy(
+            src_ref=cut_src.at[z], dst_ref=cuts_ref, send_sem=cut_send.at[0],
+            recv_sem=cut_recv.at[0], device_id=at(beside_lat, lon),
+            device_id_type=pl.DeviceIdType.MESH,
+        ).start()
+
+        @pl.when(z == LAST_RING)
+        def _():
+            remote(
+                cut_src.at[BLOCKS], cuts_ref, cut_send.at[1], cut_recv.at[0], last_lat, lon
+            ).start()
+
         wait_rows()
         slots = (jnp.where(first_band, edge, BLOCKS), jnp.where(first_band, BLOCKS, edge))
         for k, face in enumerate(face_tiles(jnp.where(first_band, ROWS, 0), 4)):
@@ -451,9 +476,8 @@
             fill(0, 2)
             fill(BLOCKS, 1)
 
-        over(2, lambda i: send_block(far_first(i)))
         send_block(jnp.int32(BLOCKS))
-        over(RINGS - 2, lambda i: send_block(far_first(2 + i)))
+        over(RINGS, lambda i: send_block(far_first(i)))
 
         wait_bytes(cuts_ref, cut_send.at[0])
 
@@ -509,61 +533,67 @@
                 kept_ref[half] = jnp.where(wave <= cuts[half][None], 1.0 / NLON, 0.0).astype(
                     F32
                 ).reshape(2 * LANES, LANES)
+            wait_bytes(coef.at[pl.ds(0, COLS - 1)], pass_recv.at[0])
+
+            def circle(k):
+                parts = [coef[c, :, k] for c in range(COLS)]
+                return jnp.stack(parts, axis=1).reshape(TILES, 2, 8, LANES)
+
+            mine = circle(4)
+            faces[:, 0] = circle(0) * neighbour(mine, -1)
+            faces[:, 1] = -mine * neighbour(circle(1), 1)
+            faces[:, 2] = circle(2)
+            faces[:, 3] = circle(3)
             wait_bytes(lam, in_recv.at[0])
 
-            def step(s):
+            def filtered():
                 for half in range(2):
                     real, imag = filter_circles(
-                        lam[:, 0, half], lam[:, 1, half], kept_ref[half], high_ref, low_ref, turn_ref
+                        lam[:, 0, half], lam[:, 1, half], kept_ref[half], high_ref, low_ref,
+                        turn_ref,
                     )
                     fil[:, 0, half] = real
                     fil[:, 1, half] = imag
 
-                @pl.when(s == 0)
+            def step(s):
+                filtered()
+                lam[...] = circle_step(fil[...], faces[...])
+
+            over(STEPS - 1, step)
+            filtered()
+
+            my_levels = pl.ds(2 * pair, 2)
+            rows = pl.ds(pl.multiple_of(8 * jnp.minimum(block, BLOCKS - 1), 8), 8)
+
+            def finish(i):
+                ring = far_first(i)
+                first = COLS * ring
+                done[pl.ds(first, COLS)] = last_step(
+                    fil[pl.ds(first, COLS)],
+                    fil[lax.rem(first + TILES - 1, TILES), :, 0],
+                    fil[lax.rem(first + COLS, TILES), :, 0],
+                    faces[pl.ds(first, COLS), :, 0],
+                )
+
+                @pl.when(jnp.logical_not(last_block))
                 def _():
-                    wait_bytes(coef.at[pl.ds(0, COLS - 1)], pass_recv.at[0])
-
-                    def circle(k):
-                        parts = [coef[c, :, k] for c in range(COLS)]
-                        return jnp.stack(parts, axis=1).reshape(TILES, 2, 8, LANES)
-
-                    mine = circle(4)
-                    faces[:, 0] = circle(0) * neighbour(mine, -1)
-                    faces[:, 1] = -mine * neighbour(circle(1), 1)
-                    faces[:, 2] = circle(2)
-                    faces[:, 3] = circle(3)
-
-                lam[...] = circle_step(fil[...], faces[...])
-
-            over(STEPS, step)
-
-            my_levels = pl.ds(2 * pair, 2)
-
-            @pl.when(jnp.logical_not(last_block))
-            def _():
-                rows = pl.ds(pl.multiple_of(8 * jnp.minimum(block, BLOCKS - 1), 8), 8)
-
-                def send_out(i):
                     for c in range(COLS):
-                        tile = COLS * far_first(i) + lax.rem(y + c, COLS)
+                        tile = first + lax.rem(y + c, COLS)
                         remote(
-                            lam.at[tile, :, 0], out.at[my_levels, rows], out_send.at[0],
+                            done.at[tile], out.at[my_levels, rows], out_send.at[0],
                             out_recv.at[0], polar_lat, tile,
                         ).start()
 
-                over(RINGS, send_out)
-
-            @pl.when(last_block)
-            def _():
-                def send_x(i):
+                @pl.when(last_block)
+                def _():
                     for c in range(COLS):
-                        tile = COLS * far_first(i) + lax.rem(y + c, COLS)
+                        tile = first + lax.rem(y + c, COLS)
                         remote(
-                            lam.at[tile, :, 0], row_x.at[my_levels], out_send.at[0], ox_recv.at[0],
+                            done.at[tile], row_x.at[my_levels], out_send.at[0], ox_recv.at[0],
                             beside_lat, tile,
                         ).start()
 
-                over(RINGS, send_x)
+            over(RINGS, finish)
 
         to_left.wait_recv()
         to_right.wait_recv()
@@ -631,7 +661,7 @@
         @pl.when(is_owner)
         def _():
             wait_bytes(coef.at[pl.ds(0, COLS - 1)], pass_send.at[0])
-            wait_bytes(lam.at[:, :, 0], out_send.at[0])
+            wait_bytes(done, out_send.at[0])
 
         to_left.wait_send()
         to_right.wait_send()
@@ -681,6 +711,7 @@
             room(BLOCKS + 1, 2, 8, LANES),
             room(TILES, 2, 2, 8, LANES),
             room(TILES, 2, 2, 8, LANES),
+            room(TILES, 2, 8, LANES),
             room(COLS, RINGS, 5, 2, 8, LANES),
             room(TILES, 4, 2, 8, LANES),
             room(2, 2 * LANES, LANES),

time: 43 us -> 44.7 us (1.040)
  Pallas kernels: 41.1 us -> 42.8 us
    pallas_call x1, Pallas kernels: 41.1 us -> 42.8 us  [shards(): pl.pallas_call(kernel, out_shape=[jax.ShapeDtypeStruct((LEVELS, ROWS, LAN...]
where the time goes in v6:
time: 44.7 us; the launch traced here: 44.6 us
  Pallas kernels  42.8 us (96%)
  other arithmetic  1.75 us (4%)
    pallas_call x1, Pallas kernels, shards(): pl.pallas_call(kernel, out_shape=[jax.ShapeDtypeStruct((LEVELS, ROWS, LAN...  42.8 us
    select_n x1, other arithmetic, shards(): return jnp.where(taken, jnp.tile(shared, (1, ROWS // 8, 1)), field)  1.74 us

profile of v6, /device:TPU:1, one launch (start us, length us, event | category | flops | bytes accessed | tf_op | source)
XLA Modules:
  0.0 44.6 jit_solution(1752392438298465237)
XLA Ops:
  0.0 42.8 %shard_map.91 = (f32[8,64,128]{2,1,0:T(8,128)}, f32[8,8,128]{2,1,0:T(8,128)}) custom-call(f32[8,64,128]{2,1,0:T(8,128)} %cot.1, f32[64,128]{1,0:T(8,128)} %diff_east_in.1, f32[64,128]{1,0:T(8,128)} %diff_north_in.1, f32[64,128]{1,0:T(8,128)} %flow_east_in.1, f32[64,128]{1,0:T(8,128)} %flow_north_in.1, s32[64,128]{1,0:T(8,128)} %sea_in.1, s32[64]{0:T(128)} %cutoff_in.1, ...), custom_call_target="tpu_custom_call" | custom-call | tf_op jit(solution)/shard_map/pallas_call | solution.py:693
  42.8 1.7 %bitcast_select_fusion = f32[8,64,128]{2,1,0:T(8,128)} fusion(f32[8,64,128]{2,1,0:T(8,128)} %get-tuple-element.8, f32[8,8,128]{2,1,0:T(8,128)} %get-tuple-element.7, pred[64]{0:T(512)(128)(4,1)S(1)} %and_or_fusion), kind=kLoop, calls=%fused_computation | loop fusion | flops 65536 | bytes 557120 | tf_op jit(solution)/shard_map/jit(_where)/select_n | solution.py:740
  (1 shorter events, 0.0 us)

commit v7 on v6

--- a/solution.py
+++ b/solution.py
@@ -26,7 +26,7 @@
 LATS = 8
 COLS = 4
 RINGS = 8
-LAST_RING = 4
+EXTRA = 3
 
 F32 = jnp.float32
 
@@ -188,12 +188,44 @@
 
 
 def neighbour(x, step):
-    shape = (TILES * 2, 8, LANES)
+    shape = (x.size // (8 * LANES), 8, LANES)
+    width = shape[0] // TILES
     lane = iota(shape, 2)
     turned = pltpu.roll(x.reshape(shape), step % LANES, 2)
-    moved = jnp.concatenate([turned[-2 * step :], turned[: -2 * step]])
+    moved = jnp.concatenate([turned[-width * step :], turned[: -width * step]])
     edge = 0 if step > 0 else LANES - 1
     return jnp.where(lane == edge, moved, turned).reshape(x.shape)
+
+
+def edge_step(x, coef, extra, coef_x):
+    full = (TILES, 2, 8, LANES)
+    row = iota(full, 2)
+    own, rim = x[:, :, 0], x[:, :, 1]
+
+    def turn(v, step):
+        return pltpu.roll(v.reshape(-1, 8, LANES), step, 1).reshape(v.shape)
+
+    up_own = jnp.where(row == 7, turn(rim, 7), turn(own, 7))
+    down_own = jnp.where(row == 0, turn(rim, 1), turn(own, 1))
+    up_rim = jnp.where(row == 7, turn(own, 7), turn(rim, 7))
+    up_rim = jnp.where(row == 3, jnp.stack([turn(extra, 3), turn(extra, 7)], axis=1), up_rim)
+    down_rim = jnp.where(row == 0, turn(own, 1), turn(rim, 1))
+    down_rim = jnp.where(row == 4, jnp.stack([turn(extra, 1), turn(extra, 5)], axis=1), down_rim)
+    row = iota(extra.shape, 1)
+    up_x = jnp.where(row == 3, turn(rim[:, 0], 7), turn(extra, 7))
+    up_x = jnp.where(row == 7, turn(rim[:, 1], 3), up_x)
+    down_x = jnp.where(row == 0, turn(rim[:, 0], 5), turn(extra, 1))
+    down_x = jnp.where(row == 4, turn(rim[:, 1], 1), down_x)
+
+    up = jnp.stack([up_own, up_rim], axis=2)
+    down = jnp.stack([down_own, down_rim], axis=2)
+    total = x
+    for k, near in enumerate((neighbour(x, -1), neighbour(x, 1), up, down)):
+        total = total + coef[:, k : k + 1] * (x - near)
+    total_x = extra
+    for k, near in enumerate((neighbour(extra, -1), neighbour(extra, 1), up_x, down_x)):
+        total_x = total_x + coef_x[:, k] * (extra - near)
+    return total, total_x
 
 
 def kernel(
@@ -201,10 +233,11 @@
     turn_in,
     out, row_x,
     sea, cutoff, wide_ref, high_ref, low_ref, turn_ref,
-    ext, lam_src, coef_src, cut_src,
+    ext, lam_src, coef_src, cut_src, extra_src, strip_src, extra, strip, faces_x, done_x,
     lam, fil, done, coef, faces, kept_ref, cuts_ref, packed, packed_l, packed_r, wide_coef, mid_out,
     load_sem, row_send, row_recv, col_send, col_recv, cut_send, cut_recv, in_send, in_recv,
-    cf_send, cf_recv, pass_send, pass_recv, out_send, out_recv, ox_recv, store_sem,
+    cf_send, cf_recv, pass_send, pass_recv, out_send, out_recv, ox_recv, store_sem, lx_send, lx_recv,
+    sx_send, sx_recv, px_send, px_recv, ox_send,
 ):
     lon = lax.axis_index("lon")
     lat = lax.axis_index("lat")
@@ -215,15 +248,12 @@
     beside = jnp.logical_or(lat == 1, lat == LATS - 2)
     polar_lat = jnp.where(first_band, 0, LATS - 1)
     beside_lat = jnp.where(first_band, 1, LATS - 2)
-    last_lat = jnp.where(first_band, 2, LATS - 3)
-    last_block = jnp.logical_and(lat == last_lat, z == LAST_RING)
-    is_owner = jnp.logical_or(beside, last_block)
-    block = jnp.where(beside, z, BLOCKS)
+    edge = jnp.where(first_band, BLOCKS - 1, 0)
+    is_edge = jnp.logical_and(beside, z == edge)
     pair = y
 
     def owner_of(b, p):
-        to_lat = jnp.where(b == BLOCKS, last_lat, beside_lat)
-        return to_lat, COLS * jnp.where(b == BLOCKS, LAST_RING, b) + p
+        return beside_lat, COLS * b + p
 
     main = pl.ds(HALO, ROWS)
     plane_loads = [
@@ -251,7 +281,7 @@
     def _():
         cut_load.start()
 
-    @pl.when(is_owner)
+    @pl.when(beside)
     def _():
         for load in table_loads:
             load.start()
@@ -297,7 +327,7 @@
 
         over(BLOCKS, greet)
 
-    @pl.when(is_owner)
+    @pl.when(beside)
     def _():
         def greet(i):
             for c in range(COLS):
@@ -310,7 +340,9 @@
     @pl.when(beside)
     def _():
         for p in range(PAIRS):
-            hail(*owner_of(BLOCKS, p))
+            @pl.when(COLS * edge + p != lon)
+            def _():
+                hail(lat, COLS * edge + p)
 
     @pl.when(jnp.logical_not(polar))
     def _():
@@ -354,8 +386,6 @@
 
     low = iota((1, 8, LANES), 1) < EDGE
     free = jnp.where(first_band, 0, 1)
-    edge = jnp.where(first_band, BLOCKS - 1, 0)
-
     @pl.when(polar)
     def _():
         zeros = jnp.zeros((PLANES, 8, LANES), F32)
@@ -391,13 +421,10 @@
         for b in range(BLOCKS):
             cut_src[b, 0] = cuts[b + 2]
             cut_src[b, 1] = jnp.where(row < EDGE, cuts[b + 3], cuts[b + 1])
-        cut_src[BLOCKS, 0] = open_cut
-        low_half = jnp.where(first_band, open_cut, cuts[2])
-        high_half = jnp.where(first_band, cuts[BLOCKS + 1], open_cut)
-        cut_src[BLOCKS, 1] = jnp.where(row < EDGE, low_half, high_half)
-
-    peers = jnp.where(polar, 1 + 9 * PAIRS, 4)
-    peers = peers + jnp.where(is_owner, TILES + COLS - 1, 0)
+
+    peers = jnp.where(polar, 1 + BLOCKS * PAIRS, 4)
+    peers = peers + jnp.where(beside, TILES + COLS - 1, 0)
+    peers = peers + jnp.where(is_edge, TILES - 1, 0)
     pl.semaphore_wait(barrier, peers)
 
     low_rows = ext.at[:, pl.ds(HALO, 8)]
@@ -450,41 +477,47 @@
             device_id_type=pl.DeviceIdType.MESH,
         ).start()
 
-        @pl.when(z == LAST_RING)
-        def _():
-            remote(
-                cut_src.at[BLOCKS], cuts_ref, cut_send.at[1], cut_recv.at[0], last_lat, lon
-            ).start()
-
         wait_rows()
-        slots = (jnp.where(first_band, edge, BLOCKS), jnp.where(first_band, BLOCKS, edge))
+        def halves(low_from, high_from):
+            lower = jnp.where(first_band, pltpu.roll(low_from, 4, 1), low_from)
+            upper = jnp.where(first_band, high_from, pltpu.roll(high_from, 4, 1))
+            return jnp.where(low, lower, upper)
+
+        strips = []
         for k, face in enumerate(face_tiles(jnp.where(first_band, ROWS, 0), 4)):
-            for j in range(2):
-                coef_src[slots[j], k, 0] = face[1 + j]
-                coef_src[slots[j], k, 1] = jnp.where(low[0], face[2 + j], face[j])
-
-        send_coef(jnp.int32(BLOCKS))
+            coef_src[edge, k, 0] = jnp.where(first_band, face[1], face[2])
+            coef_src[edge, k, 1] = jnp.where(
+                low[0], jnp.where(first_band, face[2], face[3]), jnp.where(first_band, face[0], face[1])
+            )
+            strips.append(jnp.where(first_band, face[2], face[1])[None])
+        for j in range(EXTRA):
+            strip_src[j] = halves(strips[2 * j], strips[min(2 * j + 1, 4)])[0]
         send_coef(edge)
+        remote(
+            strip_src, strip.at[y, z], sx_send.at[0], sx_recv.at[0], *owner_of(edge, y)
+        ).start()
 
         @pl.when(lat == 0)
         def _():
             fill(BLOCKS - 1, BLOCKS + 1)
-            fill(BLOCKS, BLOCKS + 2)
 
         @pl.when(lat > 0)
         def _():
             fill(0, 2)
-            fill(BLOCKS, 1)
-
-        send_block(jnp.int32(BLOCKS))
+
+        beyond_rows = pl.ds(pl.multiple_of(jnp.where(first_band, HALO + ROWS, HALO - 8), 8), 8)
+        outside = ext[pl.ds(0, LEVELS), beyond_rows]
+        for p in range(PAIRS):
+            extra_src[p] = halves(outside[2 * p : 2 * p + 1], outside[2 * p + 1 : 2 * p + 2])[0]
+            remote(
+                extra_src.at[p], extra.at[lon], lx_send.at[0], lx_recv.at[0], *owner_of(edge, p)
+            ).start()
         over(RINGS, lambda i: send_block(far_first(i)))
 
         wait_bytes(cuts_ref, cut_send.at[0])
 
-        @pl.when(z == LAST_RING)
-        def _():
-            wait_bytes(cuts_ref, cut_send.at[1])
-
+        wait_bytes(extra_src, lx_send.at[0])
+        wait_bytes(strip_src, sx_send.at[0])
         wait_bytes(lam_src, in_send.at[0])
         wait_bytes(coef_src, cf_send.at[0])
         wait_bytes(out, out_recv.at[0])
@@ -506,7 +539,7 @@
         to_right = remote(packed, packed_l, col_send.at[1], col_recv.at[1], lat, right)
         to_left.start()
         to_right.start()
-        @pl.when(is_owner)
+        @pl.when(beside)
         def _():
             for load in table_loads:
                 load.wait()
@@ -524,6 +557,16 @@
                     ).start()
 
             over(RINGS, hand_on)
+
+            @pl.when(is_edge)
+            def _():
+                wait_bytes(strip.at[y], sx_recv.at[0])
+                for c in range(1, COLS):
+                    remote(
+                        strip.at[y], strip.at[y], px_send.at[0], px_recv.at[0],
+                        lat, COLS * z + lax.rem(y + c, COLS),
+                    ).start()
+
             wait_bytes(cuts_ref, cut_recv.at[0])
             cuts = cuts_ref[...].astype(jnp.int32)
             shape = (TILES, 8, LANES)
@@ -533,18 +576,11 @@
                 kept_ref[half] = jnp.where(wave <= cuts[half][None], 1.0 / NLON, 0.0).astype(
                     F32
                 ).reshape(2 * LANES, LANES)
-            wait_bytes(coef.at[pl.ds(0, COLS - 1)], pass_recv.at[0])
-
-            def circle(k):
-                parts = [coef[c, :, k] for c in range(COLS)]
-                return jnp.stack(parts, axis=1).reshape(TILES, 2, 8, LANES)
-
-            mine = circle(4)
-            faces[:, 0] = circle(0) * neighbour(mine, -1)
-            faces[:, 1] = -mine * neighbour(circle(1), 1)
-            faces[:, 2] = circle(2)
-            faces[:, 3] = circle(3)
             wait_bytes(lam, in_recv.at[0])
+
+            @pl.when(is_edge)
+            def _():
+                wait_bytes(extra, lx_recv.at[0])
 
             def filtered():
                 for half in range(2):
@@ -557,40 +593,93 @@
 
             def step(s):
                 filtered()
-                lam[...] = circle_step(fil[...], faces[...])
+
+                @pl.when(s == 0)
+                def _():
+                    wait_bytes(coef.at[pl.ds(0, COLS - 1)], pass_recv.at[0])
+
+                    def circle(k):
+                        parts = [coef[c, :, k] for c in range(COLS)]
+                        return jnp.stack(parts, axis=1).reshape(TILES, 2, 8, LANES)
+
+                    mine = circle(4)
+                    faces[:, 0] = circle(0) * neighbour(mine, -1)
+                    faces[:, 1] = -mine * neighbour(circle(1), 1)
+                    faces[:, 2] = circle(2)
+                    faces[:, 3] = circle(3)
+
+                @pl.when(jnp.logical_and(is_edge, s == 0))
+                def _():
+                    wait_bytes(strip.at[pl.ds(0, COLS - 1)], px_recv.at[0])
+
+                    def circle(k):
+                        parts = [strip[c, :, k // 2] for c in range(COLS)]
+                        both = jnp.stack(parts, axis=1).reshape(TILES, 8, LANES)
+                        turned = pltpu.roll(both, 4, 1)
+                        lower = iota(both.shape, 1) < EDGE
+                        if k % 2:
+                            return jnp.where(lower, turned, both)
+                        return jnp.where(lower, both, turned)
+
+                    mine = circle(4)
+                    faces_x[:, 0] = circle(0) * neighbour(mine, -1)
+                    faces_x[:, 1] = -mine * neighbour(circle(1), 1)
+                    faces_x[:, 2] = circle(2)
+                    faces_x[:, 3] = circle(3)
+
+                @pl.when(is_edge)
+                def _():
+                    lam[...], extra[...] = edge_step(
+                        fil[...], faces[...], extra[...], faces_x[...]
+                    )
+
+                @pl.when(jnp.logical_not(is_edge))
+                def _():
+                    lam[...] = circle_step(fil[...], faces[...])
 
             over(STEPS - 1, step)
             filtered()
 
             my_levels = pl.ds(2 * pair, 2)
-            rows = pl.ds(pl.multiple_of(8 * jnp.minimum(block, BLOCKS - 1), 8), 8)
+            rows = pl.ds(pl.multiple_of(8 * z, 8), 8)
+
+            @pl.when(is_edge)
+            def _():
+                total, _ = edge_step(fil[...], faces[...], extra[...], faces_x[...])
+                done[...] = total[:, :, 0]
+                done_x[...] = total[:, :, 1]
 
             def finish(i):
                 ring = far_first(i)
                 first = COLS * ring
-                done[pl.ds(first, COLS)] = last_step(
-                    fil[pl.ds(first, COLS)],
-                    fil[lax.rem(first + TILES - 1, TILES), :, 0],
-                    fil[lax.rem(first + COLS, TILES), :, 0],
-                    faces[pl.ds(first, COLS), :, 0],
-                )
-
-                @pl.when(jnp.logical_not(last_block))
+
+                @pl.when(jnp.logical_not(is_edge))
                 def _():
-                    for c in range(COLS):
-                        tile = first + lax.rem(y + c, COLS)
+                    done[pl.ds(first, COLS)] = last_step(
+                        fil[pl.ds(first, COLS)],
+                        fil[lax.rem(first + TILES - 1, TILES), :, 0],
+                        fil[lax.rem(first + COLS, TILES), :, 0],
+                        faces[pl.ds(first, COLS), :, 0],
+                    )
+
+                for c in range(COLS):
+                    tile = first + lax.rem(y + c, COLS)
+                    remote(
+                        done.at[tile], out.at[my_levels, rows], out_send.at[0],
+                        out_recv.at[0], polar_lat, tile,
+                    ).start()
+
+                    @pl.when(jnp.logical_and(is_edge, tile != lon))
+                    def _():
                         remote(
-                            done.at[tile], out.at[my_levels, rows], out_send.at[0],
-                            out_recv.at[0], polar_lat, tile,
+                            done_x.at[tile], row_x.at[my_levels], ox_send.at[0], ox_recv.at[0],
+                            beside_lat, tile,
                         ).start()
 
-                @pl.when(last_block)
-                def _():
-                    for c in range(COLS):
-                        tile = first + lax.rem(y + c, COLS)
-                        remote(
-                            done.at[tile], row_x.at[my_levels], out_send.at[0], ox_recv.at[0],
-                            beside_lat, tile,
+                    @pl.when(jnp.logical_and(is_edge, tile == lon))
+                    def _():
+                        pltpu.make_async_copy(
+                            done_x.at[tile], row_x.at[my_levels], ox_recv.at[0]
                         ).start()
 
             over(RINGS, finish)
@@ -658,10 +747,16 @@
         store = pltpu.make_async_copy(mid_out, out, store_sem.at[0])
         store.start()
 
-        @pl.when(is_owner)
+        @pl.when(beside)
         def _():
             wait_bytes(coef.at[pl.ds(0, COLS - 1)], pass_send.at[0])
             wait_bytes(done, out_send.at[0])
+
+            @pl.when(is_edge)
+            def _():
+                wait_bytes(strip.at[pl.ds(0, COLS - 1)], px_send.at[0])
+                wait_bytes(done_x.at[pl.ds(0, TILES - 1)], ox_send.at[0])
+
 
         to_left.wait_send()
         to_right.wait_send()
@@ -706,9 +801,15 @@
             table,
             room(72, 8, LANES),
             room(PLANES, EXT, LANES),
-            room(BLOCKS + 1, LEVELS, 2, 8, LANES),
-            room(BLOCKS + 1, 5, 2, 8, LANES),
-            room(BLOCKS + 1, 2, 8, LANES),
+            room(BLOCKS, LEVELS, 2, 8, LANES),
+            room(BLOCKS, 5, 2, 8, LANES),
+            room(BLOCKS, 2, 8, LANES),
+            room(PAIRS, 8, LANES),
+            room(EXTRA, 8, LANES),
+            room(TILES, 8, LANES),
+            room(COLS, RINGS, EXTRA, 8, LANES),
+            room(TILES, 4, 8, LANES),
+            room(TILES, 2, 8, LANES),
             room(TILES, 2, 2, 8, LANES),
             room(TILES, 2, 2, 8, LANES),
             room(TILES, 2, 8, LANES),
@@ -724,6 +825,7 @@
             dma((9,)),
             dma((2,)), dma((2,)), dma((2,)), dma((2,)), dma((2,)), dma((1,)), dma((1,)), dma((1,)),
             dma((1,)), dma((RINGS,)), dma((1,)), dma((1,)), dma((1,)), dma((1,)), dma((1,)), dma((1,)),
+            dma((1,)), dma((1,)), dma((1,)), dma((1,)), dma((1,)), dma((1,)), dma((1,)),
         ],
         compiler_params=pltpu.CompilerParams(
             collective_id=0, has_side_effects=True, vmem_limit_bytes=63 * 1024 * 1024

time: 44.7 us -> 42.6 us (0.953)
  Pallas kernels: 42.8 us -> 40.4 us
    pallas_call x1, Pallas kernels: 42.8 us -> 40.4 us  [shards(): pl.pallas_call(kernel, out_shape=[jax.ShapeDtypeStruct((LEVELS, ROWS, LAN...]
where the time goes in v7:
time: 42.6 us; the launch traced here: 42.1 us
  Pallas kernels  40.4 us (95%)
  other arithmetic  1.75 us (4%)
    pallas_call x1, Pallas kernels, shards(): pl.pallas_call(kernel, out_shape=[jax.ShapeDtypeStruct((LEVELS, ROWS, LAN...  40.4 us
    select_n x1, other arithmetic, shards(): return jnp.where(taken, jnp.tile(shared, (1, ROWS // 8, 1)), field)  1.74 us

profile of v7, /device:TPU:1, one launch (start us, length us, event | category | flops | bytes accessed | tf_op | source)
XLA Modules:
  0.0 42.1 jit_solution(10258478531516289289)
XLA Ops:
  0.0 40.4 %shard_map.91 = (f32[8,64,128]{2,1,0:T(8,128)}, f32[8,8,128]{2,1,0:T(8,128)}) custom-call(f32[8,64,128]{2,1,0:T(8,128)} %cot.1, f32[64,128]{1,0:T(8,128)} %diff_east_in.1, f32[64,128]{1,0:T(8,128)} %diff_north_in.1, f32[64,128]{1,0:T(8,128)} %flow_east_in.1, f32[64,128]{1,0:T(8,128)} %flow_north_in.1, s32[64,128]{1,0:T(8,128)} %sea_in.1, s32[64]{0:T(128)} %cutoff_in.1, ...), custom_call_target="tpu_custom_call" | custom-call | tf_op jit(solution)/shard_map/pallas_call | solution.py:788
  40.4 1.7 %bitcast_select_fusion = f32[8,64,128]{2,1,0:T(8,128)} fusion(f32[8,64,128]{2,1,0:T(8,128)} %get-tuple-element.8, f32[8,8,128]{2,1,0:T(8,128)} %get-tuple-element.7, pred[64]{0:T(512)(128)(4,1)S(1)} %and_or_fusion), kind=kLoop, calls=%fused_computation | loop fusion | flops 65536 | bytes 557120 | tf_op jit(solution)/shard_map/jit(_where)/select_n | solution.py:842
  (1 shorter events, 0.0 us)

commit v8 on v7

--- a/solution.py
+++ b/solution.py
@@ -470,7 +470,7 @@
             def _():
                 send_coef(far_first(i))
 
-        over(RINGS, send_free)
+        over(RINGS, lambda i: send_free(RINGS - 1 - i))
         pltpu.make_async_remote_copy(
             src_ref=cut_src.at[z], dst_ref=cuts_ref, send_sem=cut_send.at[0],
             recv_sem=cut_recv.at[0], device_id=at(beside_lat, lon),
@@ -512,7 +512,7 @@
             remote(
                 extra_src.at[p], extra.at[lon], lx_send.at[0], lx_recv.at[0], *owner_of(edge, p)
             ).start()
-        over(RINGS, lambda i: send_block(far_first(i)))
+        over(RINGS, lambda i: send_block(far_first(RINGS - 1 - i)))
 
         wait_bytes(cuts_ref, cut_send.at[0])
 
@@ -548,7 +548,7 @@
             low_ref[...] = (wide_ref[...] - high.astype(F32)).astype(jnp.bfloat16)
 
             def hand_on(t):
-                ring = lax.rem(z + t, RINGS)
+                ring = far_first(RINGS - 1 - t)
                 wait_bytes(coef.at[y, ring], cf_recv.at[ring])
                 for c in range(1, COLS):
                     remote(
@@ -650,7 +650,7 @@
                 done_x[...] = total[:, :, 1]
 
             def finish(i):
-                ring = far_first(i)
+                ring = far_first(RINGS - 1 - i)
                 first = COLS * ring
 
                 @pl.when(jnp.logical_not(is_edge))

time: 42.6 us -> 40.7 us (0.955)
  Pallas kernels: 40.4 us -> 38.2 us
    pallas_call x1, Pallas kernels: 40.4 us -> 38.2 us  [shards(): pl.pallas_call(kernel, out_shape=[jax.ShapeDtypeStruct((LEVELS, ROWS, LAN...]
where the time goes in v8:
time: 40.7 us; the launch traced here: 40 us
  Pallas kernels  38.2 us (94%)
  other arithmetic  1.75 us (4%)
    pallas_call x1, Pallas kernels, shards(): pl.pallas_call(kernel, out_shape=[jax.ShapeDtypeStruct((LEVELS, ROWS, LAN...  38.2 us
    select_n x1, other arithmetic, shards(): return jnp.where(taken, jnp.tile(shared, (1, ROWS // 8, 1)), field)  1.74 us

profile of v8, /device:TPU:1, one launch (start us, length us, event | category | flops | bytes accessed | tf_op | source)
XLA Modules:
  0.0 40.0 jit_solution(2785452418975041978)
XLA Ops:
  0.0 38.2 %shard_map.91 = (f32[8,64,128]{2,1,0:T(8,128)}, f32[8,8,128]{2,1,0:T(8,128)}) custom-call(f32[8,64,128]{2,1,0:T(8,128)} %cot.1, f32[64,128]{1,0:T(8,128)} %diff_east_in.1, f32[64,128]{1,0:T(8,128)} %diff_north_in.1, f32[64,128]{1,0:T(8,128)} %flow_east_in.1, f32[64,128]{1,0:T(8,128)} %flow_north_in.1, s32[64,128]{1,0:T(8,128)} %sea_in.1, s32[64]{0:T(128)} %cutoff_in.1, ...), custom_call_target="tpu_custom_call" | custom-call | tf_op jit(solution)/shard_map/pallas_call | solution.py:788
  38.2 1.7 %bitcast_select_fusion = f32[8,64,128]{2,1,0:T(8,128)} fusion(f32[8,64,128]{2,1,0:T(8,128)} %get-tuple-element.8, f32[8,8,128]{2,1,0:T(8,128)} %get-tuple-element.7, pred[64]{0:T(512)(128)(4,1)S(1)} %and_or_fusion), kind=kLoop, calls=%fused_computation | loop fusion | flops 65536 | bytes 557120 | tf_op jit(solution)/shard_map/jit(_where)/select_n | solution.py:842
  (1 shorter events, 0.0 us)

commit v9 on v8

--- a/solution.py
+++ b/solution.py
@@ -249,11 +249,15 @@
     polar_lat = jnp.where(first_band, 0, LATS - 1)
     beside_lat = jnp.where(first_band, 1, LATS - 2)
     edge = jnp.where(first_band, BLOCKS - 1, 0)
-    is_edge = jnp.logical_and(beside, z == edge)
+
+    def flip(b):
+        return jnp.where(first_band, b, BLOCKS - 1 - b)
+
+    is_edge = jnp.logical_and(beside, z == BLOCKS - 1)
     pair = y
 
     def owner_of(b, p):
-        return beside_lat, COLS * b + p
+        return beside_lat, COLS * flip(b) + p
 
     main = pl.ds(HALO, ROWS)
     plane_loads = [
@@ -321,7 +325,7 @@
     @pl.when(polar)
     def _():
         def greet(i):
-            b = far_first(i)
+            b = flip(far_first(i))
             for p in range(PAIRS):
                 hail(*owner_of(b, p))
 
@@ -340,9 +344,9 @@
     @pl.when(beside)
     def _():
         for p in range(PAIRS):
-            @pl.when(COLS * edge + p != lon)
+            @pl.when(COLS * (BLOCKS - 1) + p != lon)
             def _():
-                hail(lat, COLS * edge + p)
+                hail(lat, COLS * (BLOCKS - 1) + p)
 
     @pl.when(jnp.logical_not(polar))
     def _():
@@ -466,13 +470,15 @@
             ).start()
 
         def send_free(i):
-            @pl.when(far_first(i) != edge)
+            b = flip(far_first(i))
+
+            @pl.when(b != edge)
             def _():
-                send_coef(far_first(i))
+                send_coef(b)
 
         over(RINGS, lambda i: send_free(RINGS - 1 - i))
         pltpu.make_async_remote_copy(
-            src_ref=cut_src.at[z], dst_ref=cuts_ref, send_sem=cut_send.at[0],
+            src_ref=cut_src.at[flip(z)], dst_ref=cuts_ref, send_sem=cut_send.at[0],
             recv_sem=cut_recv.at[0], device_id=at(beside_lat, lon),
             device_id_type=pl.DeviceIdType.MESH,
         ).start()
@@ -512,7 +518,7 @@
             remote(
                 extra_src.at[p], extra.at[lon], lx_send.at[0], lx_recv.at[0], *owner_of(edge, p)
             ).start()
-        over(RINGS, lambda i: send_block(far_first(RINGS - 1 - i)))
+        over(RINGS, lambda i: send_block(flip(far_first(RINGS - 1 - i))))
 
         wait_bytes(cuts_ref, cut_send.at[0])
 
@@ -641,7 +647,7 @@
             filtered()
 
             my_levels = pl.ds(2 * pair, 2)
-            rows = pl.ds(pl.multiple_of(8 * z, 8), 8)
+            rows = pl.ds(pl.multiple_of(8 * flip(z), 8), 8)
 
             @pl.when(is_edge)
             def _():
@@ -650,7 +656,7 @@
                 done_x[...] = total[:, :, 1]
 
             def finish(i):
-                ring = far_first(RINGS - 1 - i)
+                ring = i
                 first = COLS * ring
 
                 @pl.when(jnp.logical_not(is_edge))

time: 40.7 us -> 41.3 us (1.015)
  the two profiles are of different devices: /device:TPU:1 before, /device:TPU:71 now
where the time goes in v9:
time: 41.3 us; the launch traced here: 41.2 us
  Pallas kernels  39.4 us (95%)
  other arithmetic  1.75 us (4%)
    pallas_call x1, Pallas kernels, shards(): pl.pallas_call(kernel, out_shape=[jax.ShapeDtypeStruct((LEVELS, ROWS, LAN...  39.4 us
    select_n x1, other arithmetic, shards(): return jnp.where(taken, jnp.tile(shared, (1, ROWS // 8, 1)), field)  1.74 us

profile of v9, /device:TPU:71, one launch (start us, length us, event | category | flops | bytes accessed | tf_op | source)
XLA Modules:
  0.0 41.2 jit_solution(15118120072583690510)
XLA Ops:
  0.0 39.4 %shard_map.91 = (f32[8,64,128]{2,1,0:T(8,128)}, f32[8,8,128]{2,1,0:T(8,128)}) custom-call(f32[8,64,128]{2,1,0:T(8,128)} %cot.1, f32[64,128]{1,0:T(8,128)} %diff_east_in.1, f32[64,128]{1,0:T(8,128)} %diff_north_in.1, f32[64,128]{1,0:T(8,128)} %flow_east_in.1, f32[64,128]{1,0:T(8,128)} %flow_north_in.1, s32[64,128]{1,0:T(8,128)} %sea_in.1, s32[64]{0:T(128)} %cutoff_in.1, ...), custom_call_target="tpu_custom_call" | custom-call | tf_op jit(solution)/shard_map/pallas_call | solution.py:794
  39.4 1.7 %bitcast_select_fusion = f32[8,64,128]{2,1,0:T(8,128)} fusion(f32[8,64,128]{2,1,0:T(8,128)} %get-tuple-element.8, f32[8,8,128]{2,1,0:T(8,128)} %get-tuple-element.7, pred[64]{0:T(512)(128)(4,1)S(1)} %and_or_fusion), kind=kLoop, calls=%fused_computation | loop fusion | flops 65536 | bytes 557120 | tf_op jit(solution)/shard_map/jit(_where)/select_n | solution.py:848
  (1 shorter events, 0.0 us)

commit v10 on v8

--- a/solution.py
+++ b/solution.py
@@ -567,123 +567,6 @@
                         lat, COLS * z + lax.rem(y + c, COLS),
                     ).start()
 
-            wait_bytes(cuts_ref, cut_recv.at[0])
-            cuts = cuts_ref[...].astype(jnp.int32)
-            shape = (TILES, 8, LANES)
-            wave = iota(shape, 0) + TILES * iota(shape, 2)
-            wave = jnp.minimum(wave, NLON - wave)
-            for half in range(2):
-                kept_ref[half] = jnp.where(wave <= cuts[half][None], 1.0 / NLON, 0.0).astype(
-                    F32
-                ).reshape(2 * LANES, LANES)
-            wait_bytes(lam, in_recv.at[0])
-
-            @pl.when(is_edge)
-            def _():
-                wait_bytes(extra, lx_recv.at[0])
-
-            def filtered():
-                for half in range(2):
-                    real, imag = filter_circles(
-                        lam[:, 0, half], lam[:, 1, half], kept_ref[half], high_ref, low_ref,
-                        turn_ref,
-                    )
-                    fil[:, 0, half] = real
-                    fil[:, 1, half] = imag
-
-            def step(s):
-                filtered()
-
-                @pl.when(s == 0)
-                def _():
-                    wait_bytes(coef.at[pl.ds(0, COLS - 1)], pass_recv.at[0])
-
-                    def circle(k):
-                        parts = [coef[c, :, k] for c in range(COLS)]
-                        return jnp.stack(parts, axis=1).reshape(TILES, 2, 8, LANES)
-
-                    mine = circle(4)
-                    faces[:, 0] = circle(0) * neighbour(mine, -1)
-                    faces[:, 1] = -mine * neighbour(circle(1), 1)
-                    faces[:, 2] = circle(2)
-                    faces[:, 3] = circle(3)
-
-                @pl.when(jnp.logical_and(is_edge, s == 0))
-                def _():
-                    wait_bytes(strip.at[pl.ds(0, COLS - 1)], px_recv.at[0])
-
-                    def circle(k):
-                        parts = [strip[c, :, k // 2] for c in range(COLS)]
-                        both = jnp.stack(parts, axis=1).reshape(TILES, 8, LANES)
-                        turned = pltpu.roll(both, 4, 1)
-                        lower = iota(both.shape, 1) < EDGE
-                        if k % 2:
-                            return jnp.where(lower, turned, both)
-                        return jnp.where(lower, both, turned)
-
-                    mine = circle(4)
-                    faces_x[:, 0] = circle(0) * neighbour(mine, -1)
-                    faces_x[:, 1] = -mine * neighbour(circle(1), 1)
-                    faces_x[:, 2] = circle(2)
-                    faces_x[:, 3] = circle(3)
-
-                @pl.when(is_edge)
-                def _():
-                    lam[...], extra[...] = edge_step(
-                        fil[...], faces[...], extra[...], faces_x[...]
-                    )
-
-                @pl.when(jnp.logical_not(is_edge))
-                def _():
-                    lam[...] = circle_step(fil[...], faces[...])
-
-            over(STEPS - 1, step)
-            filtered()
-
-            my_levels = pl.ds(2 * pair, 2)
-            rows = pl.ds(pl.multiple_of(8 * z, 8), 8)
-
-            @pl.when(is_edge)
-            def _():
-                total, _ = edge_step(fil[...], faces[...], extra[...], faces_x[...])
-                done[...] = total[:, :, 0]
-                done_x[...] = total[:, :, 1]
-
-            def finish(i):
-                ring = far_first(RINGS - 1 - i)
-                first = COLS * ring
-
-                @pl.when(jnp.logical_not(is_edge))
-                def _():
-                    done[pl.ds(first, COLS)] = last_step(
-                        fil[pl.ds(first, COLS)],
-                        fil[lax.rem(first + TILES - 1, TILES), :, 0],
-                        fil[lax.rem(first + COLS, TILES), :, 0],
-                        faces[pl.ds(first, COLS), :, 0],
-                    )
-
-                for c in range(COLS):
-                    tile = first + lax.rem(y + c, COLS)
-                    remote(
-                        done.at[tile], out.at[my_levels, rows], out_send.at[0],
-                        out_recv.at[0], polar_lat, tile,
-                    ).start()
-
-                    @pl.when(jnp.logical_and(is_edge, tile != lon))
-                    def _():
-                        remote(
-                            done_x.at[tile], row_x.at[my_levels], ox_send.at[0], ox_recv.at[0],
-                            beside_lat, tile,
-                        ).start()
-
-                    @pl.when(jnp.logical_and(is_edge, tile == lon))
-                    def _():
-                        pltpu.make_async_copy(
-                            done_x.at[tile], row_x.at[my_levels], ox_recv.at[0]
-                        ).start()
-
-            over(RINGS, finish)
-
         to_left.wait_recv()
         to_right.wait_recv()
 
@@ -746,6 +629,125 @@
 
         store = pltpu.make_async_copy(mid_out, out, store_sem.at[0])
         store.start()
+
+        @pl.when(beside)
+        def _():
+            wait_bytes(cuts_ref, cut_recv.at[0])
+            cuts = cuts_ref[...].astype(jnp.int32)
+            shape = (TILES, 8, LANES)
+            wave = iota(shape, 0) + TILES * iota(shape, 2)
+            wave = jnp.minimum(wave, NLON - wave)
+            for half in range(2):
+                kept_ref[half] = jnp.where(wave <= cuts[half][None], 1.0 / NLON, 0.0).astype(
+                    F32
+                ).reshape(2 * LANES, LANES)
+            wait_bytes(lam, in_recv.at[0])
+
+            @pl.when(is_edge)
+            def _():
+                wait_bytes(extra, lx_recv.at[0])
+
+            def filtered():
+                for half in range(2):
+                    real, imag = filter_circles(
+                        lam[:, 0, half], lam[:, 1, half], kept_ref[half], high_ref, low_ref,
+                        turn_ref,
+                    )
+                    fil[:, 0, half] = real
+                    fil[:, 1, half] = imag
+
+            def step(s):
+                filtered()
+
+                @pl.when(s == 0)
+                def _():
+                    wait_bytes(coef.at[pl.ds(0, COLS - 1)], pass_recv.at[0])
+
+                    def circle(k):
+                        parts = [coef[c, :, k] for c in range(COLS)]
+                        return jnp.stack(parts, axis=1).reshape(TILES, 2, 8, LANES)
+
+                    mine = circle(4)
+                    faces[:, 0] = circle(0) * neighbour(mine, -1)
+                    faces[:, 1] = -mine * neighbour(circle(1), 1)
+                    faces[:, 2] = circle(2)
+                    faces[:, 3] = circle(3)
+
+                @pl.when(jnp.logical_and(is_edge, s == 0))
+                def _():
+                    wait_bytes(strip.at[pl.ds(0, COLS - 1)], px_recv.at[0])
+
+                    def circle(k):
+                        parts = [strip[c, :, k // 2] for c in range(COLS)]
+                        both = jnp.stack(parts, axis=1).reshape(TILES, 8, LANES)
+                        turned = pltpu.roll(both, 4, 1)
+                        lower = iota(both.shape, 1) < EDGE
+                        if k % 2:
+                            return jnp.where(lower, turned, both)
+                        return jnp.where(lower, both, turned)
+
+                    mine = circle(4)
+                    faces_x[:, 0] = circle(0) * neighbour(mine, -1)
+                    faces_x[:, 1] = -mine * neighbour(circle(1), 1)
+                    faces_x[:, 2] = circle(2)
+                    faces_x[:, 3] = circle(3)
+
+                @pl.when(is_edge)
+                def _():
+                    lam[...], extra[...] = edge_step(
+                        fil[...], faces[...], extra[...], faces_x[...]
+                    )
+
+                @pl.when(jnp.logical_not(is_edge))
+                def _():
+                    lam[...] = circle_step(fil[...], faces[...])
+
+            over(STEPS - 1, step)
+            filtered()
+
+            my_levels = pl.ds(2 * pair, 2)
+            rows = pl.ds(pl.multiple_of(8 * z, 8), 8)
+
+            @pl.when(is_edge)
+            def _():
+                total, _ = edge_step(fil[...], faces[...], extra[...], faces_x[...])
+                done[...] = total[:, :, 0]
+                done_x[...] = total[:, :, 1]
+
+            def finish(i):
+                ring = i
+                first = COLS * ring
+
+                @pl.when(jnp.logical_not(is_edge))
+                def _():
+                    done[pl.ds(first, COLS)] = last_step(
+                        fil[pl.ds(first, COLS)],
+                        fil[lax.rem(first + TILES - 1, TILES), :, 0],
+                        fil[lax.rem(first + COLS, TILES), :, 0],
+                        faces[pl.ds(first, COLS), :, 0],
+                    )
+
+                for c in range(COLS):
+                    tile = first + lax.rem(y + c, COLS)
+                    remote(
+                        done.at[tile], out.at[my_levels, rows], out_send.at[0],
+                        out_recv.at[0], polar_lat, tile,
+                    ).start()
+
+                    @pl.when(jnp.logical_and(is_edge, tile != lon))
+                    def _():
+                        remote(
+                            done_x.at[tile], row_x.at[my_levels], ox_send.at[0], ox_recv.at[0],
+                            beside_lat, tile,
+                        ).start()
+
+                    @pl.when(jnp.logical_and(is_edge, tile == lon))
+                    def _():
+                        pltpu.make_async_copy(
+                            done_x.at[tile], row_x.at[my_levels], ox_recv.at[0]
+                        ).start()
+
+            over(RINGS, finish)
 
         @pl.when(beside)
         def _():

time: 40.7 us -> 40.2 us (0.988)
  no operation moved by 1% of the time
where the time goes in v10:
time: 40.2 us; the launch traced here: 39.8 us
  Pallas kernels  38 us (95%)
  other arithmetic  1.75 us (4%)
    pallas_call x1, Pallas kernels, shards(): pl.pallas_call(kernel, out_shape=[jax.ShapeDtypeStruct((LEVELS, ROWS, LAN...  38 us
    select_n x1, other arithmetic, shards(): return jnp.where(taken, jnp.tile(shared, (1, ROWS // 8, 1)), field)  1.74 us

profile of v10, /device:TPU:1, one launch (start us, length us, event | category | flops | bytes accessed | tf_op | source)
XLA Modules:
  0.0 39.8 jit_solution(3567004598986257501)
XLA Ops:
  0.0 38.0 %shard_map.91 = (f32[8,64,128]{2,1,0:T(8,128)}, f32[8,8,128]{2,1,0:T(8,128)}) custom-call(f32[8,64,128]{2,1,0:T(8,128)} %cot.1, f32[64,128]{1,0:T(8,128)} %diff_east_in.1, f32[64,128]{1,0:T(8,128)} %diff_north_in.1, f32[64,128]{1,0:T(8,128)} %flow_east_in.1, f32[64,128]{1,0:T(8,128)} %flow_north_in.1, s32[64,128]{1,0:T(8,128)} %sea_in.1, s32[64]{0:T(128)} %cutoff_in.1, ...), custom_call_target="tpu_custom_call" | custom-call | tf_op jit(solution)/shard_map/pallas_call | solution.py:790
  38.0 1.7 %bitcast_select_fusion = f32[8,64,128]{2,1,0:T(8,128)} fusion(f32[8,64,128]{2,1,0:T(8,128)} %get-tuple-element.8, f32[8,8,128]{2,1,0:T(8,128)} %get-tuple-element.7, pred[64]{0:T(512)(128)(4,1)S(1)} %and_or_fusion), kind=kLoop, calls=%fused_computation | loop fusion | flops 65536 | bytes 557120 | tf_op jit(solution)/shard_map/jit(_where)/select_n | solution.py:844
  (1 shorter events, 0.0 us)

commit v11 on v10

--- a/solution.py
+++ b/solution.py
@@ -249,11 +249,16 @@
     polar_lat = jnp.where(first_band, 0, LATS - 1)
     beside_lat = jnp.where(first_band, 1, LATS - 2)
     edge = jnp.where(first_band, BLOCKS - 1, 0)
-    is_edge = jnp.logical_and(beside, z == edge)
+
+    def flip(b):
+        return jnp.where(first_band, BLOCKS - 1 - b, b)
+
+    edge_ring = flip(edge)
+    is_edge = jnp.logical_and(beside, z == edge_ring)
     pair = y
 
     def owner_of(b, p):
-        return beside_lat, COLS * b + p
+        return beside_lat, COLS * flip(b) + p
 
     main = pl.ds(HALO, ROWS)
     plane_loads = [
@@ -321,7 +326,7 @@
     @pl.when(polar)
     def _():
         def greet(i):
-            b = far_first(i)
+            b = flip(far_first(i))
             for p in range(PAIRS):
                 hail(*owner_of(b, p))
 
@@ -340,9 +345,9 @@
     @pl.when(beside)
     def _():
         for p in range(PAIRS):
-            @pl.when(COLS * edge + p != lon)
+            @pl.when(COLS * edge_ring + p != lon)
             def _():
-                hail(lat, COLS * edge + p)
+                hail(lat, COLS * edge_ring + p)
 
     @pl.when(jnp.logical_not(polar))
     def _():
@@ -466,13 +471,15 @@
             ).start()
 
         def send_free(i):
-            @pl.when(far_first(i) != edge)
+            b = flip(far_first(i))
+
+            @pl.when(b != edge)
             def _():
-                send_coef(far_first(i))
+                send_coef(b)
 
         over(RINGS, lambda i: send_free(RINGS - 1 - i))
         pltpu.make_async_remote_copy(
-            src_ref=cut_src.at[z], dst_ref=cuts_ref, send_sem=cut_send.at[0],
+            src_ref=cut_src.at[flip(z)], dst_ref=cuts_ref, send_sem=cut_send.at[0],
             recv_sem=cut_recv.at[0], device_id=at(beside_lat, lon),
             device_id_type=pl.DeviceIdType.MESH,
         ).start()
@@ -512,7 +519,7 @@
             remote(
                 extra_src.at[p], extra.at[lon], lx_send.at[0], lx_recv.at[0], *owner_of(edge, p)
             ).start()
-        over(RINGS, lambda i: send_block(far_first(RINGS - 1 - i)))
+        over(RINGS, lambda i: send_block(flip(far_first(RINGS - 1 - i))))
 
         wait_bytes(cuts_ref, cut_send.at[0])
 
@@ -706,7 +713,7 @@
             filtered()
 
             my_levels = pl.ds(2 * pair, 2)
-            rows = pl.ds(pl.multiple_of(8 * z, 8), 8)
+            rows = pl.ds(pl.multiple_of(8 * flip(z), 8), 8)
 
             @pl.when(is_edge)
             def _():
@@ -776,6 +783,43 @@
     @pl.when(lat < LATS - 1)
     def _():
         to_north.wait_send()
+
+
+def merge(field, shared, result, rows, extra, load_sem, store_sem):
+    lat = lax.axis_index("lat")
+    beside = jnp.logical_or(lat == 1, lat == LATS - 2)
+    loads, stores = [], []
+    for l in range(0, LEVELS, 1):
+        some = pl.ds(l, 1)
+        loads.append(pltpu.make_async_copy(field.at[some], rows.at[some], load_sem.at[l]))
+        stores.append(pltpu.make_async_copy(rows.at[some], result.at[some], store_sem.at[l]))
+    load_extra = pltpu.make_async_copy(shared, extra, load_sem.at[LEVELS])
+    for load in loads:
+        load.start()
+
+    @pl.when(beside)
+    def _():
+        load_extra.start()
+        load_extra.wait()
+
+    row = iota((1, 8, LANES), 1)
+    for k, l in enumerate(range(0, LEVELS, 1)):
+        loads[k].wait()
+        some = slice(l, l + 1)
+
+        @pl.when(lat == 1)
+        def _():
+            rows[some, 0:8] = jnp.where(row < EDGE, extra[some], rows[some, 0:8])
+
+        @pl.when(lat == LATS - 2)
+        def _():
+            rows[some, ROWS - 8 : ROWS] = jnp.where(
+                row < EDGE, rows[some, ROWS - 8 : ROWS], extra[some]
+            )
+
+        stores[k].start()
+    for store in stores:
+        store.wait()
 
 
 def shards(cotangent, diff_east, diff_north, flow_east, flow_north, sea_mask, cutoff):
@@ -836,12 +880,19 @@
         cotangent, diff_east, diff_north, flow_east, flow_north, sea_mask, cutoff,
         jnp.asarray(wide), jnp.asarray(turn),
     )
-    lat = lax.axis_index("lat")
-    row = lax.broadcasted_iota(jnp.int32, field.shape, 1)
-    taken = jnp.logical_or(
-        jnp.logical_and(lat == 1, row < EDGE), jnp.logical_and(lat == LATS - 2, row >= ROWS - EDGE)
-    )
-    return jnp.where(taken, jnp.tile(shared, (1, ROWS // 8, 1)), field)
+    return pl.pallas_call(
+        merge,
+        out_shape=jax.ShapeDtypeStruct((LEVELS, ROWS, LANES), F32),
+        in_specs=[hbm, hbm],
+        out_specs=hbm,
+        scratch_shapes=[
+            room(LEVELS, ROWS, LANES),
+            room(LEVELS, 8, LANES),
+            dma((LEVELS + 1,)),
+            dma((LEVELS + 1,)),
+        ],
+        compiler_params=pltpu.CompilerParams(vmem_limit_bytes=63 * 1024 * 1024),
+    )(field, shared)
 
 
 def solution(mesh):

time: 40.2 us -> 40.2 us (level)
  the two profiles are of different devices: /device:TPU:1 before, /device:TPU:134 now
where the time goes in v11:
time: 40.2 us; the launch traced here: 40 us
  Pallas kernels  40 us (100%)
    pallas_call x1, Pallas kernels, shards(): pl.pallas_call(kernel, out_shape=[jax.ShapeDtypeStruct((LEVELS, ROWS, LAN...  38.3 us
    pallas_call x1, Pallas kernels, shards(): pl.pallas_call(merge, out_shape=jax.ShapeDtypeStruct((LEVELS, ROWS, LANES...  1.74 us

profile of v11, /device:TPU:134, one launch (start us, length us, event | category | flops | bytes accessed | tf_op | source)
XLA Modules:
  0.0 40.0 jit_solution(3962311956730196600)
XLA Ops:
  0.0 38.3 %shard_map.91 = (f32[8,64,128]{2,1,0:T(8,128)}, f32[8,8,128]{2,1,0:T(8,128)}) custom-call(f32[8,64,128]{2,1,0:T(8,128)} %cot.1, f32[64,128]{1,0:T(8,128)} %diff_east_in.1, f32[64,128]{1,0:T(8,128)} %diff_north_in.1, f32[64,128]{1,0:T(8,128)} %flow_east_in.1, f32[64,128]{1,0:T(8,128)} %flow_north_in.1, s32[64,128]{1,0:T(8,128)} %sea_in.1, s32[64]{0:T(128)} %cutoff_in.1, ...), custom_call_target="tpu_custom_call" | custom-call | tf_op jit(solution)/shard_map/pallas_call | solution.py:834
  38.3 1.7 %shard_map.92 = f32[8,64,128]{2,1,0:T(8,128)} custom-call(f32[8,64,128]{2,1,0:T(8,128)} %get-tuple-element.7.field, f32[8,8,128]{2,1,0:T(8,128)} %get-tuple-element.8.shared), custom_call_target="tpu_custom_call" | custom-call | tf_op jit(solution)/shard_map/pallas_call | solution.py:883

commit v12 on v10

--- a/solution.py
+++ b/solution.py
@@ -722,13 +722,13 @@
                 def _():
                     done[pl.ds(first, COLS)] = last_step(
                         fil[pl.ds(first, COLS)],
-                        fil[lax.rem(first + TILES - 1, TILES), :, 0],
-                        fil[lax.rem(first + COLS, TILES), :, 0],
+                        fil[(first + TILES - 1) % TILES, :, 0],
+                        fil[(first + COLS) % TILES, :, 0],
                         faces[pl.ds(first, COLS), :, 0],
                     )
 
                 for c in range(COLS):
-                    tile = first + lax.rem(y + c, COLS)
+                    tile = first + c
                     remote(
                         done.at[tile], out.at[my_levels, rows], out_send.at[0],
                         out_recv.at[0], polar_lat, tile,
@@ -747,7 +747,8 @@
                             done_x.at[tile], row_x.at[my_levels], ox_recv.at[0]
                         ).start()
 
-            over(RINGS, finish)
+            for i in range(RINGS):
+                finish(i)
 
         @pl.when(beside)
         def _():

time: 40.2 us -> 40.1 us (level)
    pallas_call x1, Pallas kernels: 38 us -> 37.6 us  [shards(): pl.pallas_call(kernel, out_shape=[jax.ShapeDtypeStruct((LEVELS, ROWS, LAN...]
where the time goes in v12:
time: 40.1 us; the launch traced here: 39.4 us
  Pallas kernels  37.6 us (94%)
  other arithmetic  1.75 us (4%)
    pallas_call x1, Pallas kernels, shards(): pl.pallas_call(kernel, out_shape=[jax.ShapeDtypeStruct((LEVELS, ROWS, LAN...  37.6 us
    select_n x1, other arithmetic, shards(): return jnp.where(taken, jnp.tile(shared, (1, ROWS // 8, 1)), field)  1.74 us

profile of v12, /device:TPU:1, one launch (start us, length us, event | category | flops | bytes accessed | tf_op | source)
XLA Modules:
  0.0 39.4 jit_solution(14137207111939531387)
XLA Ops:
  0.0 37.6 %shard_map.91 = (f32[8,64,128]{2,1,0:T(8,128)}, f32[8,8,128]{2,1,0:T(8,128)}) custom-call(f32[8,64,128]{2,1,0:T(8,128)} %cot.1, f32[64,128]{1,0:T(8,128)} %diff_east_in.1, f32[64,128]{1,0:T(8,128)} %diff_north_in.1, f32[64,128]{1,0:T(8,128)} %flow_east_in.1, f32[64,128]{1,0:T(8,128)} %flow_north_in.1, s32[64,128]{1,0:T(8,128)} %sea_in.1, s32[64]{0:T(128)} %cutoff_in.1, ...), custom_call_target="tpu_custom_call" | custom-call | tf_op jit(solution)/shard_map/pallas_call | solution.py:791
  37.6 1.7 %bitcast_select_fusion = f32[8,64,128]{2,1,0:T(8,128)} fusion(f32[8,64,128]{2,1,0:T(8,128)} %get-tuple-element.8, f32[8,8,128]{2,1,0:T(8,128)} %get-tuple-element.7, pred[64]{0:T(512)(128)(4,1)S(1)} %and_or_fusion), kind=kLoop, calls=%fused_computation | loop fusion | flops 65536 | bytes 557120 | tf_op jit(solution)/shard_map/jit(_where)/select_n | solution.py:845
  (1 shorter events, 0.0 us)
